TPU v7x, 32 devices: a whole 2x2x4 slice. The times are simulated.
32 devices in a mesh: grp: 2 (over y), seg: 16 (over z, x, core).
Axes of the slice: x: 2, y: 2, z: 4, core: 2. Of those that a mesh axis runs over, the one named last changes fastest.
Arguments:
- waveform: bfloat16 [512, 256, 512], P('grp', 'seg')
- valid_count: int32 [512, 256], P('grp', 'seg'), may hold values from 128 to 512
- plan: int32 [2, 8], replicated, may hold values from 0 to 1, as said below
Outputs:
- cross: bfloat16 [128, 2, 512, 8, 256], P('seg', None, 'grp')
Inputs may be any that keep to these rules, and one draw needn't show every extreme that they name: `plan`: row g lists, round by round, the partner group of group g: in every round g is the partner of its partner and each group is named once, and every row names each of the 2 groups at least once.
All inputs are finite; a program needn't handle non-finite values.
Results may differ from a plain program's by a relative error of at most 0.0061.
Values may be sent and summed in bfloat16 or wider, within the bound.
No kernel may reach another device: no remote copies, remote signals or barrier semaphores. Data moves between devices by JAX's collectives and lax.ppermute only.
A program may use at most 128 MiB of HBM per device.

v0:
```python
import math

import jax
import jax.numpy as jnp
from jax import lax
from jax.sharding import PartitionSpec as P

F = 128
K0 = 2


def make_basis(samples):
    times = jnp.arange(samples, dtype=jnp.int32)[:, None]
    bins = K0 + jnp.arange(F, dtype=jnp.int32)[None, :]
    phase = (times * bins % samples).astype(jnp.float32) * (2.0 * math.pi / samples)
    return jnp.concatenate([jnp.cos(phase), -jnp.sin(phase)], axis=1).astype(jnp.bfloat16)


def add_block(carry, piece, start, left_side, group_rows):
    count = piece.shape[3]
    span = min(count, group_rows)
    seg_total = left_side.shape[2] // 2
    for portion in range(count // span):
        partner = piece[:, :, :, portion * span : (portion + 1) * span]
        right_side = jnp.concatenate([partner[0], partner[1]], axis=1)
        block = jnp.einsum(
            "cbsi,bsj->bcij", left_side, right_side, preferred_element_type=jnp.float32
        )
        block = (block / float(seg_total)).astype(jnp.bfloat16)
        first = start + portion * span
        owner = jnp.asarray(first // group_rows, dtype=jnp.int32)
        offset = jnp.asarray(first % group_rows, dtype=jnp.int32)
        zero = jnp.asarray(0, dtype=jnp.int32)
        carry = lax.dynamic_update_slice(
            carry, block[:, :, :, None, :], (zero, zero, zero, owner, offset)
        )
    return carry


def shards(waveform, valid_count, plan):
    group_rows, seg_local, samples = waveform.shape
    basis = make_basis(samples)
    times = lax.broadcasted_iota(jnp.int32, waveform.shape, 2)
    gated = jnp.where(times < valid_count[:, :, None], waveform, jnp.zeros_like(waveform))
    spectrum = jnp.einsum("tk,ist->ksi", basis, gated, preferred_element_type=jnp.float32)
    spectrum = spectrum.reshape(2, F, seg_local, group_rows)
    power = jnp.sum(spectrum * spectrum, axis=(0, 1)) / F
    keep = (valid_count.T >= samples // 2).astype(jnp.float32)
    weight = keep / jnp.sqrt(power + 1e-06)
    white = (spectrum * weight[None, None, :, :]).astype(jnp.bfloat16)
    group_index = lax.axis_index("grp")
    sched_row = lax.dynamic_index_in_dim(plan, group_index, 0, keepdims=False)
    mine = lax.all_to_all(white, "seg", split_axis=1, concat_axis=2, tiled=True)
    real_part = mine[0]
    imag_part = mine[1]
    left_side = jnp.stack(
        [
            jnp.concatenate([real_part, imag_part], axis=1),
            jnp.concatenate([imag_part, -real_part], axis=1),
        ],
        axis=0,
    )
    bins_local = mine.shape[1]
    groups_total = lax.axis_size("grp")
    empty = jnp.zeros((bins_local, 2, group_rows, groups_total, group_rows), jnp.bfloat16)
    everyone_bins = lax.all_gather(mine, "grp", axis=3, tiled=True)
    per_group = add_block(empty, everyone_bins, 0, left_side, group_rows)
    return jnp.take(per_group, sched_row, axis=3)


def solution(mesh):
    return jax.shard_map(
        shards,
        mesh=mesh,
        in_specs=(P("grp", "seg", None), P("grp", "seg"), P()),
        out_specs=P("seg", None, "grp", None, None),
        check_vma=False,
    )
```

profile of v0, /device:TPU:0, one launch (start us, length us, event | category | flops | bytes accessed | tf_op | source)
XLA Modules:
  0.0 177.4 jit_solution(15679145175087141644)
XLA Ops:
  6.5 0.8 copy.29
  7.4 1.2 cosine_convert_fusion
  8.6 2.9 %fusion = bf16[256,16,512]{2,1,0:T(8,128)(2,1)S(1)} fusion(bf16[256,16,512]{2,1,0:T(8,128)(2,1)} %param.3, s32[256,16]{1,0:T(8,128)S(1)} %copy.29), kind=kLoop, calls=%fused_computation.4 | loop fusion | flops 4194304 | bytes 8404992 | tf_op jit(solution)/shard_map/jit(_where)/select_n | solution.py:44
  11.5 3.0 %fusion.1 = (f32[16,256]{1,0:T(8,128)S(1)}, f32[256,16,256]{0,2,1:T(8,128)S(1)}) fusion(bf16[512,128]{0,1:T(8,128)(2,1)S(1)} %get-tuple-element.16, bf16[512,128]{0,1:T(8,128)(2,1)S(1)} %get-tuple-element.15, bf16[256,16,512]{2,1,0:T(8,128)(2,1)S(1)} %fusion), kind=kOutput, calls=%fused_computation.9 | convolution fusion | flops 1076359168 | bytes 8667136 | tf_op jit(solution)/shard_map/tk,ist->ksi/dot_general | solution.py:45
  14.6 2.3 %fusion.2 = bf16[2,128,16,256]{3,2,0,1:T(8,128)(2,1)S(1)} fusion(f32[2,128,16,256]{3,1,0,2:T(8,128)S(1)} %bitcast.63, f32[16,256]{1,0:T(8,128)S(1)} %rsqrt_select_fusion), kind=kLoop, calls=%fused_computation.11 | loop fusion | flops 2097152 | bytes 6307840 | tf_op jit(solution)/shard_map/convert_element_type | solution.py:50
  16.9 54.5 %all_to_all.18 = bf16[2,128,16,256]{3,2,0,1:T(8,128)(2,1)S(1)} all-to-all(bf16[2,128,16,256]{3,2,0,1:T(8,128)(2,1)S(1)} %fusion.2), channel_id=1, replica_groups=mesh['grp'=2,'seg'=16] {'seg'}, dimensions={1} | all-to-all | bytes 4194304 | tf_op jit(solution)/shard_map/all_to_all | solution.py:53
  71.3 1.5 copy.39
  73.0 0.2 copy.32
  73.2 1.2 fusion.26
  74.4 0.5 copy.36
  74.9 1.3 copy.33
  76.3 0.5 copy.35
  76.8 0.2 neg.7
  77.0 2.4 %maximum_bitcast_fusion = (bf16[1,8,512,256]{2,3,0,1:T(8,128)(2,1)}, bf16[1,8,512,256]{2,3,0,1:T(8,128)(2,1)}) fusion(bf16[8,256,256]{1,2,0:T(8,128)(2,1)S(1)} %copy.36, bf16[8,256,256]{1,2,0:T(8,128)(2,1)S(1)} %copy.35, bf16[8,256,256]{1,2,0:T(8,128)(2,1)S(1)} %neg.7), kind=kLoop, calls=%fused_computation.22 | loop fusion | flops 8388608 | bytes 7340032 | tf_op jit(solution)/shard_map/stack | solution.py:56
  79.4 50.9 %all-gather.2.cloned.1.call-done = bf16[2,8,256,512]{3,2,1,0:T(8,128)(2,1)} async-done(((bf16[2,8,256,256]{3,2,1,0:T(8,128)(2,1)}), bf16[2,8,256,512]{3,2,1,0:T(8,128)(2,1)}) %all-gather.2.cloned.1.call-update) | async-done | bytes 4194320 | tf_op jit(solution)/shard_map/all_gather | solution.py:66
  130.2 2.6 %slice_bitcast_fusion.3 = (bf16[8,256,256]{2,1,0:T(8,128)(2,1)S(1)}, bf16[8,256,256]{2,1,0:T(8,128)(2,1)S(1)}, bf16[8,256,256]{2,1,0:T(8,128)(2,1)S(1)}, bf16[8,256,256]{2,1,0:T(8,128)(2,1)S(1)}) fusion(bf16[2,8,256,512]{3,2,1,0:T(8,128)(2,1)} %all-gather.2.cloned.1.call-done), kind=kLoop, calls=%fused_computation.33 | loop fusion | bytes 8388608 | tf_op jit(solution)/shard_map/squeeze | solution.py:25
  132.8 0.2 copy-done.1
  133.1 1.5 fusion.8
  134.6 1.5 fusion.7
  136.1 1.5 fusion.9
  137.5 6.1 %gather_fusion = bf16[8,8,2,128,256]{4,3,2,1,0:T(8,128)(2,1)} fusion(bf16[8,2,128,2,256]{4,2,1,0,3:T(8,128)(2,1)} %get-tuple-element.5, s32[1024]{0:T(1024)S(1)} %pad_clamp_fusion), kind=kCustom, calls=%fused_computation | custom fusion | bytes 16777248 | tf_op jit(solution)/shard_map/jit(_take)/gather | solution.py:68
  143.7 4.7 %gather_fusion.1 = bf16[8,8,2,128,256]{4,3,2,1,0:T(8,128)(2,1)} fusion(bf16[8,2,128,2,256]{4,2,1,0,3:T(8,128)(2,1)S(1)} %get-tuple-element.6, s32[1024]{0:T(1024)S(1)} %pad_clamp_fusion), kind=kCustom, calls=%fused_computation.1 | custom fusion | bytes 16777248 | tf_op jit(solution)/shard_map/jit(_take)/gather | solution.py:68
  148.4 11.0 %maximum_select_fusion = bf16[8,2,256,8,256]{4,2,1,0,3:T(8,128)(2,1)S(1)} fusion(bf16[8,2,128,8,256]{4,2,1,0,3:T(8,128)(2,1)} %bitcast.59, bf16[8,2,128,8,256]{4,2,1,0,3:T(8,128)(2,1)} %bitcast.58, pred[8]{0:T(512)(128)(4,1)S(1)} %compare_and_fusion), kind=kLoop, calls=%fused_computation.2 | loop fusion | flops 41943040 | bytes 33554440 | tf_op jit(solution)/shard_map/jit(_take)/select_n | solution.py:68
  159.4 11.2 %copy.40 = bf16[8,2,256,8,256]{4,3,2,1,0:T(8,128)(2,1)} copy(bf16[8,2,256,8,256]{4,2,1,0,3:T(8,128)(2,1)S(1)} %maximum_select_fusion) | data formatting | bytes 33554432 | tf_op jit(solution)/shard_map/jit(_take)/select_n | solution.py:68
  (15 shorter events, 0.2 us)
Async XLA Ops:
  6.5 123.7 %all-gather.2.cloned.1.call-start = ((), (), s32[]{:S(2)}) async-start(), calls=%async_computation.1 | async-start | bytes 6291456 | tf_op jit(solution)/shard_map/all_gather | solution.py:66
  11.5 3.0 %copy-start.2 = (s32[256,16]{0,1:T(8,128)S(1)}, s32[256,16]{0,1:T(8,128)}, u32[]{:S(2)}) copy-start(s32[256,16]{0,1:T(8,128)} %param.4) | copy-start | bytes 49156
  71.3 1.6 copy-start.3
  79.4 53.5 %copy-start = (bf16[1,8,512,256]{2,3,0,1:T(8,128)(2,1)S(1)}, bf16[1,8,512,256]{2,3,0,1:T(8,128)(2,1)}, u32[]{:S(2)}) copy-start(bf16[1,8,512,256]{2,3,0,1:T(8,128)(2,1)} %get-tuple-element.13) | copy-start | bytes 6291460
  130.2 2.9 %copy-start.1 = (bf16[1,8,512,256]{2,3,0,1:T(8,128)(2,1)S(1)}, bf16[1,8,512,256]{2,3,0,1:T(8,128)(2,1)}, u32[]{:S(2)}) copy-start(bf16[1,8,512,256]{2,3,0,1:T(8,128)(2,1)} %get-tuple-element.14) | copy-start | bytes 6291460
Sparse Core Ops, SparseCore 0:
  73.0 57.1 all-gather.1
where the time goes:
time: 178 us; the launch traced here: 177 us
  blocking collectives  54.5 us (31%)
  waiting for transfers between devices  50.9 us (29%)
  local copies, waits for them, and re-layouts  31 us (17%)
  other arithmetic  21.5 us (12%)
  between operations  13.6 us (8%)
  matrix products  5.96 us (3%)
    all_to_all x1, blocking collectives, shards(): mine = lax.all_to_all(white, 'seg', split_axis=1, concat_axis=2, tiled=True)  54.5 us
    all_gather x1, waiting for transfers between devices, shards(): everyone_bins = lax.all_gather(mine, 'grp', axis=3, tiled=True)  50.9 us
    select_n x1, local copies, waits for them, and re-layouts, shards(): return jnp.take(per_group, sched_row, axis=3)  11.2 us
    select_n x2, other arithmetic, shards(): return jnp.take(per_group, sched_row, axis=3)  11 us
    gather x2, local copies, waits for them, and re-layouts, shards(): return jnp.take(per_group, sched_row, axis=3)  10.8 us
  transfers between devices with their start and end apart: 1, of which 1 were waited for; matrix products, arithmetic and copies ran while one was open for 4% of the time, Pallas kernels for 0%

commit v1 on v0

v1 whole, which is shorter than its diff:
```python
import functools
import math

import jax
import jax.numpy as jnp
import numpy as np
from jax import lax
from jax.experimental import pallas as pl
from jax.experimental.pallas import tpu as pltpu
from jax.sharding import PartitionSpec as P

F = 128
K0 = 2
PLANES = 4
LANES = 128
MIB = 1024 * 1024


def make_basis(samples, parts):
    bins = np.arange(F).reshape(parts, 1, F // parts)
    bins = np.concatenate([bins, bins], axis=1)
    imag = np.zeros_like(bins)
    imag[:, 1] = 1
    bins, imag = bins.reshape(-1, 1), imag.reshape(-1, 1)
    phase = (np.arange(samples)[None, :] * (K0 + bins) % samples) * (2.0 * math.pi / samples)
    return np.where(imag == 1, -np.sin(phase), np.cos(phase))


def head_kernel(me_ref, wave_ref, valid_ref, basis_ref, *rest, parts):
    out_refs, (held_ref, wide_ref, white_ref, sems) = rest[:-4], rest[-4:]
    rows, segs, samples = wave_ref.shape
    half = samples // 2
    step, copies = 16, sems.shape[0]
    share = rows // copies
    sample_tiles, row_tiles = samples // LANES, rows // LANES

    def copy(n):
        part = pl.ds(n * share, share)
        return pltpu.make_async_copy(wave_ref.at[part], held_ref.at[part], sems.at[n])

    for n in range(copies):
        copy(n).start()
    for n in range(copies):
        copy(n).wait()

        @pl.loop(n * share // step, (n + 1) * share // step)
        def _(j):
            block = held_ref[pl.ds(j * step, step)].astype(jnp.float32).reshape(step * segs, samples)
            for q in range(sample_tiles):
                wide_ref[q, pl.ds(pl.multiple_of(j * step * segs, step * segs), step * segs), :] = block[
                    :, q * LANES : (q + 1) * LANES
                ]

    valid_rows = valid_ref[...]
    valid_cols = valid_rows.T
    times = lax.broadcasted_iota(jnp.int32, (rows, LANES), 1)
    for s in range(segs):
        count = valid_cols[:, s : s + 1]
        gated = jnp.concatenate(
            [
                jnp.where(times + q * LANES < count, wide_ref[q, pl.ds(s, rows, stride=segs), :], 0.0)
                for q in range(sample_tiles)
            ],
            axis=1,
        ).astype(jnp.bfloat16)
        spectrum = lax.dot_general(
            basis_ref[...], gated, (((1,), (1,)), ((), ())), preferred_element_type=jnp.float32
        )
        power = jnp.sum(spectrum * spectrum, axis=0, keepdims=True) / F
        keep = (valid_rows[s : s + 1, :] >= half).astype(jnp.float32)
        white = spectrum * (keep / jnp.sqrt(power + 1e-06))
        for q in range(row_tiles):
            white_ref[q, pl.ds(s, 2 * F, stride=segs), :] = white[:, q * LANES : (q + 1) * LANES]

    me = me_ref[0]
    bins_local = F // parts
    span = bins_local * segs

    def put(d, out_ref, index):
        for part in range(2):
            first = pl.multiple_of(((me ^ d) * 2 + part) * span, span)
            piece = jnp.concatenate([white_ref[q, pl.ds(first, span), :] for q in range(row_tiles)], axis=1)
            out_ref[index, part] = piece.astype(jnp.bfloat16).reshape(bins_local, segs, rows)

    for pair, out_ref in enumerate(out_refs[:-1]):
        put(2 * pair, out_ref, 0)
        put(2 * pair + 1, out_refs[-1], pair)


def head(waveform, valid_count, me, parts):
    rows, segs, samples = waveform.shape
    basis = jnp.asarray(make_basis(samples, parts), dtype=jnp.bfloat16)
    vmem = pl.BlockSpec(memory_space=pltpu.VMEM)
    pairs = parts // 2
    block = (2, F // parts, segs, rows)
    return pl.pallas_call(
        functools.partial(head_kernel, parts=parts),
        out_shape=[jax.ShapeDtypeStruct((n,) + block, jnp.bfloat16) for n in [1] * pairs + [pairs]],
        in_specs=[pl.BlockSpec(memory_space=pltpu.SMEM), pl.BlockSpec(memory_space=pltpu.HBM), vmem, vmem],
        out_specs=[vmem] * (pairs + 1),
        scratch_shapes=[
            pltpu.VMEM(waveform.shape, waveform.dtype),
            pltpu.VMEM((samples // LANES, rows * segs, LANES), jnp.float32),
            pltpu.VMEM((rows // LANES, 2 * F * segs, LANES), jnp.float32),
            pltpu.SemaphoreType.DMA((4,)),
        ],
        compiler_params=pltpu.CompilerParams(vmem_limit_bytes=48 * MIB),
        name="spectra",
    )(me[None].astype(jnp.int32), waveform, valid_count.T, basis)


def cross_kernel(select_ref, *rest, groups, held, low):
    pieces = len(held)
    sides = [rest[e * pieces : (e + 1) * pieces] for e in range(groups)]
    out_ref = rest[-1]
    _, _, rows, rounds, columns = out_ref.shape
    chunk = select_ref.shape[0] // rounds
    k = low + pl.program_id(0)

    def whole(e, part):
        return jnp.concatenate(
            [ref[:, part, k - first].reshape(-1, columns) for first, ref in zip(held, sides[e])], axis=0
        )

    real, imag = whole(0, 0), whole(0, 1)
    seg_total = real.shape[0]
    real, imag = real.T, imag.T
    left = jnp.concatenate(
        [jnp.concatenate([real, imag], axis=1), jnp.concatenate([imag, -real], axis=1)], axis=0
    )
    sums = []
    for e in range(groups):
        right = jnp.concatenate([whole(e, 0), whole(e, 1)], axis=0)
        total = jnp.dot(left, right, preferred_element_type=jnp.float32) / float(seg_total)
        sums.append(total.astype(jnp.bfloat16))
    for part in range(2):
        for first in range(0, rows, chunk):
            start = part * rows + first
            values = jnp.concatenate([total[start : start + chunk] for total in sums], axis=0)
            filled = jnp.dot(select_ref[...], values, preferred_element_type=jnp.float32)
            out_ref[0, part, first : first + chunk] = filled.reshape(chunk, rounds, columns).astype(jnp.bfloat16)


def selection(offset, groups, rows):
    chunk = max(16, rows // groups)
    shape = (chunk, offset.shape[0], groups, chunk)
    pick = lax.broadcasted_iota(jnp.int32, shape, 2) == offset[None, :, None, None]
    same = lax.broadcasted_iota(jnp.int32, shape, 0) == lax.broadcasted_iota(jnp.int32, shape, 3)
    return (pick & same).astype(jnp.bfloat16).reshape(chunk * offset.shape[0], groups * chunk)


def add_bins(out, select, sides, held, low, high, bins_local, rounds):
    groups = len(sides)
    segs, rows = sides[0][0].shape[3:]
    seg_total = segs * sum(piece.shape[0] for piece in sides[0])
    pieces = [piece for side in sides for piece in side]
    bins = high - low
    aliased = out is not None
    vmem = pl.BlockSpec(memory_space=pltpu.VMEM)
    return pl.pallas_call(
        functools.partial(cross_kernel, groups=groups, held=held, low=low),
        grid=(bins,),
        out_shape=jax.ShapeDtypeStruct((bins_local, 2, rows, rounds, rows), jnp.bfloat16),
        in_specs=[vmem] * (1 + len(pieces)) + [pl.BlockSpec(memory_space=pl.ANY)] * aliased,
        out_specs=pl.BlockSpec((1, 2, rows, rounds, rows), lambda b: (low + b, 0, 0, 0, 0)),
        input_output_aliases={1 + len(pieces): 0} if aliased else {},
        compiler_params=pltpu.CompilerParams(vmem_limit_bytes=40 * MIB),
        cost_estimate=pl.CostEstimate(
            flops=8 * bins * groups * rows * rows * seg_total,
            bytes_accessed=4 * bins * rows * rounds * rows,
            transcendentals=0,
        ),
        name="cross",
    )(select, *pieces, *([out] if aliased else []))


class Lane:
    def __init__(self, window):
        self.window = window
        self.sent = []

    def send(self, block, axis, pairs, after=()):
        after = list(after) + self.sent[-self.window :][: len(self.sent) // self.window and 1]
        if after:
            block, _ = lax.optimization_barrier((block, after))
        self.sent.append(lax.ppermute(block, axis, pairs))
        return self.sent[-1]


def shards(waveform, valid_count, plan):
    groups = lax.axis_size("grp")
    parts = lax.axis_size("seg")
    chips = parts // PLANES // 2
    bins_local = F // parts
    middle = (5 * bins_local + 4) // 8
    group = lax.axis_index("grp")
    rounds = plan.shape[1]
    offset = lax.dynamic_index_in_dim(plan, group, 0, keepdims=False) ^ group
    select = selection(offset, groups, waveform.shape[0])

    *mine, for_sibling = head(waveform, valid_count, lax.axis_index("seg"), parts)
    theirs = lax.ppermute(for_sibling, "seg", [(s, s ^ 1) for s in range(parts)])
    seg_lane, far_lane, grp_lane = Lane(parts), Lane(2), Lane(2 * (groups - 1))
    sides = [[] for _ in range(groups)]

    def both(n, low=0, high=bins_local):
        return jnp.concatenate([mine[n], theirs[n : n + 1]], axis=0)[:, :, low:high]

    def scatter(lane, n, low=0, high=bins_local, after=()):
        return lane.send(both(n, low, high), "seg", [(s, s ^ (2 * n)) for s in range(parts)], after)

    def forward(blocks):
        block = jnp.concatenate(blocks, axis=0) if len(blocks) > 1 else blocks[0]
        sides[0].append(block)
        for e in range(1, groups):
            sides[e].append(grp_lane.send(block, "grp", [(g, g ^ e) for g in range(groups)]))
        return sides[1][-1]

    own, beside, far, farthest = (range(p * chips, (p + 1) * chips) for p in range(PLANES))
    forward([both(own[0])])
    own_blocks = [scatter(seg_lane, n) for n in own[1:]]
    own_blocks, select = lax.optimization_barrier((own_blocks, select))
    own_done = forward(own_blocks)
    far_blocks = [scatter(far_lane, n, after=own_blocks if n > far[0] else ()) for n in far]
    beside_blocks = [scatter(seg_lane, n, after=far_blocks[:1] if n > beside[0] else ()) for n in beside]
    beside_done = [forward([block]) for block in beside_blocks][-1]
    far_done = [forward([block]) for block in far_blocks]
    waits = {(0, farthest[0]): [own_done], (0, farthest[-1]): [beside_done]}
    waits[middle, farthest[0]] = [far_done[0]]
    for low, high in ((0, middle), (middle, bins_local)):
        for n in farthest:
            forward([scatter(far_lane, n, low, high, waits.get((low, n), ()))])

    out = None
    whole, last = len(sides[0]) - 2 * chips, chips
    for n, (low, high) in enumerate(((0, middle), (middle, bins_local))):
        held = [0] * whole + [low] * last
        chosen = [side[:whole] + side[whole + n * last :][:last] for side in sides]
        out = add_bins(out, select, chosen, held, low, high, bins_local, rounds)
    return out


def solution(mesh):
    return jax.shard_map(
        shards,
        mesh=mesh,
        in_specs=(P("grp", "seg", None), P("grp", "seg"), P()),
        out_specs=P("seg", None, "grp", None, None),
        check_vma=False,
    )
```

time: 178 us -> 85 us (0.48)
  blocking collectives: 54.5 us -> 0 us
  starting transfers between devices: 0.01 us -> 44.3 us
  waiting for transfers between devices: 50.9 us -> 16.8 us
  local copies, waits for them, and re-layouts: 31 us -> 1.96 us
  Pallas kernels: 0 us -> 20.3 us
  other arithmetic: 21.5 us -> 1.23 us
  between operations: 13.6 us -> 0.11 us
  matrix products: 5.96 us -> 0 us
    all_to_all x1 -> x0, blocking collectives: 54.5 us -> none  [shards(): mine = lax.all_to_all(white, 'seg', split_axis=1, concat_axis=2, tiled=True)]
    all_gather x1 -> x0, waiting for transfers between devices: 50.9 us -> none  [shards(): everyone_bins = lax.all_gather(mine, 'grp', axis=3, tiled=True)]
    ppermute x0 -> x20, starting transfers between devices: none -> 44.3 us  [the longest x19 43.8 us: send(): self.sent.append(lax.ppermute(block, axis, pairs))]
    pallas_call x0 -> x3, Pallas kernels: none -> 20.3 us  [the longest x2 12.1 us: add_bins(): pl.pallas_call(functools.partial(cross_kernel, groups=groups, held=held,...]
    ppermute x0 -> x20, waiting for transfers between devices: none -> 16.8 us  [the longest x19 15.8 us: send(): self.sent.append(lax.ppermute(block, axis, pairs))]
    select_n x3 -> x0, other arithmetic: 13.9 us -> none  [the longest x2 11 us: shards(): return jnp.take(per_group, sched_row, axis=3)]
    select_n x1 -> x0, local copies, waits for them, and re-layouts: 11.2 us -> none  [shards(): return jnp.take(per_group, sched_row, axis=3)]
    gather x2 -> x0, local copies, waits for them, and re-layouts: 10.8 us -> none  [shards(): return jnp.take(per_group, sched_row, axis=3)]
  transfers between devices with their start and end apart: 1 -> 20, of which waited for: 1 -> 6; matrix products, arithmetic and copies ran while one was open for 4% -> 2% of each run, Pallas kernels for 0% -> 9%
where the time goes in v1:
time: 85 us; the launch traced here: 84.7 us
  starting transfers between devices  44.3 us (52%)
  Pallas kernels  20.3 us (24%)
  waiting for transfers between devices  16.8 us (20%)
  local copies, waits for them, and re-layouts  1.96 us (2%)
  other arithmetic  1.23 us (1%)
    ppermute x19, starting transfers between devices, send(): self.sent.append(lax.ppermute(block, axis, pairs))  43.8 us
    ppermute x19, waiting for transfers between devices, send(): self.sent.append(lax.ppermute(block, axis, pairs))  15.8 us
    pallas_call x2, Pallas kernels, add_bins(): pl.pallas_call(functools.partial(cross_kernel, groups=groups, held=held,...  12.1 us
    pallas_call x1, Pallas kernels, head(): pl.pallas_call(functools.partial(head_kernel, parts=parts), out_shape=[ja...  8.23 us
  transfers between devices with their start and end apart: 20, of which 6 were waited for; matrix products, arithmetic and copies ran while one was open for 2% of the time, Pallas kernels for 9%

profile of v1, /device:TPU:0, one launch (start us, length us, event | category | flops | bytes accessed | tf_op | source)
XLA Modules:
  0.0 84.7 jit_solution(13253811327176327374)
XLA Ops:
  0.0 0.9 %copy-done = bf16[256,512]{1,0:T(8,128)(2,1)S(1)} copy-done((bf16[256,512]{1,0:T(8,128)(2,1)S(1)}, bf16[256,512]{1,0:T(8,128)(2,1)}, u32[]{:S(2)}) %copy-start) | copy-done | bytes 262168
  1.0 0.7 copy-done.1
  1.7 8.2 %spectra.1 = (bf16[1,2,8,16,256]{4,3,2,1,0:T(8,128)(2,1)S(1)}, bf16[1,2,8,16,256]{4,3,2,1,0:T(8,128)(2,1)S(1)}, bf16[1,2,8,16,256]{4,3,2,1,0:T(8,128)(2,1)S(1)},...) custom-call(s32[1]{0:T(128)} %bitcast.me_ref, ...), custom_call_target="tpu_custom_call" | custom-call | tf_op jit(solution)/shard_map/spectra/pallas_call | solution.py:96
  10.4 0.7 xor_bitcast_fusion
  11.7 1.0 %collective-permute-done = bf16[8,2,8,16,256]{4,3,2,1,0:T(8,128)(2,1)S(1)} collective-permute-done((bf16[8,2,8,16,256]{4,3,2,1,0:T(8,128)(2,1)S(1)}, bf16[8,2,8,16,256]{4,3,2,1,0:T(8,128)(2,1)S(1)}, u32[]{:S(2)}, u32[]{:S(2)}) %collective-permute-start) | collective-permute-done | bytes 1048608 | tf_op jit(solution)/shard_map/ppermute | solution.py:202
  12.8 2.9 %collective-permute-start.1 = (bf16[2,2,8,16,256]{4,3,2,1,0:T(8,128)(2,1)S(1)}, bf16[2,2,8,16,256]{4,3,2,1,0:T(8,128)(2,1)S(1)}, u32[]{:S(2)}, u32[]{:S(2)}) collective-permute-start(bf16[2,2,8,16,256]{4,3,2,1,0:T(8,128)(2,1)S(1)} %pad_maximum_fusion), channel_id=1, source_target_pairs={{0,2},{1,3},{2,0},{3,1},{4,6},{5,7},{6,4},{7,5},{8,10},{9,11},{10,... | collective-permute-start | bytes 786440 | tf_op jit(solution)/shard_map/ppermute | solution.py:186
  15.8 2.7 %collective-permute-start.3 = (bf16[2,2,8,16,256]{4,3,2,1,0:T(8,128)(2,1)S(1)}, bf16[2,2,8,16,256]{4,3,2,1,0:T(8,128)(2,1)S(1)}, u32[]{:S(2)}, u32[]{:S(2)}) collective-permute-start(bf16[2,2,8,16,256]{4,3,2,1,0:T(8,128)(2,1)S(1)} %pad_maximum_fusion.4), channel_id=1, source_target_pairs={{0,8},{1,9},{2,10},{3,11},{4,12},{5,13},{6,14},{7,15},{8,0},{9,1},... | collective-permute-start | bytes 786440 | tf_op jit(solution)/shard_map/ppermute | solution.py:186
  18.5 1.6 %collective-permute-start.2 = (bf16[2,2,8,16,256]{4,3,2,1,0:T(8,128)(2,1)S(1)}, bf16[2,2,8,16,256]{4,3,2,1,0:T(8,128)(2,1)S(1)}, u32[]{:S(2)}, u32[]{:S(2)}) collective-permute-start(bf16[2,2,8,16,256]{4,3,2,1,0:T(8,128)(2,1)S(1)} %pad_maximum_fusion.2), channel_id=1, source_target_pairs={{0,4},{1,5},{2,6},{3,7},{4,0},{5,1},{6,2},{7,3},{8,12},{9,13},{10,... | collective-permute-start | bytes 786440 | tf_op jit(solution)/shard_map/ppermute | solution.py:186
  20.2 1.6 %collective-permute-start.6 = (bf16[2,2,8,16,256]{4,3,2,1,0:T(8,128)(2,1)S(1)}, bf16[2,2,8,16,256]{4,3,2,1,0:T(8,128)(2,1)S(1)}, u32[]{:S(2)}, u32[]{:S(2)}) collective-permute-start(bf16[2,2,8,16,256]{4,3,2,1,0:T(8,128)(2,1)S(1)} %pad_maximum_fusion.1.rest_0_), channel_id=1, source_target_pairs={{0,16},{16,0},{1,17},{17,1},{2,18},{18,2},{3,19},{19,3},{4,20},{20... | collective-permute-start | bytes 786440 | tf_op jit(solution)/shard_map/ppermute | solution.py:186
  22.4 1.8 %collective-permute-start.9 = (bf16[2,2,8,16,256]{4,3,2,1,0:T(8,128)(2,1)S(1)}, bf16[2,2,8,16,256]{4,3,2,1,0:T(8,128)(2,1)S(1)}, u32[]{:S(2)}, u32[]{:S(2)}) collective-permute-start(bf16[2,2,8,16,256]{4,3,2,1,0:T(8,128)(2,1)S(1)} %collective-permute-done.1.rest_1_), channel_id=1, source_target_pairs={{0,16},{16,0},{1,17},{17,1},{2,18},{18,2},{3,19},{19,3},{4,20},{20... | collective-permute-start | bytes 786440 | tf_op jit(solution)/shard_map/ppermute | solution.py:186
  24.1 6.4 %collective-permute-done.3.rest_4_ = bf16[2,2,8,16,256]{4,3,2,1,0:T(8,128)(2,1)S(1)} collective-permute-done((bf16[2,2,8,16,256]{4,3,2,1,0:T(8,128)(2,1)S(1)}, bf16[2,2,8,16,256]{4,3,2,1,0:T(8,128)(2,1)S(1)}, u32[]{:S(2)}, u32[]{:S(2)}) %collective-permute-start.3) | collective-permute-done | bytes 262176 | tf_op jit(solution)/shard_map/ppermute | solution.py:186
  31.1 4.3 %collective-permute-start.5 = (bf16[2,2,8,16,256]{4,3,2,1,0:T(8,128)(2,1)S(1)}, bf16[2,2,8,16,256]{4,3,2,1,0:T(8,128)(2,1)S(1)}, u32[]{:S(2)}, u32[]{:S(2)}) collective-permute-start(bf16[2,2,8,16,256]{4,3,2,1,0:T(8,128)(2,1)S(1)} %get-tuple-element.40), channel_id=1, source_target_pairs={{0,10},{1,11},{2,8},{3,9},{4,14},{5,15},{6,12},{7,13},{8,2},{9,3},... | collective-permute-start | bytes 786440 | tf_op jit(solution)/shard_map/ppermute | solution.py:186
  35.4 1.5 %collective-permute-start.7 = (bf16[2,2,8,16,256]{4,3,2,1,0:T(8,128)(2,1)S(1)}, bf16[2,2,8,16,256]{4,3,2,1,0:T(8,128)(2,1)S(1)}, u32[]{:S(2)}, u32[]{:S(2)}) collective-permute-start(bf16[2,2,8,16,256]{4,3,2,1,0:T(8,128)(2,1)S(1)} %collective-permute-done.2.rest_2_), channel_id=1, source_target_pairs={{0,16},{16,0},{1,17},{17,1},{2,18},{18,2},{3,19},{19,3},{4,20},{20... | collective-permute-start | bytes 786440 | tf_op jit(solution)/shard_map/ppermute | solution.py:186
  36.9 6.1 %collective-permute-done.4.rest_3_ = bf16[2,2,8,16,256]{4,3,2,1,0:T(8,128)(2,1)S(1)} collective-permute-done((bf16[2,2,8,16,256]{4,3,2,1,0:T(8,128)(2,1)S(1)}, bf16[2,2,8,16,256]{4,3,2,1,0:T(8,128)(2,1)S(1)}, u32[]{:S(2)}, u32[]{:S(2)}) %collective-permute-start.4) | collective-permute-done | bytes 262176 | tf_op jit(solution)/shard_map/ppermute | solution.py:186
  43.1 1.5 %collective-permute-start.12 = (bf16[2,2,8,16,256]{4,3,2,1,0:T(8,128)(2,1)S(1)}, bf16[2,2,8,16,256]{4,3,2,1,0:T(8,128)(2,1)S(1)}, u32[]{:S(2)}, u32[]{:S(2)}) collective-permute-start(bf16[2,2,8,16,256]{4,3,2,1,0:T(8,128)(2,1)S(1)} %collective-permute-done.4.rest_3_), channel_id=1, source_target_pairs={{0,16},{16,0},{1,17},{17,1},{2,18},{18,2},{3,19},{19,3},{4,20},{20... | collective-permute-start | bytes 786440 | tf_op jit(solution)/shard_map/ppermute | solution.py:186
  44.6 3.8 %collective-permute-start.10 = (bf16[2,2,5,16,256]{4,3,2,1,0:T(8,128)(2,1)S(1)}, bf16[2,2,5,16,256]{4,3,2,1,0:T(8,128)(2,1)S(1)}, u32[]{:S(2)}, u32[]{:S(2)}) collective-permute-start(bf16[2,2,5,16,256]{4,3,2,1,0:T(8,128)(2,1)S(1)} %pad_maximum_fusion.7), channel_id=1, source_target_pairs={{0,12},{1,13},{2,14},{3,15},{4,8},{5,9},{6,10},{7,11},{8,4},{9,5},... | collective-permute-start | bytes 491528 | tf_op jit(solution)/shard_map/ppermute | solution.py:186
  49.4 2.2 %collective-permute-start.15 = (bf16[2,2,8,16,256]{4,3,2,1,0:T(8,128)(2,1)S(1)}, bf16[2,2,8,16,256]{4,3,2,1,0:T(8,128)(2,1)S(1)}, u32[]{:S(2)}, u32[]{:S(2)}) collective-permute-start(bf16[2,2,8,16,256]{4,3,2,1,0:T(8,128)(2,1)S(1)} %collective-permute-done.5.rest_5_), channel_id=1, source_target_pairs={{0,16},{16,0},{1,17},{17,1},{2,18},{18,2},{3,19},{19,3},{4,20},{20... | collective-permute-start | bytes 786440 | tf_op jit(solution)/shard_map/ppermute | solution.py:186
  51.7 6.5 %collective-permute-start.13 = (bf16[2,2,5,16,256]{4,3,2,1,0:T(8,128)(2,1)S(1)}, bf16[2,2,5,16,256]{4,3,2,1,0:T(8,128)(2,1)S(1)}, u32[]{:S(2)}, u32[]{:S(2)}) collective-permute-start(bf16[2,2,5,16,256]{4,3,2,1,0:T(8,128)(2,1)S(1)} %pad_maximum_fusion.6), channel_id=1, source_target_pairs={{0,14},{1,15},{2,12},{3,13},{4,10},{5,11},{6,8},{7,9},{8,6},{9,7},... | collective-permute-start | bytes 491528 | tf_op jit(solution)/shard_map/ppermute | solution.py:186
  58.3 3.4 %collective-permute-start.11 = (bf16[2,2,3,16,256]{4,3,2,1,0:T(8,128)(2,1)S(1)}, bf16[2,2,3,16,256]{4,3,2,1,0:T(8,128)(2,1)S(1)}, u32[]{:S(2)}, u32[]{:S(2)}) collective-permute-start(bf16[2,2,3,16,256]{4,3,2,1,0:T(8,128)(2,1)S(1)} %pad_maximum_fusion.9), channel_id=1, source_target_pairs={{0,12},{1,13},{2,14},{3,15},{4,8},{5,9},{6,10},{7,11},{8,4},{9,5},... | collective-permute-start | bytes 294920 | tf_op jit(solution)/shard_map/ppermute | solution.py:186
  61.7 1.5 %collective-permute-start.16 = (bf16[2,2,5,16,256]{4,3,2,1,0:T(8,128)(2,1)S(1)}, bf16[2,2,5,16,256]{4,3,2,1,0:T(8,128)(2,1)S(1)}, u32[]{:S(2)}, u32[]{:S(2)}) collective-permute-start(bf16[2,2,5,16,256]{4,3,2,1,0:T(8,128)(2,1)S(1)} %collective-permute-done.10.rest_6_), channel_id=1, source_target_pairs={{0,16},{16,0},{1,17},{17,1},{2,18},{18,2},{3,19},{19,3},{4,20},{20... | collective-permute-start | bytes 491528 | tf_op jit(solution)/shard_map/ppermute | solution.py:186
  63.7 5.8 %collective-permute-start.14 = (bf16[2,2,3,16,256]{4,3,2,1,0:T(8,128)(2,1)S(1)}, bf16[2,2,3,16,256]{4,3,2,1,0:T(8,128)(2,1)S(1)}, u32[]{:S(2)}, u32[]{:S(2)}) collective-permute-start(bf16[2,2,3,16,256]{4,3,2,1,0:T(8,128)(2,1)S(1)} %pad_maximum_fusion.8), channel_id=1, source_target_pairs={{0,14},{1,15},{2,12},{3,13},{4,10},{5,11},{6,8},{7,9},{8,6},{9,7},... | collective-permute-start | bytes 294920 | tf_op jit(solution)/shard_map/ppermute | solution.py:186
  70.0 2.1 %collective-permute-done.14.rest_7_ = bf16[2,2,3,16,256]{4,3,2,1,0:T(8,128)(2,1)S(1)} collective-permute-done((bf16[2,2,3,16,256]{4,3,2,1,0:T(8,128)(2,1)S(1)}, bf16[2,2,3,16,256]{4,3,2,1,0:T(8,128)(2,1)S(1)}, u32[]{:S(2)}, u32[]{:S(2)}) %collective-permute-start.14) | collective-permute-done | bytes 98336 | tf_op jit(solution)/shard_map/ppermute | solution.py:186
  72.6 7.2 %cross.2.rest_16_ = bf16[8,2,256,8,256]{4,3,2,1,0:T(8,128)(2,1)} custom-call(bf16[1024,256]{1,0:T(8,128)(2,1)S(1)} %and_convert_fusion.select_ref, bf16[2,2,8,16,256]{4,3,2,1,0:T(8,128)(2,1)S(1)} %pad_maximum_fusion.1.rest_0_, bf16[2,2,8,16,256]{4,3,2,1,0:T(8,128)(2,1)S(1)} %collective-permute-done.1.rest_1_, ...), custom_call_target="tpu_custom_call" | custom-call | flops 1342177280 | bytes 10485760 | tf_op jit(solution)/shard_map/cross/pallas_call | solution.py:160
  79.9 4.9 %cross.3 = bf16[8,2,256,8,256]{4,3,2,1,0:T(8,128)(2,1)} custom-call(bf16[1024,256]{1,0:T(8,128)(2,1)S(1)} %and_convert_fusion.select_ref, bf16[2,2,8,16,256]{4,3,2,1,0:T(8,128)(2,1)S(1)} %pad_maximum_fusion.1.rest_0_, bf16[2,2,8,16,256]{4,3,2,1,0:T(8,128)(2,1)S(1)} %collective-permute-done.1.rest_1_, ...), custom_call_target="tpu_custom_call", output_to_operand_aliasing={{}: (17, {})} | custom-call | flops 805306368 | bytes 6291456 | tf_op jit(solution)/shard_map/cross/pallas_call | solution.py:160
  (40 shorter events, 5.1 us)
Async XLA Ops:
  0.0 0.9 %copy-start = (bf16[256,512]{1,0:T(8,128)(2,1)S(1)}, bf16[256,512]{1,0:T(8,128)(2,1)}, u32[]{:S(2)}) copy-start(bf16[256,512]{1,0:T(8,128)(2,1)} %constant.17.clone.basis_ref) | copy-start | bytes 786436
  1.0 0.7 copy-start.1
  9.9 2.8 %collective-permute-start = (bf16[8,2,8,16,256]{4,3,2,1,0:T(8,128)(2,1)S(1)}, bf16[8,2,8,16,256]{4,3,2,1,0:T(8,128)(2,1)S(1)}, u32[]{:S(2)}, u32[]{:S(2)}) collective-permute-start(bf16[8,2,8,16,256]{4,3,2,1,0:T(8,128)(2,1)S(1)} %get-tuple-element.31), channel_id=1, source_target_pairs={{0,1},{1,0},{2,3},{3,2},{4,5},{5,4},{6,7},{7,6},{8,9},{9,8},{10,11... | collective-permute-start | bytes 3145736 | tf_op jit(solution)/shard_map/ppermute | solution.py:202
  12.8 9.5 %collective-permute-start.1 = (bf16[2,2,8,16,256]{4,3,2,1,0:T(8,128)(2,1)S(1)}, bf16[2,2,8,16,256]{4,3,2,1,0:T(8,128)(2,1)S(1)}, u32[]{:S(2)}, u32[]{:S(2)}) collective-permute-start(bf16[2,2,8,16,256]{4,3,2,1,0:T(8,128)(2,1)S(1)} %pad_maximum_fusion), channel_id=1, source_target_pairs={{0,2},{1,3},{2,0},{3,1},{4,6},{5,7},{6,4},{7,5},{8,10},{9,11},{10,... | collective-permute-start | bytes 786440 | tf_op jit(solution)/shard_map/ppermute | solution.py:186
  15.8 14.8 %collective-permute-start.3 = (bf16[2,2,8,16,256]{4,3,2,1,0:T(8,128)(2,1)S(1)}, bf16[2,2,8,16,256]{4,3,2,1,0:T(8,128)(2,1)S(1)}, u32[]{:S(2)}, u32[]{:S(2)}) collective-permute-start(bf16[2,2,8,16,256]{4,3,2,1,0:T(8,128)(2,1)S(1)} %pad_maximum_fusion.4), channel_id=1, source_target_pairs={{0,8},{1,9},{2,10},{3,11},{4,12},{5,13},{6,14},{7,15},{8,0},{9,1},... | collective-permute-start | bytes 786440 | tf_op jit(solution)/shard_map/ppermute | solution.py:186
  18.5 16.9 %collective-permute-start.2 = (bf16[2,2,8,16,256]{4,3,2,1,0:T(8,128)(2,1)S(1)}, bf16[2,2,8,16,256]{4,3,2,1,0:T(8,128)(2,1)S(1)}, u32[]{:S(2)}, u32[]{:S(2)}) collective-permute-start(bf16[2,2,8,16,256]{4,3,2,1,0:T(8,128)(2,1)S(1)} %pad_maximum_fusion.2), channel_id=1, source_target_pairs={{0,4},{1,5},{2,6},{3,7},{4,0},{5,1},{6,2},{7,3},{8,12},{9,13},{10,... | collective-permute-start | bytes 786440 | tf_op jit(solution)/shard_map/ppermute | solution.py:186
  20.2 15.3 %collective-permute-start.6 = (bf16[2,2,8,16,256]{4,3,2,1,0:T(8,128)(2,1)S(1)}, bf16[2,2,8,16,256]{4,3,2,1,0:T(8,128)(2,1)S(1)}, u32[]{:S(2)}, u32[]{:S(2)}) collective-permute-start(bf16[2,2,8,16,256]{4,3,2,1,0:T(8,128)(2,1)S(1)} %pad_maximum_fusion.1.rest_0_), channel_id=1, source_target_pairs={{0,16},{16,0},{1,17},{17,1},{2,18},{18,2},{3,19},{19,3},{4,20},{20... | collective-permute-start | bytes 786440 | tf_op jit(solution)/shard_map/ppermute | solution.py:186
  22.4 14.6 %collective-permute-start.9 = (bf16[2,2,8,16,256]{4,3,2,1,0:T(8,128)(2,1)S(1)}, bf16[2,2,8,16,256]{4,3,2,1,0:T(8,128)(2,1)S(1)}, u32[]{:S(2)}, u32[]{:S(2)}) collective-permute-start(bf16[2,2,8,16,256]{4,3,2,1,0:T(8,128)(2,1)S(1)} %collective-permute-done.1.rest_1_), channel_id=1, source_target_pairs={{0,16},{16,0},{1,17},{17,1},{2,18},{18,2},{3,19},{19,3},{4,20},{20... | collective-permute-start | bytes 786440 | tf_op jit(solution)/shard_map/ppermute | solution.py:186
  30.6 12.5 %collective-permute-start.4 = (bf16[2,2,8,16,256]{4,3,2,1,0:T(8,128)(2,1)S(1)}, bf16[2,2,8,16,256]{4,3,2,1,0:T(8,128)(2,1)S(1)}, u32[]{:S(2)}, u32[]{:S(2)}) collective-permute-start(bf16[2,2,8,16,256]{4,3,2,1,0:T(8,128)(2,1)S(1)} %get-tuple-element.38), channel_id=1, source_target_pairs={{0,6},{1,7},{2,4},{3,5},{4,2},{5,3},{6,0},{7,1},{8,14},{9,15},{10,... | collective-permute-start | bytes 786440 | tf_op jit(solution)/shard_map/ppermute | solution.py:186
  31.1 17.8 %collective-permute-start.5 = (bf16[2,2,8,16,256]{4,3,2,1,0:T(8,128)(2,1)S(1)}, bf16[2,2,8,16,256]{4,3,2,1,0:T(8,128)(2,1)S(1)}, u32[]{:S(2)}, u32[]{:S(2)}) collective-permute-start(bf16[2,2,8,16,256]{4,3,2,1,0:T(8,128)(2,1)S(1)} %get-tuple-element.40), channel_id=1, source_target_pairs={{0,10},{1,11},{2,8},{3,9},{4,14},{5,15},{6,12},{7,13},{8,2},{9,3},... | collective-permute-start | bytes 786440 | tf_op jit(solution)/shard_map/ppermute | solution.py:186
  35.4 13.0 %collective-permute-start.7 = (bf16[2,2,8,16,256]{4,3,2,1,0:T(8,128)(2,1)S(1)}, bf16[2,2,8,16,256]{4,3,2,1,0:T(8,128)(2,1)S(1)}, u32[]{:S(2)}, u32[]{:S(2)}) collective-permute-start(bf16[2,2,8,16,256]{4,3,2,1,0:T(8,128)(2,1)S(1)} %collective-permute-done.2.rest_2_), channel_id=1, source_target_pairs={{0,16},{16,0},{1,17},{17,1},{2,18},{18,2},{3,19},{19,3},{4,20},{20... | collective-permute-start | bytes 786440 | tf_op jit(solution)/shard_map/ppermute | solution.py:186
  43.1 6.4 %collective-permute-start.12 = (bf16[2,2,8,16,256]{4,3,2,1,0:T(8,128)(2,1)S(1)}, bf16[2,2,8,16,256]{4,3,2,1,0:T(8,128)(2,1)S(1)}, u32[]{:S(2)}, u32[]{:S(2)}) collective-permute-start(bf16[2,2,8,16,256]{4,3,2,1,0:T(8,128)(2,1)S(1)} %collective-permute-done.4.rest_3_), channel_id=1, source_target_pairs={{0,16},{16,0},{1,17},{17,1},{2,18},{18,2},{3,19},{19,3},{4,20},{20... | collective-permute-start | bytes 786440 | tf_op jit(solution)/shard_map/ppermute | solution.py:186
  44.6 13.7 %collective-permute-start.10 = (bf16[2,2,5,16,256]{4,3,2,1,0:T(8,128)(2,1)S(1)}, bf16[2,2,5,16,256]{4,3,2,1,0:T(8,128)(2,1)S(1)}, u32[]{:S(2)}, u32[]{:S(2)}) collective-permute-start(bf16[2,2,5,16,256]{4,3,2,1,0:T(8,128)(2,1)S(1)} %pad_maximum_fusion.7), channel_id=1, source_target_pairs={{0,12},{1,13},{2,14},{3,15},{4,8},{5,9},{6,10},{7,11},{8,4},{9,5},... | collective-permute-start | bytes 491528 | tf_op jit(solution)/shard_map/ppermute | solution.py:186
  48.4 9.9 %collective-permute-start.8 = (bf16[2,2,8,16,256]{4,3,2,1,0:T(8,128)(2,1)S(1)}, bf16[2,2,8,16,256]{4,3,2,1,0:T(8,128)(2,1)S(1)}, u32[]{:S(2)}, u32[]{:S(2)}) collective-permute-start(bf16[2,2,8,16,256]{4,3,2,1,0:T(8,128)(2,1)S(1)} %collective-permute-done.3.rest_4_), channel_id=1, source_target_pairs={{0,16},{16,0},{1,17},{17,1},{2,18},{18,2},{3,19},{19,3},{4,20},{20... | collective-permute-start | bytes 786440 | tf_op jit(solution)/shard_map/ppermute | solution.py:186
  49.4 13.8 %collective-permute-start.15 = (bf16[2,2,8,16,256]{4,3,2,1,0:T(8,128)(2,1)S(1)}, bf16[2,2,8,16,256]{4,3,2,1,0:T(8,128)(2,1)S(1)}, u32[]{:S(2)}, u32[]{:S(2)}) collective-permute-start(bf16[2,2,8,16,256]{4,3,2,1,0:T(8,128)(2,1)S(1)} %collective-permute-done.5.rest_5_), channel_id=1, source_target_pairs={{0,16},{16,0},{1,17},{17,1},{2,18},{18,2},{3,19},{19,3},{4,20},{20... | collective-permute-start | bytes 786440 | tf_op jit(solution)/shard_map/ppermute | solution.py:186
  51.7 11.5 %collective-permute-start.13 = (bf16[2,2,5,16,256]{4,3,2,1,0:T(8,128)(2,1)S(1)}, bf16[2,2,5,16,256]{4,3,2,1,0:T(8,128)(2,1)S(1)}, u32[]{:S(2)}, u32[]{:S(2)}) collective-permute-start(bf16[2,2,5,16,256]{4,3,2,1,0:T(8,128)(2,1)S(1)} %pad_maximum_fusion.6), channel_id=1, source_target_pairs={{0,14},{1,15},{2,12},{3,13},{4,10},{5,11},{6,8},{7,9},{8,6},{9,7},... | collective-permute-start | bytes 491528 | tf_op jit(solution)/shard_map/ppermute | solution.py:186
  58.3 11.2 %collective-permute-start.11 = (bf16[2,2,3,16,256]{4,3,2,1,0:T(8,128)(2,1)S(1)}, bf16[2,2,3,16,256]{4,3,2,1,0:T(8,128)(2,1)S(1)}, u32[]{:S(2)}, u32[]{:S(2)}) collective-permute-start(bf16[2,2,3,16,256]{4,3,2,1,0:T(8,128)(2,1)S(1)} %pad_maximum_fusion.9), channel_id=1, source_target_pairs={{0,12},{1,13},{2,14},{3,15},{4,8},{5,9},{6,10},{7,11},{8,4},{9,5},... | collective-permute-start | bytes 294920 | tf_op jit(solution)/shard_map/ppermute | solution.py:186
  61.7 7.8 %collective-permute-start.16 = (bf16[2,2,5,16,256]{4,3,2,1,0:T(8,128)(2,1)S(1)}, bf16[2,2,5,16,256]{4,3,2,1,0:T(8,128)(2,1)S(1)}, u32[]{:S(2)}, u32[]{:S(2)}) collective-permute-start(bf16[2,2,5,16,256]{4,3,2,1,0:T(8,128)(2,1)S(1)} %collective-permute-done.10.rest_6_), channel_id=1, source_target_pairs={{0,16},{16,0},{1,17},{17,1},{2,18},{18,2},{3,19},{19,3},{4,20},{20... | collective-permute-start | bytes 491528 | tf_op jit(solution)/shard_map/ppermute | solution.py:186
  63.2 8.9 %collective-permute-start.18 = (bf16[2,2,5,16,256]{4,3,2,1,0:T(8,128)(2,1)S(1)}, bf16[2,2,5,16,256]{4,3,2,1,0:T(8,128)(2,1)S(1)}, u32[]{:S(2)}, u32[]{:S(2)}) collective-permute-start(bf16[2,2,5,16,256]{4,3,2,1,0:T(8,128)(2,1)S(1)} %collective-permute-done.13.rest_7_), channel_id=1, source_target_pairs={{0,16},{16,0},{1,17},{17,1},{2,18},{18,2},{3,19},{19,3},{4,20},{20... | collective-permute-start | bytes 491528 | tf_op jit(solution)/shard_map/ppermute | solution.py:186
  63.7 8.4 %collective-permute-start.14 = (bf16[2,2,3,16,256]{4,3,2,1,0:T(8,128)(2,1)S(1)}, bf16[2,2,3,16,256]{4,3,2,1,0:T(8,128)(2,1)S(1)}, u32[]{:S(2)}, u32[]{:S(2)}) collective-permute-start(bf16[2,2,3,16,256]{4,3,2,1,0:T(8,128)(2,1)S(1)} %pad_maximum_fusion.8), channel_id=1, source_target_pairs={{0,14},{1,15},{2,12},{3,13},{4,10},{5,11},{6,8},{7,9},{8,6},{9,7},... | collective-permute-start | bytes 294920 | tf_op jit(solution)/shard_map/ppermute | solution.py:186
  69.5 10.4 %collective-permute-start.17 = (bf16[2,2,3,16,256]{4,3,2,1,0:T(8,128)(2,1)S(1)}, bf16[2,2,3,16,256]{4,3,2,1,0:T(8,128)(2,1)S(1)}, u32[]{:S(2)}, u32[]{:S(2)}) collective-permute-start(bf16[2,2,3,16,256]{4,3,2,1,0:T(8,128)(2,1)S(1)} %collective-permute-done.11.rest_6_), channel_id=1, source_target_pairs={{0,16},{16,0},{1,17},{17,1},{2,18},{18,2},{3,19},{19,3},{4,20},{20... | collective-permute-start | bytes 294920 | tf_op jit(solution)/shard_map/ppermute | solution.py:186
  72.1 7.8 %collective-permute-start.19 = (bf16[2,2,3,16,256]{4,3,2,1,0:T(8,128)(2,1)S(1)}, bf16[2,2,3,16,256]{4,3,2,1,0:T(8,128)(2,1)S(1)}, u32[]{:S(2)}, u32[]{:S(2)}) collective-permute-start(bf16[2,2,3,16,256]{4,3,2,1,0:T(8,128)(2,1)S(1)} %collective-permute-done.14.rest_7_), channel_id=1, source_target_pairs={{0,16},{16,0},{1,17},{17,1},{2,18},{18,2},{3,19},{19,3},{4,20},{20... | collective-permute-start | bytes 294920 | tf_op jit(solution)/shard_map/ppermute | solution.py:186

commit v2 on v1

--- a/solution.py
+++ b/solution.py
@@ -10,9 +10,9 @@
 from jax.sharding import PartitionSpec as P
 
 F = 128
+LANES = 128
 K0 = 2
 PLANES = 4
-LANES = 128
 MIB = 1024 * 1024
 
 
@@ -26,13 +26,19 @@
     return np.where(imag == 1, -np.sin(phase), np.cos(phase))
 
 
+def swap_matrix(outer, inner):
+    shape = (inner * outer, inner * outer)
+    row, column = (lax.broadcasted_iota(jnp.int32, shape, axis) for axis in range(2))
+    source = (row % outer) * inner + row // outer
+    return (source == column).astype(jnp.float32).astype(jnp.bfloat16)
+
+
 def head_kernel(me_ref, wave_ref, valid_ref, basis_ref, *rest, parts):
-    out_refs, (held_ref, wide_ref, white_ref, sems) = rest[:-4], rest[-4:]
+    out_refs, (held_ref, gated_ref, white_ref, sems) = rest[:-4], rest[-4:]
     rows, segs, samples = wave_ref.shape
     half = samples // 2
     step, copies = 16, sems.shape[0]
     share = rows // copies
-    sample_tiles, row_tiles = samples // LANES, rows // LANES
 
     def copy(n):
         part = pl.ds(n * share, share)
@@ -40,51 +46,40 @@
 
     for n in range(copies):
         copy(n).start()
-    for n in range(copies):
-        copy(n).wait()
-
-        @pl.loop(n * share // step, (n + 1) * share // step)
-        def _(j):
-            block = held_ref[pl.ds(j * step, step)].astype(jnp.float32).reshape(step * segs, samples)
-            for q in range(sample_tiles):
-                wide_ref[q, pl.ds(pl.multiple_of(j * step * segs, step * segs), step * segs), :] = block[
-                    :, q * LANES : (q + 1) * LANES
-                ]
-
     valid_rows = valid_ref[...]
     valid_cols = valid_rows.T
-    times = lax.broadcasted_iota(jnp.int32, (rows, LANES), 1)
+    times = lax.broadcasted_iota(jnp.int32, (step * segs, samples), 1)
+    to_segs = swap_matrix(step, segs)
+    for first in range(0, rows, step):
+        if first % share == 0:
+            copy(first // share).wait()
+        block = held_ref[first : first + step].reshape(step * segs, samples)
+        block = jnp.dot(to_segs, block, preferred_element_type=jnp.float32)
+        count = jnp.concatenate([valid_cols[first : first + step, s : s + 1] for s in range(segs)], axis=0)
+        block = jnp.where(times < count, block, 0.0).astype(jnp.bfloat16)
+        gated_ref[:, first : first + step] = block.reshape(segs, step, samples)
+
     for s in range(segs):
-        count = valid_cols[:, s : s + 1]
-        gated = jnp.concatenate(
-            [
-                jnp.where(times + q * LANES < count, wide_ref[q, pl.ds(s, rows, stride=segs), :], 0.0)
-                for q in range(sample_tiles)
-            ],
-            axis=1,
-        ).astype(jnp.bfloat16)
         spectrum = lax.dot_general(
-            basis_ref[...], gated, (((1,), (1,)), ((), ())), preferred_element_type=jnp.float32
+            basis_ref[...], gated_ref[s], (((1,), (1,)), ((), ())), preferred_element_type=jnp.float32
         )
         power = jnp.sum(spectrum * spectrum, axis=0, keepdims=True) / F
         keep = (valid_rows[s : s + 1, :] >= half).astype(jnp.float32)
-        white = spectrum * (keep / jnp.sqrt(power + 1e-06))
-        for q in range(row_tiles):
-            white_ref[q, pl.ds(s, 2 * F, stride=segs), :] = white[:, q * LANES : (q + 1) * LANES]
+        white_ref[s] = spectrum * (keep / jnp.sqrt(power + 1e-06))
 
     me = me_ref[0]
-    bins_local = F // parts
-    span = bins_local * segs
-
-    def put(d, out_ref, index):
-        for part in range(2):
-            first = pl.multiple_of(((me ^ d) * 2 + part) * span, span)
-            piece = jnp.concatenate([white_ref[q, pl.ds(first, span), :] for q in range(row_tiles)], axis=1)
-            out_ref[index, part] = piece.astype(jnp.bfloat16).reshape(bins_local, segs, rows)
+    span = 2 * F // parts
+    to_bins = swap_matrix(segs, span)
+
+    def block_for(d):
+        first = pl.multiple_of((me ^ d) * span, span)
+        piece = jnp.concatenate([white_ref[s, pl.ds(first, span), :] for s in range(segs)], axis=0)
+        piece = jnp.dot(to_bins, piece.astype(jnp.bfloat16), preferred_element_type=jnp.float32)
+        return piece.astype(jnp.bfloat16).reshape(2, span // 2, segs, rows)
 
     for pair, out_ref in enumerate(out_refs[:-1]):
-        put(2 * pair, out_ref, 0)
-        put(2 * pair + 1, out_refs[-1], pair)
+        out_ref[0] = block_for(2 * pair)
+        out_refs[-1][pair] = block_for(2 * pair + 1)
 
 
 def head(waveform, valid_count, me, parts):
@@ -100,9 +95,9 @@
         out_specs=[vmem] * (pairs + 1),
         scratch_shapes=[
             pltpu.VMEM(waveform.shape, waveform.dtype),
-            pltpu.VMEM((samples // LANES, rows * segs, LANES), jnp.float32),
-            pltpu.VMEM((rows // LANES, 2 * F * segs, LANES), jnp.float32),
-            pltpu.SemaphoreType.DMA((4,)),
+            pltpu.VMEM((segs, rows, samples), jnp.bfloat16),
+            pltpu.VMEM((segs, 2 * F, rows), jnp.float32),
+            pltpu.SemaphoreType.DMA((8,)),
         ],
         compiler_params=pltpu.CompilerParams(vmem_limit_bytes=48 * MIB),
         name="spectra",
@@ -112,10 +107,21 @@
 def cross_kernel(select_ref, *rest, groups, held, low):
     pieces = len(held)
     sides = [rest[e * pieces : (e + 1) * pieces] for e in range(groups)]
-    out_ref = rest[-1]
-    _, _, rows, rounds, columns = out_ref.shape
+    out_ref, held_ref, sems = rest[-3:]
+    side_shape = sides[0][0].shape
+    rows, columns = side_shape[-1], side_shape[-1]
+    rounds, tiles_across = out_ref.shape[2] // (rows * (columns // LANES)), columns // LANES
     chunk = select_ref.shape[0] // rounds
-    k = low + pl.program_id(0)
+    step, last = pl.program_id(0), pl.num_programs(0) - 1
+    slot = step % 2
+    k = low + step
+    tiles = [(part, first) for part in range(2) for first in range(0, rows, chunk)]
+
+    def copy(n, slot, k):
+        part, first = tiles[n]
+        height = rounds * tiles_across
+        block = pl.ds(first * height, chunk * height)
+        return pltpu.make_async_copy(held_ref.at[slot, part, block], out_ref.at[k, part, block], sems.at[slot, n])
 
     def whole(e, part):
         return jnp.concatenate(
@@ -133,12 +139,33 @@
         right = jnp.concatenate([whole(e, 0), whole(e, 1)], axis=0)
         total = jnp.dot(left, right, preferred_element_type=jnp.float32) / float(seg_total)
         sums.append(total.astype(jnp.bfloat16))
-    for part in range(2):
-        for first in range(0, rows, chunk):
-            start = part * rows + first
-            values = jnp.concatenate([total[start : start + chunk] for total in sums], axis=0)
-            filled = jnp.dot(select_ref[...], values, preferred_element_type=jnp.float32)
-            out_ref[0, part, first : first + chunk] = filled.reshape(chunk, rounds, columns).astype(jnp.bfloat16)
+
+    @pl.when(step >= 2)
+    def _():
+        for n in range(len(tiles)):
+            copy(n, slot, k - 2).wait()
+
+    for n, (part, first) in enumerate(tiles):
+        start = part * rows + first
+        values = jnp.concatenate([total[start : start + chunk] for total in sums], axis=0)
+        filled = jnp.dot(select_ref[...], values, preferred_element_type=jnp.float32)
+        filled = filled.reshape(chunk, rounds, columns)
+        filled = jnp.stack([filled[:, :, q * LANES : (q + 1) * LANES] for q in range(tiles_across)], axis=1)
+        height = rounds * tiles_across
+        held_ref[slot, part, first * height : (first + chunk) * height] = filled.reshape(
+            chunk * height, LANES
+        ).astype(jnp.bfloat16)
+        copy(n, slot, k).start()
+
+    @pl.when(step == last)
+    def _():
+        for n in range(len(tiles)):
+            copy(n, slot, k).wait()
+
+    @pl.when((step == last) & (step > 0))
+    def _():
+        for n in range(len(tiles)):
+            copy(n, 1 - slot, k - 1).wait()
 
 
 def selection(offset, groups, rows):
@@ -160,9 +187,13 @@
     return pl.pallas_call(
         functools.partial(cross_kernel, groups=groups, held=held, low=low),
         grid=(bins,),
-        out_shape=jax.ShapeDtypeStruct((bins_local, 2, rows, rounds, rows), jnp.bfloat16),
-        in_specs=[vmem] * (1 + len(pieces)) + [pl.BlockSpec(memory_space=pl.ANY)] * aliased,
-        out_specs=pl.BlockSpec((1, 2, rows, rounds, rows), lambda b: (low + b, 0, 0, 0, 0)),
+        out_shape=jax.ShapeDtypeStruct((bins_local, 2, rows * rounds * (rows // LANES), LANES), jnp.bfloat16),
+        in_specs=[vmem] * (1 + len(pieces)) + [pl.BlockSpec(memory_space=pltpu.HBM)] * aliased,
+        out_specs=pl.BlockSpec(memory_space=pltpu.HBM),
+        scratch_shapes=[
+            pltpu.VMEM((2, 2, rows * rounds * (rows // LANES), LANES), jnp.bfloat16),
+            pltpu.SemaphoreType.DMA((2, 2 * rows * rounds // select.shape[0])),
+        ],
         input_output_aliases={1 + len(pieces): 0} if aliased else {},
         compiler_params=pltpu.CompilerParams(vmem_limit_bytes=40 * MIB),
         cost_estimate=pl.CostEstimate(
@@ -237,7 +268,9 @@
         held = [0] * whole + [low] * last
         chosen = [side[:whole] + side[whole + n * last :][:last] for side in sides]
         out = add_bins(out, select, chosen, held, low, high, bins_local, rounds)
-    return out
+    rows = waveform.shape[0]
+    out = out.reshape(bins_local, 2, rows, rows // LANES, rounds, LANES).transpose(0, 1, 2, 4, 3, 5)
+    return out.reshape(bins_local, 2, rows, rounds, rows)
 
 
 def solution(mesh):

time: 85 us -> 83.2 us (0.979)
  Pallas kernels: 20.3 us -> 18.5 us
    pallas_call x1, Pallas kernels: 8.23 us -> 6.18 us  [head(): pl.pallas_call(functools.partial(head_kernel, parts=parts), out_shape=[ja...]
where the time goes in v2:
time: 83.2 us; the launch traced here: 82.9 us
  starting transfers between devices  44.3 us (53%)
  Pallas kernels  18.5 us (22%)
  waiting for transfers between devices  16.8 us (20%)
  local copies, waits for them, and re-layouts  1.96 us (2%)
  other arithmetic  1.23 us (1%)
    ppermute x19, starting transfers between devices, send(): self.sent.append(lax.ppermute(block, axis, pairs))  43.8 us
    ppermute x19, waiting for transfers between devices, send(): self.sent.append(lax.ppermute(block, axis, pairs))  15.8 us
    pallas_call x2, Pallas kernels, add_bins(): pl.pallas_call(functools.partial(cross_kernel, groups=groups, held=held,...  12.3 us
    pallas_call x1, Pallas kernels, head(): pl.pallas_call(functools.partial(head_kernel, parts=parts), out_shape=[ja...  6.18 us
    unnamed x4, local copies, waits for them, and re-layouts  1.67 us
  transfers between devices with their start and end apart: 20, of which 6 were waited for; matrix products, arithmetic and copies ran while one was open for 2% of the time, Pallas kernels for 9%

profile of v2, /device:TPU:0, one launch (start us, length us, event | category | flops | bytes accessed | tf_op | source)
XLA Modules:
  0.0 82.9 jit_solution(10158828435708902923)
XLA Ops:
  0.0 0.9 %copy-done = bf16[256,512]{1,0:T(8,128)(2,1)S(1)} copy-done((bf16[256,512]{1,0:T(8,128)(2,1)S(1)}, bf16[256,512]{1,0:T(8,128)(2,1)}, u32[]{:S(2)}) %copy-start) | copy-done | bytes 262168
  1.0 0.7 copy-done.1
  1.7 6.2 %spectra.1 = (bf16[1,2,8,16,256]{4,3,2,1,0:T(8,128)(2,1)S(1)}, bf16[1,2,8,16,256]{4,3,2,1,0:T(8,128)(2,1)S(1)}, bf16[1,2,8,16,256]{4,3,2,1,0:T(8,128)(2,1)S(1)},...) custom-call(s32[1]{0:T(128)} %bitcast.me_ref, ...), custom_call_target="tpu_custom_call" | custom-call | tf_op jit(solution)/shard_map/spectra/pallas_call | solution.py:91
  8.4 0.7 xor_bitcast_fusion
  9.6 1.0 %collective-permute-done = bf16[8,2,8,16,256]{4,3,2,1,0:T(8,128)(2,1)S(1)} collective-permute-done((bf16[8,2,8,16,256]{4,3,2,1,0:T(8,128)(2,1)S(1)}, bf16[8,2,8,16,256]{4,3,2,1,0:T(8,128)(2,1)S(1)}, u32[]{:S(2)}, u32[]{:S(2)}) %collective-permute-start) | collective-permute-done | bytes 1048608 | tf_op jit(solution)/shard_map/ppermute | solution.py:233
  10.8 2.9 %collective-permute-start.1 = (bf16[2,2,8,16,256]{4,3,2,1,0:T(8,128)(2,1)S(1)}, bf16[2,2,8,16,256]{4,3,2,1,0:T(8,128)(2,1)S(1)}, u32[]{:S(2)}, u32[]{:S(2)}) collective-permute-start(bf16[2,2,8,16,256]{4,3,2,1,0:T(8,128)(2,1)S(1)} %pad_maximum_fusion), channel_id=1, source_target_pairs={{0,2},{1,3},{2,0},{3,1},{4,6},{5,7},{6,4},{7,5},{8,10},{9,11},{10,... | collective-permute-start | bytes 786440 | tf_op jit(solution)/shard_map/ppermute | solution.py:217
  13.8 2.7 %collective-permute-start.3 = (bf16[2,2,8,16,256]{4,3,2,1,0:T(8,128)(2,1)S(1)}, bf16[2,2,8,16,256]{4,3,2,1,0:T(8,128)(2,1)S(1)}, u32[]{:S(2)}, u32[]{:S(2)}) collective-permute-start(bf16[2,2,8,16,256]{4,3,2,1,0:T(8,128)(2,1)S(1)} %pad_maximum_fusion.4), channel_id=1, source_target_pairs={{0,8},{1,9},{2,10},{3,11},{4,12},{5,13},{6,14},{7,15},{8,0},{9,1},... | collective-permute-start | bytes 786440 | tf_op jit(solution)/shard_map/ppermute | solution.py:217
  16.4 1.7 %collective-permute-start.2 = (bf16[2,2,8,16,256]{4,3,2,1,0:T(8,128)(2,1)S(1)}, bf16[2,2,8,16,256]{4,3,2,1,0:T(8,128)(2,1)S(1)}, u32[]{:S(2)}, u32[]{:S(2)}) collective-permute-start(bf16[2,2,8,16,256]{4,3,2,1,0:T(8,128)(2,1)S(1)} %pad_maximum_fusion.2), channel_id=1, source_target_pairs={{0,4},{1,5},{2,6},{3,7},{4,0},{5,1},{6,2},{7,3},{8,12},{9,13},{10,... | collective-permute-start | bytes 786440 | tf_op jit(solution)/shard_map/ppermute | solution.py:217
  18.1 1.6 %collective-permute-start.6 = (bf16[2,2,8,16,256]{4,3,2,1,0:T(8,128)(2,1)S(1)}, bf16[2,2,8,16,256]{4,3,2,1,0:T(8,128)(2,1)S(1)}, u32[]{:S(2)}, u32[]{:S(2)}) collective-permute-start(bf16[2,2,8,16,256]{4,3,2,1,0:T(8,128)(2,1)S(1)} %pad_maximum_fusion.1.rest_0_), channel_id=1, source_target_pairs={{0,16},{16,0},{1,17},{17,1},{2,18},{18,2},{3,19},{19,3},{4,20},{20... | collective-permute-start | bytes 786440 | tf_op jit(solution)/shard_map/ppermute | solution.py:217
  20.3 1.8 %collective-permute-start.9 = (bf16[2,2,8,16,256]{4,3,2,1,0:T(8,128)(2,1)S(1)}, bf16[2,2,8,16,256]{4,3,2,1,0:T(8,128)(2,1)S(1)}, u32[]{:S(2)}, u32[]{:S(2)}) collective-permute-start(bf16[2,2,8,16,256]{4,3,2,1,0:T(8,128)(2,1)S(1)} %collective-permute-done.1.rest_1_), channel_id=1, source_target_pairs={{0,16},{16,0},{1,17},{17,1},{2,18},{18,2},{3,19},{19,3},{4,20},{20... | collective-permute-start | bytes 786440 | tf_op jit(solution)/shard_map/ppermute | solution.py:217
  22.1 6.4 %collective-permute-done.3.rest_4_ = bf16[2,2,8,16,256]{4,3,2,1,0:T(8,128)(2,1)S(1)} collective-permute-done((bf16[2,2,8,16,256]{4,3,2,1,0:T(8,128)(2,1)S(1)}, bf16[2,2,8,16,256]{4,3,2,1,0:T(8,128)(2,1)S(1)}, u32[]{:S(2)}, u32[]{:S(2)}) %collective-permute-start.3) | collective-permute-done | bytes 262176 | tf_op jit(solution)/shard_map/ppermute | solution.py:217
  29.1 4.3 %collective-permute-start.5 = (bf16[2,2,8,16,256]{4,3,2,1,0:T(8,128)(2,1)S(1)}, bf16[2,2,8,16,256]{4,3,2,1,0:T(8,128)(2,1)S(1)}, u32[]{:S(2)}, u32[]{:S(2)}) collective-permute-start(bf16[2,2,8,16,256]{4,3,2,1,0:T(8,128)(2,1)S(1)} %get-tuple-element.40), channel_id=1, source_target_pairs={{0,10},{1,11},{2,8},{3,9},{4,14},{5,15},{6,12},{7,13},{8,2},{9,3},... | collective-permute-start | bytes 786440 | tf_op jit(solution)/shard_map/ppermute | solution.py:217
  33.4 1.5 %collective-permute-start.7 = (bf16[2,2,8,16,256]{4,3,2,1,0:T(8,128)(2,1)S(1)}, bf16[2,2,8,16,256]{4,3,2,1,0:T(8,128)(2,1)S(1)}, u32[]{:S(2)}, u32[]{:S(2)}) collective-permute-start(bf16[2,2,8,16,256]{4,3,2,1,0:T(8,128)(2,1)S(1)} %collective-permute-done.2.rest_2_), channel_id=1, source_target_pairs={{0,16},{16,0},{1,17},{17,1},{2,18},{18,2},{3,19},{19,3},{4,20},{20... | collective-permute-start | bytes 786440 | tf_op jit(solution)/shard_map/ppermute | solution.py:217
  34.9 6.2 %collective-permute-done.4.rest_3_ = bf16[2,2,8,16,256]{4,3,2,1,0:T(8,128)(2,1)S(1)} collective-permute-done((bf16[2,2,8,16,256]{4,3,2,1,0:T(8,128)(2,1)S(1)}, bf16[2,2,8,16,256]{4,3,2,1,0:T(8,128)(2,1)S(1)}, u32[]{:S(2)}, u32[]{:S(2)}) %collective-permute-start.4) | collective-permute-done | bytes 262176 | tf_op jit(solution)/shard_map/ppermute | solution.py:217
  41.0 1.5 %collective-permute-start.12 = (bf16[2,2,8,16,256]{4,3,2,1,0:T(8,128)(2,1)S(1)}, bf16[2,2,8,16,256]{4,3,2,1,0:T(8,128)(2,1)S(1)}, u32[]{:S(2)}, u32[]{:S(2)}) collective-permute-start(bf16[2,2,8,16,256]{4,3,2,1,0:T(8,128)(2,1)S(1)} %collective-permute-done.4.rest_3_), channel_id=1, source_target_pairs={{0,16},{16,0},{1,17},{17,1},{2,18},{18,2},{3,19},{19,3},{4,20},{20... | collective-permute-start | bytes 786440 | tf_op jit(solution)/shard_map/ppermute | solution.py:217
  42.6 3.8 %collective-permute-start.10 = (bf16[2,2,5,16,256]{4,3,2,1,0:T(8,128)(2,1)S(1)}, bf16[2,2,5,16,256]{4,3,2,1,0:T(8,128)(2,1)S(1)}, u32[]{:S(2)}, u32[]{:S(2)}) collective-permute-start(bf16[2,2,5,16,256]{4,3,2,1,0:T(8,128)(2,1)S(1)} %pad_maximum_fusion.7), channel_id=1, source_target_pairs={{0,12},{1,13},{2,14},{3,15},{4,8},{5,9},{6,10},{7,11},{8,4},{9,5},... | collective-permute-start | bytes 491528 | tf_op jit(solution)/shard_map/ppermute | solution.py:217
  47.4 2.3 %collective-permute-start.15 = (bf16[2,2,8,16,256]{4,3,2,1,0:T(8,128)(2,1)S(1)}, bf16[2,2,8,16,256]{4,3,2,1,0:T(8,128)(2,1)S(1)}, u32[]{:S(2)}, u32[]{:S(2)}) collective-permute-start(bf16[2,2,8,16,256]{4,3,2,1,0:T(8,128)(2,1)S(1)} %collective-permute-done.5.rest_5_), channel_id=1, source_target_pairs={{0,16},{16,0},{1,17},{17,1},{2,18},{18,2},{3,19},{19,3},{4,20},{20... | collective-permute-start | bytes 786440 | tf_op jit(solution)/shard_map/ppermute | solution.py:217
  49.8 6.4 %collective-permute-start.13 = (bf16[2,2,5,16,256]{4,3,2,1,0:T(8,128)(2,1)S(1)}, bf16[2,2,5,16,256]{4,3,2,1,0:T(8,128)(2,1)S(1)}, u32[]{:S(2)}, u32[]{:S(2)}) collective-permute-start(bf16[2,2,5,16,256]{4,3,2,1,0:T(8,128)(2,1)S(1)} %pad_maximum_fusion.6), channel_id=1, source_target_pairs={{0,14},{1,15},{2,12},{3,13},{4,10},{5,11},{6,8},{7,9},{8,6},{9,7},... | collective-permute-start | bytes 491528 | tf_op jit(solution)/shard_map/ppermute | solution.py:217
  56.2 3.4 %collective-permute-start.11 = (bf16[2,2,3,16,256]{4,3,2,1,0:T(8,128)(2,1)S(1)}, bf16[2,2,3,16,256]{4,3,2,1,0:T(8,128)(2,1)S(1)}, u32[]{:S(2)}, u32[]{:S(2)}) collective-permute-start(bf16[2,2,3,16,256]{4,3,2,1,0:T(8,128)(2,1)S(1)} %pad_maximum_fusion.9), channel_id=1, source_target_pairs={{0,12},{1,13},{2,14},{3,15},{4,8},{5,9},{6,10},{7,11},{8,4},{9,5},... | collective-permute-start | bytes 294920 | tf_op jit(solution)/shard_map/ppermute | solution.py:217
  59.6 1.5 %collective-permute-start.16 = (bf16[2,2,5,16,256]{4,3,2,1,0:T(8,128)(2,1)S(1)}, bf16[2,2,5,16,256]{4,3,2,1,0:T(8,128)(2,1)S(1)}, u32[]{:S(2)}, u32[]{:S(2)}) collective-permute-start(bf16[2,2,5,16,256]{4,3,2,1,0:T(8,128)(2,1)S(1)} %collective-permute-done.10.rest_6_), channel_id=1, source_target_pairs={{0,16},{16,0},{1,17},{17,1},{2,18},{18,2},{3,19},{19,3},{4,20},{20... | collective-permute-start | bytes 491528 | tf_op jit(solution)/shard_map/ppermute | solution.py:217
  61.7 5.7 %collective-permute-start.14 = (bf16[2,2,3,16,256]{4,3,2,1,0:T(8,128)(2,1)S(1)}, bf16[2,2,3,16,256]{4,3,2,1,0:T(8,128)(2,1)S(1)}, u32[]{:S(2)}, u32[]{:S(2)}) collective-permute-start(bf16[2,2,3,16,256]{4,3,2,1,0:T(8,128)(2,1)S(1)} %pad_maximum_fusion.8), channel_id=1, source_target_pairs={{0,14},{1,15},{2,12},{3,13},{4,10},{5,11},{6,8},{7,9},{8,6},{9,7},... | collective-permute-start | bytes 294920 | tf_op jit(solution)/shard_map/ppermute | solution.py:217
  68.0 2.1 %collective-permute-done.14.rest_7_ = bf16[2,2,3,16,256]{4,3,2,1,0:T(8,128)(2,1)S(1)} collective-permute-done((bf16[2,2,3,16,256]{4,3,2,1,0:T(8,128)(2,1)S(1)}, bf16[2,2,3,16,256]{4,3,2,1,0:T(8,128)(2,1)S(1)}, u32[]{:S(2)}, u32[]{:S(2)}) %collective-permute-start.14) | collective-permute-done | bytes 98336 | tf_op jit(solution)/shard_map/ppermute | solution.py:217
  70.6 7.5 %cross.2.rest_16_ = bf16[8,2,4096,128]{3,2,1,0:T(8,128)(2,1)} custom-call(bf16[1024,256]{1,0:T(8,128)(2,1)S(1)} %and_convert_fusion.select_ref, bf16[2,2,8,16,256]{4,3,2,1,0:T(8,128)(2,1)S(1)} %pad_maximum_fusion.1.rest_0_, bf16[2,2,8,16,256]{4,3,2,1,0:T(8,128)(2,1)S(1)} %collective-permute-done.1.rest_1_, ...), custom_call_target="tpu_custom_call" | custom-call | flops 1342177280 | bytes 10485760 | tf_op jit(solution)/shard_map/cross/pallas_call | solution.py:187
  78.1 4.9 %cross.3 = bf16[8,2,4096,128]{3,2,1,0:T(8,128)(2,1)} custom-call(bf16[1024,256]{1,0:T(8,128)(2,1)S(1)} %and_convert_fusion.select_ref, bf16[2,2,8,16,256]{4,3,2,1,0:T(8,128)(2,1)S(1)} %pad_maximum_fusion.1.rest_0_, bf16[2,2,8,16,256]{4,3,2,1,0:T(8,128)(2,1)S(1)} %collective-permute-done.1.rest_1_, ...), custom_call_target="tpu_custom_call", output_to_operand_aliasing={{}: (17, {})} | custom-call | flops 805306368 | bytes 6291456 | tf_op jit(solution)/shard_map/cross/pallas_call | solution.py:187
  (40 shorter events, 5.2 us)
Async XLA Ops:
  0.0 0.9 %copy-start = (bf16[256,512]{1,0:T(8,128)(2,1)S(1)}, bf16[256,512]{1,0:T(8,128)(2,1)}, u32[]{:S(2)}) copy-start(bf16[256,512]{1,0:T(8,128)(2,1)} %constant.17.clone.basis_ref) | copy-start | bytes 786436
  1.0 0.7 copy-start.1
  7.9 2.8 %collective-permute-start = (bf16[8,2,8,16,256]{4,3,2,1,0:T(8,128)(2,1)S(1)}, bf16[8,2,8,16,256]{4,3,2,1,0:T(8,128)(2,1)S(1)}, u32[]{:S(2)}, u32[]{:S(2)}) collective-permute-start(bf16[8,2,8,16,256]{4,3,2,1,0:T(8,128)(2,1)S(1)} %get-tuple-element.31), channel_id=1, source_target_pairs={{0,1},{1,0},{2,3},{3,2},{4,5},{5,4},{6,7},{7,6},{8,9},{9,8},{10,11... | collective-permute-start | bytes 3145736 | tf_op jit(solution)/shard_map/ppermute | solution.py:233
  10.8 9.5 %collective-permute-start.1 = (bf16[2,2,8,16,256]{4,3,2,1,0:T(8,128)(2,1)S(1)}, bf16[2,2,8,16,256]{4,3,2,1,0:T(8,128)(2,1)S(1)}, u32[]{:S(2)}, u32[]{:S(2)}) collective-permute-start(bf16[2,2,8,16,256]{4,3,2,1,0:T(8,128)(2,1)S(1)} %pad_maximum_fusion), channel_id=1, source_target_pairs={{0,2},{1,3},{2,0},{3,1},{4,6},{5,7},{6,4},{7,5},{8,10},{9,11},{10,... | collective-permute-start | bytes 786440 | tf_op jit(solution)/shard_map/ppermute | solution.py:217
  13.8 14.8 %collective-permute-start.3 = (bf16[2,2,8,16,256]{4,3,2,1,0:T(8,128)(2,1)S(1)}, bf16[2,2,8,16,256]{4,3,2,1,0:T(8,128)(2,1)S(1)}, u32[]{:S(2)}, u32[]{:S(2)}) collective-permute-start(bf16[2,2,8,16,256]{4,3,2,1,0:T(8,128)(2,1)S(1)} %pad_maximum_fusion.4), channel_id=1, source_target_pairs={{0,8},{1,9},{2,10},{3,11},{4,12},{5,13},{6,14},{7,15},{8,0},{9,1},... | collective-permute-start | bytes 786440 | tf_op jit(solution)/shard_map/ppermute | solution.py:217
  16.4 16.9 %collective-permute-start.2 = (bf16[2,2,8,16,256]{4,3,2,1,0:T(8,128)(2,1)S(1)}, bf16[2,2,8,16,256]{4,3,2,1,0:T(8,128)(2,1)S(1)}, u32[]{:S(2)}, u32[]{:S(2)}) collective-permute-start(bf16[2,2,8,16,256]{4,3,2,1,0:T(8,128)(2,1)S(1)} %pad_maximum_fusion.2), channel_id=1, source_target_pairs={{0,4},{1,5},{2,6},{3,7},{4,0},{5,1},{6,2},{7,3},{8,12},{9,13},{10,... | collective-permute-start | bytes 786440 | tf_op jit(solution)/shard_map/ppermute | solution.py:217
  18.1 15.2 %collective-permute-start.6 = (bf16[2,2,8,16,256]{4,3,2,1,0:T(8,128)(2,1)S(1)}, bf16[2,2,8,16,256]{4,3,2,1,0:T(8,128)(2,1)S(1)}, u32[]{:S(2)}, u32[]{:S(2)}) collective-permute-start(bf16[2,2,8,16,256]{4,3,2,1,0:T(8,128)(2,1)S(1)} %pad_maximum_fusion.1.rest_0_), channel_id=1, source_target_pairs={{0,16},{16,0},{1,17},{17,1},{2,18},{18,2},{3,19},{19,3},{4,20},{20... | collective-permute-start | bytes 786440 | tf_op jit(solution)/shard_map/ppermute | solution.py:217
  20.3 14.5 %collective-permute-start.9 = (bf16[2,2,8,16,256]{4,3,2,1,0:T(8,128)(2,1)S(1)}, bf16[2,2,8,16,256]{4,3,2,1,0:T(8,128)(2,1)S(1)}, u32[]{:S(2)}, u32[]{:S(2)}) collective-permute-start(bf16[2,2,8,16,256]{4,3,2,1,0:T(8,128)(2,1)S(1)} %collective-permute-done.1.rest_1_), channel_id=1, source_target_pairs={{0,16},{16,0},{1,17},{17,1},{2,18},{18,2},{3,19},{19,3},{4,20},{20... | collective-permute-start | bytes 786440 | tf_op jit(solution)/shard_map/ppermute | solution.py:217
  28.5 12.5 %collective-permute-start.4 = (bf16[2,2,8,16,256]{4,3,2,1,0:T(8,128)(2,1)S(1)}, bf16[2,2,8,16,256]{4,3,2,1,0:T(8,128)(2,1)S(1)}, u32[]{:S(2)}, u32[]{:S(2)}) collective-permute-start(bf16[2,2,8,16,256]{4,3,2,1,0:T(8,128)(2,1)S(1)} %get-tuple-element.38), channel_id=1, source_target_pairs={{0,6},{1,7},{2,4},{3,5},{4,2},{5,3},{6,0},{7,1},{8,14},{9,15},{10,... | collective-permute-start | bytes 786440 | tf_op jit(solution)/shard_map/ppermute | solution.py:217
  29.1 17.8 %collective-permute-start.5 = (bf16[2,2,8,16,256]{4,3,2,1,0:T(8,128)(2,1)S(1)}, bf16[2,2,8,16,256]{4,3,2,1,0:T(8,128)(2,1)S(1)}, u32[]{:S(2)}, u32[]{:S(2)}) collective-permute-start(bf16[2,2,8,16,256]{4,3,2,1,0:T(8,128)(2,1)S(1)} %get-tuple-element.40), channel_id=1, source_target_pairs={{0,10},{1,11},{2,8},{3,9},{4,14},{5,15},{6,12},{7,13},{8,2},{9,3},... | collective-permute-start | bytes 786440 | tf_op jit(solution)/shard_map/ppermute | solution.py:217
  33.4 13.0 %collective-permute-start.7 = (bf16[2,2,8,16,256]{4,3,2,1,0:T(8,128)(2,1)S(1)}, bf16[2,2,8,16,256]{4,3,2,1,0:T(8,128)(2,1)S(1)}, u32[]{:S(2)}, u32[]{:S(2)}) collective-permute-start(bf16[2,2,8,16,256]{4,3,2,1,0:T(8,128)(2,1)S(1)} %collective-permute-done.2.rest_2_), channel_id=1, source_target_pairs={{0,16},{16,0},{1,17},{17,1},{2,18},{18,2},{3,19},{19,3},{4,20},{20... | collective-permute-start | bytes 786440 | tf_op jit(solution)/shard_map/ppermute | solution.py:217
  41.0 6.4 %collective-permute-start.12 = (bf16[2,2,8,16,256]{4,3,2,1,0:T(8,128)(2,1)S(1)}, bf16[2,2,8,16,256]{4,3,2,1,0:T(8,128)(2,1)S(1)}, u32[]{:S(2)}, u32[]{:S(2)}) collective-permute-start(bf16[2,2,8,16,256]{4,3,2,1,0:T(8,128)(2,1)S(1)} %collective-permute-done.4.rest_3_), channel_id=1, source_target_pairs={{0,16},{16,0},{1,17},{17,1},{2,18},{18,2},{3,19},{19,3},{4,20},{20... | collective-permute-start | bytes 786440 | tf_op jit(solution)/shard_map/ppermute | solution.py:217
  42.6 13.6 %collective-permute-start.10 = (bf16[2,2,5,16,256]{4,3,2,1,0:T(8,128)(2,1)S(1)}, bf16[2,2,5,16,256]{4,3,2,1,0:T(8,128)(2,1)S(1)}, u32[]{:S(2)}, u32[]{:S(2)}) collective-permute-start(bf16[2,2,5,16,256]{4,3,2,1,0:T(8,128)(2,1)S(1)} %pad_maximum_fusion.7), channel_id=1, source_target_pairs={{0,12},{1,13},{2,14},{3,15},{4,8},{5,9},{6,10},{7,11},{8,4},{9,5},... | collective-permute-start | bytes 491528 | tf_op jit(solution)/shard_map/ppermute | solution.py:217
  46.4 9.8 %collective-permute-start.8 = (bf16[2,2,8,16,256]{4,3,2,1,0:T(8,128)(2,1)S(1)}, bf16[2,2,8,16,256]{4,3,2,1,0:T(8,128)(2,1)S(1)}, u32[]{:S(2)}, u32[]{:S(2)}) collective-permute-start(bf16[2,2,8,16,256]{4,3,2,1,0:T(8,128)(2,1)S(1)} %collective-permute-done.3.rest_4_), channel_id=1, source_target_pairs={{0,16},{16,0},{1,17},{17,1},{2,18},{18,2},{3,19},{19,3},{4,20},{20... | collective-permute-start | bytes 786440 | tf_op jit(solution)/shard_map/ppermute | solution.py:217
  47.4 13.7 %collective-permute-start.15 = (bf16[2,2,8,16,256]{4,3,2,1,0:T(8,128)(2,1)S(1)}, bf16[2,2,8,16,256]{4,3,2,1,0:T(8,128)(2,1)S(1)}, u32[]{:S(2)}, u32[]{:S(2)}) collective-permute-start(bf16[2,2,8,16,256]{4,3,2,1,0:T(8,128)(2,1)S(1)} %collective-permute-done.5.rest_5_), channel_id=1, source_target_pairs={{0,16},{16,0},{1,17},{17,1},{2,18},{18,2},{3,19},{19,3},{4,20},{20... | collective-permute-start | bytes 786440 | tf_op jit(solution)/shard_map/ppermute | solution.py:217
  49.8 11.4 %collective-permute-start.13 = (bf16[2,2,5,16,256]{4,3,2,1,0:T(8,128)(2,1)S(1)}, bf16[2,2,5,16,256]{4,3,2,1,0:T(8,128)(2,1)S(1)}, u32[]{:S(2)}, u32[]{:S(2)}) collective-permute-start(bf16[2,2,5,16,256]{4,3,2,1,0:T(8,128)(2,1)S(1)} %pad_maximum_fusion.6), channel_id=1, source_target_pairs={{0,14},{1,15},{2,12},{3,13},{4,10},{5,11},{6,8},{7,9},{8,6},{9,7},... | collective-permute-start | bytes 491528 | tf_op jit(solution)/shard_map/ppermute | solution.py:217
  56.2 11.2 %collective-permute-start.11 = (bf16[2,2,3,16,256]{4,3,2,1,0:T(8,128)(2,1)S(1)}, bf16[2,2,3,16,256]{4,3,2,1,0:T(8,128)(2,1)S(1)}, u32[]{:S(2)}, u32[]{:S(2)}) collective-permute-start(bf16[2,2,3,16,256]{4,3,2,1,0:T(8,128)(2,1)S(1)} %pad_maximum_fusion.9), channel_id=1, source_target_pairs={{0,12},{1,13},{2,14},{3,15},{4,8},{5,9},{6,10},{7,11},{8,4},{9,5},... | collective-permute-start | bytes 294920 | tf_op jit(solution)/shard_map/ppermute | solution.py:217
  59.6 7.8 %collective-permute-start.16 = (bf16[2,2,5,16,256]{4,3,2,1,0:T(8,128)(2,1)S(1)}, bf16[2,2,5,16,256]{4,3,2,1,0:T(8,128)(2,1)S(1)}, u32[]{:S(2)}, u32[]{:S(2)}) collective-permute-start(bf16[2,2,5,16,256]{4,3,2,1,0:T(8,128)(2,1)S(1)} %collective-permute-done.10.rest_6_), channel_id=1, source_target_pairs={{0,16},{16,0},{1,17},{17,1},{2,18},{18,2},{3,19},{19,3},{4,20},{20... | collective-permute-start | bytes 491528 | tf_op jit(solution)/shard_map/ppermute | solution.py:217
  61.2 8.9 %collective-permute-start.18 = (bf16[2,2,5,16,256]{4,3,2,1,0:T(8,128)(2,1)S(1)}, bf16[2,2,5,16,256]{4,3,2,1,0:T(8,128)(2,1)S(1)}, u32[]{:S(2)}, u32[]{:S(2)}) collective-permute-start(bf16[2,2,5,16,256]{4,3,2,1,0:T(8,128)(2,1)S(1)} %collective-permute-done.13.rest_7_), channel_id=1, source_target_pairs={{0,16},{16,0},{1,17},{17,1},{2,18},{18,2},{3,19},{19,3},{4,20},{20... | collective-permute-start | bytes 491528 | tf_op jit(solution)/shard_map/ppermute | solution.py:217
  61.7 8.3 %collective-permute-start.14 = (bf16[2,2,3,16,256]{4,3,2,1,0:T(8,128)(2,1)S(1)}, bf16[2,2,3,16,256]{4,3,2,1,0:T(8,128)(2,1)S(1)}, u32[]{:S(2)}, u32[]{:S(2)}) collective-permute-start(bf16[2,2,3,16,256]{4,3,2,1,0:T(8,128)(2,1)S(1)} %pad_maximum_fusion.8), channel_id=1, source_target_pairs={{0,14},{1,15},{2,12},{3,13},{4,10},{5,11},{6,8},{7,9},{8,6},{9,7},... | collective-permute-start | bytes 294920 | tf_op jit(solution)/shard_map/ppermute | solution.py:217
  67.4 10.6 %collective-permute-start.17 = (bf16[2,2,3,16,256]{4,3,2,1,0:T(8,128)(2,1)S(1)}, bf16[2,2,3,16,256]{4,3,2,1,0:T(8,128)(2,1)S(1)}, u32[]{:S(2)}, u32[]{:S(2)}) collective-permute-start(bf16[2,2,3,16,256]{4,3,2,1,0:T(8,128)(2,1)S(1)} %collective-permute-done.11.rest_6_), channel_id=1, source_target_pairs={{0,16},{16,0},{1,17},{17,1},{2,18},{18,2},{3,19},{19,3},{4,20},{20... | collective-permute-start | bytes 294920 | tf_op jit(solution)/shard_map/ppermute | solution.py:217
  70.0 8.0 %collective-permute-start.19 = (bf16[2,2,3,16,256]{4,3,2,1,0:T(8,128)(2,1)S(1)}, bf16[2,2,3,16,256]{4,3,2,1,0:T(8,128)(2,1)S(1)}, u32[]{:S(2)}, u32[]{:S(2)}) collective-permute-start(bf16[2,2,3,16,256]{4,3,2,1,0:T(8,128)(2,1)S(1)} %collective-permute-done.14.rest_7_), channel_id=1, source_target_pairs={{0,16},{16,0},{1,17},{17,1},{2,18},{18,2},{3,19},{19,3},{4,20},{20... | collective-permute-start | bytes 294920 | tf_op jit(solution)/shard_map/ppermute | solution.py:217

commit v3 on v2

--- a/solution.py
+++ b/solution.py
@@ -252,22 +252,27 @@
     own_blocks = [scatter(seg_lane, n) for n in own[1:]]
     own_blocks, select = lax.optimization_barrier((own_blocks, select))
     own_done = forward(own_blocks)
-    far_blocks = [scatter(far_lane, n, after=own_blocks if n > far[0] else ()) for n in far]
-    beside_blocks = [scatter(seg_lane, n, after=far_blocks[:1] if n > beside[0] else ()) for n in beside]
-    beside_done = [forward([block]) for block in beside_blocks][-1]
-    far_done = [forward([block]) for block in far_blocks]
-    waits = {(0, farthest[0]): [own_done], (0, farthest[-1]): [beside_done]}
-    waits[middle, farthest[0]] = [far_done[0]]
-    for low, high in ((0, middle), (middle, bins_local)):
-        for n in farthest:
-            forward([scatter(far_lane, n, low, high, waits.get((low, n), ()))])
-
-    out = None
-    whole, last = len(sides[0]) - 2 * chips, chips
-    for n, (low, high) in enumerate(((0, middle), (middle, bins_local))):
-        held = [0] * whole + [low] * last
-        chosen = [side[:whole] + side[whole + n * last :][:last] for side in sides]
-        out = add_bins(out, select, chosen, held, low, high, bins_local, rounds)
+    waits = {(0, n): own_blocks for n in far[1:]}
+    first = [scatter(far_lane, n, 0, middle, waits.get((0, n), ())) for n in far]
+    beside_blocks = [scatter(seg_lane, n, after=first[:1] if n > beside[0] else ()) for n in beside]
+    beside_done = [forward([block]) for block in beside_blocks]
+    far_done = forward(first)
+    first = [scatter(far_lane, n, 0, middle, beside_done[:1] if n == farthest[-1] else ()) for n in farthest]
+    last_done = [forward([block]) for block in first]
+    second = [scatter(far_lane, far[0], middle, bins_local, beside_done[-1:])]
+    second += [scatter(far_lane, n, middle, bins_local, [far_done]) for n in far[1:]]
+    forward(second)
+    split = 1 + chips
+    whole = len(sides[0]) - 1 - split
+    out = add_bins(
+        None, select, [side[: whole + split] for side in sides], [0] * (whole + split), 0, middle, bins_local, rounds
+    )
+    second = [scatter(far_lane, n, middle, bins_local, last_done[:1]) for n in farthest]
+    second[0], out = lax.optimization_barrier((second[0], out))
+    for block in second:
+        forward([block])
+    chosen = [side[:whole] + side[-split:] for side in sides]
+    out = add_bins(out, select, chosen, [0] * whole + [middle] * split, middle, bins_local, bins_local, rounds)
     rows = waveform.shape[0]
     out = out.reshape(bins_local, 2, rows, rows // LANES, rounds, LANES).transpose(0, 1, 2, 4, 3, 5)
     return out.reshape(bins_local, 2, rows, rounds, rows)

time: 83.2 us -> 83.1 us (level)
  starting transfers between devices: 44.3 us -> 38.1 us
  waiting for transfers between devices: 16.8 us -> 22.9 us
    ppermute x19 -> x21, starting transfers between devices: 43.8 us -> 37.5 us  [send(): self.sent.append(lax.ppermute(block, axis, pairs))]
    ppermute x19 -> x21, waiting for transfers between devices: 15.8 us -> 21.5 us  [send(): self.sent.append(lax.ppermute(block, axis, pairs))]
    unnamed x4 -> x6, local copies, waits for them, and re-layouts: 1.67 us -> 1.69 us
  transfers between devices with their start and end apart: 20 -> 22, of which waited for: 6 -> 10; matrix products, arithmetic and copies ran while one was open for 2% -> 2% of each run, Pallas kernels for 9% -> 9%
where the time goes in v3:
time: 83.1 us; the launch traced here: 82.8 us
  starting transfers between devices  38.1 us (46%)
  waiting for transfers between devices  22.9 us (28%)
  Pallas kernels  18.5 us (22%)
  local copies, waits for them, and re-layouts  2 us (2%)
  other arithmetic  1.23 us (1%)
    ppermute x21, starting transfers between devices, send(): self.sent.append(lax.ppermute(block, axis, pairs))  37.5 us
    ppermute x21, waiting for transfers between devices, send(): self.sent.append(lax.ppermute(block, axis, pairs))  21.5 us
    pallas_call x2, Pallas kernels, add_bins(): pl.pallas_call(functools.partial(cross_kernel, groups=groups, held=held,...  12.3 us
    pallas_call x1, Pallas kernels, head(): pl.pallas_call(functools.partial(head_kernel, parts=parts), out_shape=[ja...  6.18 us
    unnamed x6, local copies, waits for them, and re-layouts  1.69 us
  transfers between devices with their start and end apart: 22, of which 10 were waited for; matrix products, arithmetic and copies ran while one was open for 2% of the time, Pallas kernels for 9%

profile of v3, /device:TPU:0, one launch (start us, length us, event | category | flops | bytes accessed | tf_op | source)
XLA Modules:
  0.0 82.8 jit_solution(11069077083990320944)
XLA Ops:
  1.7 6.2 %spectra.1 = (bf16[1,2,8,16,256]{4,3,2,1,0:T(8,128)(2,1)S(1)}, bf16[1,2,8,16,256]{4,3,2,1,0:T(8,128)(2,1)S(1)}, bf16[1,2,8,16,256]{4,3,2,1,0:T(8,128)(2,1)S(1)},...) custom-call(s32[1]{0:T(128)} %bitcast.me_ref, ...), custom_call_target="tpu_custom_call" | custom-call | tf_op jit(solution)/shard_map/spectra/pallas_call | solution.py:91
  9.3 1.4 %collective-permute-done = bf16[8,2,8,16,256]{4,3,2,1,0:T(8,128)(2,1)S(1)} collective-permute-done((bf16[8,2,8,16,256]{4,3,2,1,0:T(8,128)(2,1)S(1)}, bf16[8,2,8,16,256]{4,3,2,1,0:T(8,128)(2,1)S(1)}, u32[]{:S(2)}, u32[]{:S(2)}) %collective-permute-start) | collective-permute-done | bytes 1048608 | tf_op jit(solution)/shard_map/ppermute | solution.py:233
  10.8 4.1 %collective-permute-start.3 = (bf16[2,2,5,16,256]{4,3,2,1,0:T(8,128)(2,1)S(1)}, bf16[2,2,5,16,256]{4,3,2,1,0:T(8,128)(2,1)S(1)}, u32[]{:S(2)}, u32[]{:S(2)}) collective-permute-start(bf16[2,2,5,16,256]{4,3,2,1,0:T(8,128)(2,1)S(1)} %fusion.2), channel_id=1, source_target_pairs={{0,8},{1,9},{2,10},{3,11},{4,12},{5,13},{6,14},{7,15},{8,0},{9,1},... | collective-permute-start | bytes 491528 | tf_op jit(solution)/shard_map/ppermute | solution.py:217
  14.9 1.5 %collective-permute-start.1 = (bf16[2,2,8,16,256]{4,3,2,1,0:T(8,128)(2,1)S(1)}, bf16[2,2,8,16,256]{4,3,2,1,0:T(8,128)(2,1)S(1)}, u32[]{:S(2)}, u32[]{:S(2)}) collective-permute-start(bf16[2,2,8,16,256]{4,3,2,1,0:T(8,128)(2,1)S(1)} %pad_maximum_fusion), channel_id=1, source_target_pairs={{0,2},{1,3},{2,0},{3,1},{4,6},{5,7},{6,4},{7,5},{8,10},{9,11},{10,... | collective-permute-start | bytes 786440 | tf_op jit(solution)/shard_map/ppermute | solution.py:217
  16.4 1.7 %collective-permute-start.2 = (bf16[2,2,8,16,256]{4,3,2,1,0:T(8,128)(2,1)S(1)}, bf16[2,2,8,16,256]{4,3,2,1,0:T(8,128)(2,1)S(1)}, u32[]{:S(2)}, u32[]{:S(2)}) collective-permute-start(bf16[2,2,8,16,256]{4,3,2,1,0:T(8,128)(2,1)S(1)} %pad_maximum_fusion.2), channel_id=1, source_target_pairs={{0,4},{1,5},{2,6},{3,7},{4,0},{5,1},{6,2},{7,3},{8,12},{9,13},{10,... | collective-permute-start | bytes 786440 | tf_op jit(solution)/shard_map/ppermute | solution.py:217
  18.1 1.6 %collective-permute-start.10 = (bf16[2,2,8,16,256]{4,3,2,1,0:T(8,128)(2,1)S(1)}, bf16[2,2,8,16,256]{4,3,2,1,0:T(8,128)(2,1)S(1)}, u32[]{:S(2)}, u32[]{:S(2)}) collective-permute-start(bf16[2,2,8,16,256]{4,3,2,1,0:T(8,128)(2,1)S(1)} %pad_maximum_fusion.1.rest_0_), channel_id=1, source_target_pairs={{0,16},{16,0},{1,17},{17,1},{2,18},{18,2},{3,19},{19,3},{4,20},{20... | collective-permute-start | bytes 786440 | tf_op jit(solution)/shard_map/ppermute | solution.py:217
  20.1 2.9 %collective-permute-done.3 = bf16[2,2,5,16,256]{4,3,2,1,0:T(8,128)(2,1)S(1)} collective-permute-done((bf16[2,2,5,16,256]{4,3,2,1,0:T(8,128)(2,1)S(1)}, bf16[2,2,5,16,256]{4,3,2,1,0:T(8,128)(2,1)S(1)}, u32[]{:S(2)}, u32[]{:S(2)}) %collective-permute-start.3) | collective-permute-done | bytes 163872 | tf_op jit(solution)/shard_map/ppermute | solution.py:217
  23.0 1.6 %collective-permute-start.4 = (bf16[2,2,8,16,256]{4,3,2,1,0:T(8,128)(2,1)S(1)}, bf16[2,2,8,16,256]{4,3,2,1,0:T(8,128)(2,1)S(1)}, u32[]{:S(2)}, u32[]{:S(2)}) collective-permute-start(bf16[2,2,8,16,256]{4,3,2,1,0:T(8,128)(2,1)S(1)} %pad_maximum_fusion.3), channel_id=1, source_target_pairs={{0,6},{1,7},{2,4},{3,5},{4,2},{5,3},{6,0},{7,1},{8,14},{9,15},{10,... | collective-permute-start | bytes 786440 | tf_op jit(solution)/shard_map/ppermute | solution.py:217
  24.5 1.5 %collective-permute-start.5 = (bf16[2,2,8,16,256]{4,3,2,1,0:T(8,128)(2,1)S(1)}, bf16[2,2,8,16,256]{4,3,2,1,0:T(8,128)(2,1)S(1)}, u32[]{:S(2)}, u32[]{:S(2)}) collective-permute-start(bf16[2,2,8,16,256]{4,3,2,1,0:T(8,128)(2,1)S(1)} %collective-permute-done.1.rest_1_), channel_id=1, source_target_pairs={{0,16},{16,0},{1,17},{17,1},{2,18},{18,2},{3,19},{19,3},{4,20},{20... | collective-permute-start | bytes 786440 | tf_op jit(solution)/shard_map/ppermute | solution.py:217
  26.1 3.5 %collective-permute-start.9 = (bf16[2,2,5,16,256]{4,3,2,1,0:T(8,128)(2,1)S(1)}, bf16[2,2,5,16,256]{4,3,2,1,0:T(8,128)(2,1)S(1)}, u32[]{:S(2)}, u32[]{:S(2)}) collective-permute-start(bf16[2,2,5,16,256]{4,3,2,1,0:T(8,128)(2,1)S(1)} %get-tuple-element.48), channel_id=1, source_target_pairs={{0,10},{1,11},{2,8},{3,9},{4,14},{5,15},{6,12},{7,13},{8,2},{9,3},... | collective-permute-start | bytes 491528 | tf_op jit(solution)/shard_map/ppermute | solution.py:217
  30.7 4.5 %collective-permute-done.4.rest_3_ = bf16[2,2,8,16,256]{4,3,2,1,0:T(8,128)(2,1)S(1)} collective-permute-done((bf16[2,2,8,16,256]{4,3,2,1,0:T(8,128)(2,1)S(1)}, bf16[2,2,8,16,256]{4,3,2,1,0:T(8,128)(2,1)S(1)}, u32[]{:S(2)}, u32[]{:S(2)}) %collective-permute-start.4) | collective-permute-done | bytes 262176 | tf_op jit(solution)/shard_map/ppermute | solution.py:217
  35.2 2.1 %collective-permute-start.6 = (bf16[2,2,8,16,256]{4,3,2,1,0:T(8,128)(2,1)S(1)}, bf16[2,2,8,16,256]{4,3,2,1,0:T(8,128)(2,1)S(1)}, u32[]{:S(2)}, u32[]{:S(2)}) collective-permute-start(bf16[2,2,8,16,256]{4,3,2,1,0:T(8,128)(2,1)S(1)} %collective-permute-done.4.rest_3_), channel_id=1, source_target_pairs={{0,16},{16,0},{1,17},{17,1},{2,18},{18,2},{3,19},{19,3},{4,20},{20... | collective-permute-start | bytes 786440 | tf_op jit(solution)/shard_map/ppermute | solution.py:217
  37.3 4.8 %collective-permute-done.9 = bf16[2,2,5,16,256]{4,3,2,1,0:T(8,128)(2,1)S(1)} collective-permute-done((bf16[2,2,5,16,256]{4,3,2,1,0:T(8,128)(2,1)S(1)}, bf16[2,2,5,16,256]{4,3,2,1,0:T(8,128)(2,1)S(1)}, u32[]{:S(2)}, u32[]{:S(2)}) %collective-permute-start.9) | collective-permute-done | bytes 163872 | tf_op jit(solution)/shard_map/ppermute | solution.py:217
  42.2 3.5 %collective-permute-start.13 = (bf16[2,2,5,16,256]{4,3,2,1,0:T(8,128)(2,1)S(1)}, bf16[2,2,5,16,256]{4,3,2,1,0:T(8,128)(2,1)S(1)}, u32[]{:S(2)}, u32[]{:S(2)}) collective-permute-start(bf16[2,2,5,16,256]{4,3,2,1,0:T(8,128)(2,1)S(1)} %fusion), channel_id=1, source_target_pairs={{0,14},{1,15},{2,12},{3,13},{4,10},{5,11},{6,8},{7,9},{8,6},{9,7},... | collective-permute-start | bytes 491528 | tf_op jit(solution)/shard_map/ppermute | solution.py:217
  45.7 2.7 %collective-permute-start.8 = (bf16[2,2,3,16,256]{4,3,2,1,0:T(8,128)(2,1)S(1)}, bf16[2,2,3,16,256]{4,3,2,1,0:T(8,128)(2,1)S(1)}, u32[]{:S(2)}, u32[]{:S(2)}) collective-permute-start(bf16[2,2,3,16,256]{4,3,2,1,0:T(8,128)(2,1)S(1)} %pad_maximum_fusion.8), channel_id=1, source_target_pairs={{0,8},{1,9},{2,10},{3,11},{4,12},{5,13},{6,14},{7,15},{8,0},{9,1},... | collective-permute-start | bytes 294920 | tf_op jit(solution)/shard_map/ppermute | solution.py:217
  48.4 1.6 %collective-permute-start.15 = (bf16[2,2,5,16,256]{4,3,2,1,0:T(8,128)(2,1)S(1)}, bf16[2,2,5,16,256]{4,3,2,1,0:T(8,128)(2,1)S(1)}, u32[]{:S(2)}, u32[]{:S(2)}) collective-permute-start(bf16[2,2,5,16,256]{4,3,2,1,0:T(8,128)(2,1)S(1)} %collective-permute-done.7.rest_5_), channel_id=1, source_target_pairs={{0,16},{16,0},{1,17},{17,1},{2,18},{18,2},{3,19},{19,3},{4,20},{20... | collective-permute-start | bytes 491528 | tf_op jit(solution)/shard_map/ppermute | solution.py:217
  50.4 2.1 %collective-permute-done.12.rest_11_ = bf16[4,2,5,16,256]{4,3,2,1,0:T(8,128)(2,1)S(1)} collective-permute-done((bf16[4,2,5,16,256]{4,3,2,1,0:T(8,128)(2,1)S(1)}, bf16[4,2,5,16,256]{4,3,2,1,0:T(8,128)(2,1)S(1)}, u32[]{:S(2)}, u32[]{:S(2)}) %collective-permute-start.12) | collective-permute-done | bytes 327712 | tf_op jit(solution)/shard_map/ppermute | solution.py:217
  52.5 4.1 %collective-permute-start.14 = (bf16[2,2,3,16,256]{4,3,2,1,0:T(8,128)(2,1)S(1)}, bf16[2,2,3,16,256]{4,3,2,1,0:T(8,128)(2,1)S(1)}, u32[]{:S(2)}, u32[]{:S(2)}) collective-permute-start(bf16[2,2,3,16,256]{4,3,2,1,0:T(8,128)(2,1)S(1)} %pad_maximum_fusion.7), channel_id=1, source_target_pairs={{0,10},{1,11},{2,8},{3,9},{4,14},{5,15},{6,12},{7,13},{8,2},{9,3},... | collective-permute-start | bytes 294920 | tf_op jit(solution)/shard_map/ppermute | solution.py:217
  57.3 2.9 %collective-permute-done.14 = bf16[2,2,3,16,256]{4,3,2,1,0:T(8,128)(2,1)S(1)} collective-permute-done((bf16[2,2,3,16,256]{4,3,2,1,0:T(8,128)(2,1)S(1)}, bf16[2,2,3,16,256]{4,3,2,1,0:T(8,128)(2,1)S(1)}, u32[]{:S(2)}, u32[]{:S(2)}) %collective-permute-start.14) | collective-permute-done | bytes 98336 | tf_op jit(solution)/shard_map/ppermute | solution.py:217
  61.2 1.7 %collective-permute-start.16 = (bf16[2,2,3,16,256]{4,3,2,1,0:T(8,128)(2,1)S(1)}, bf16[2,2,3,16,256]{4,3,2,1,0:T(8,128)(2,1)S(1)}, u32[]{:S(2)}, u32[]{:S(2)}) collective-permute-start(bf16[2,2,3,16,256]{4,3,2,1,0:T(8,128)(2,1)S(1)} %pad_maximum_fusion.6), channel_id=1, source_target_pairs={{0,12},{1,13},{2,14},{3,15},{4,8},{5,9},{6,10},{7,11},{8,4},{9,5},... | collective-permute-start | bytes 294920 | tf_op jit(solution)/shard_map/ppermute | solution.py:217
  62.9 1.7 %collective-permute-start.18 = (bf16[2,2,3,16,256]{4,3,2,1,0:T(8,128)(2,1)S(1)}, bf16[2,2,3,16,256]{4,3,2,1,0:T(8,128)(2,1)S(1)}, u32[]{:S(2)}, u32[]{:S(2)}) collective-permute-start(bf16[2,2,3,16,256]{4,3,2,1,0:T(8,128)(2,1)S(1)} %pad_maximum_fusion.5), channel_id=1, source_target_pairs={{0,14},{1,15},{2,12},{3,13},{4,10},{5,11},{6,8},{7,9},{8,6},{9,7},... | collective-permute-start | bytes 294920 | tf_op jit(solution)/shard_map/ppermute | solution.py:217
  64.7 7.5 %cross.2.rest_14_ = bf16[8,2,4096,128]{3,2,1,0:T(8,128)(2,1)} custom-call(bf16[1024,256]{1,0:T(8,128)(2,1)S(1)} %and_convert_fusion.select_ref, bf16[2,2,8,16,256]{4,3,2,1,0:T(8,128)(2,1)S(1)} %pad_maximum_fusion.1.rest_0_, bf16[2,2,8,16,256]{4,3,2,1,0:T(8,128)(2,1)S(1)} %collective-permute-done.1.rest_1_, ...), custom_call_target="tpu_custom_call" | custom-call | flops 1342177280 | bytes 10485760 | tf_op jit(solution)/shard_map/cross/pallas_call | solution.py:187
  74.2 2.6 %collective-permute-done.20.rest_12_ = bf16[2,2,3,16,256]{4,3,2,1,0:T(8,128)(2,1)S(1)} collective-permute-done((bf16[2,2,3,16,256]{4,3,2,1,0:T(8,128)(2,1)S(1)}, bf16[2,2,3,16,256]{4,3,2,1,0:T(8,128)(2,1)S(1)}, u32[]{:S(2)}, u32[]{:S(2)}) %collective-permute-start.20) | collective-permute-done | bytes 98336 | tf_op jit(solution)/shard_map/ppermute | solution.py:217
  78.0 4.8 %cross.3 = bf16[8,2,4096,128]{3,2,1,0:T(8,128)(2,1)} custom-call(bf16[1024,256]{1,0:T(8,128)(2,1)S(1)} %and_convert_fusion.select_ref, bf16[2,2,8,16,256]{4,3,2,1,0:T(8,128)(2,1)S(1)} %pad_maximum_fusion.1.rest_0_, bf16[2,2,8,16,256]{4,3,2,1,0:T(8,128)(2,1)S(1)} %collective-permute-done.1.rest_1_, ...), custom_call_target="tpu_custom_call", output_to_operand_aliasing={{}: (15, {})} | custom-call | flops 805306368 | bytes 6291456 | tf_op jit(solution)/shard_map/cross/pallas_call | solution.py:187
  (50 shorter events, 10.2 us)
Async XLA Ops:
  0.0 0.9 %copy-start = (bf16[256,512]{1,0:T(8,128)(2,1)S(1)}, bf16[256,512]{1,0:T(8,128)(2,1)}, u32[]{:S(2)}) copy-start(bf16[256,512]{1,0:T(8,128)(2,1)} %constant.17.clone.basis_ref) | copy-start | bytes 786436
  1.0 0.7 copy-start.1
  7.9 2.8 %collective-permute-start = (bf16[8,2,8,16,256]{4,3,2,1,0:T(8,128)(2,1)S(1)}, bf16[8,2,8,16,256]{4,3,2,1,0:T(8,128)(2,1)S(1)}, u32[]{:S(2)}, u32[]{:S(2)}) collective-permute-start(bf16[8,2,8,16,256]{4,3,2,1,0:T(8,128)(2,1)S(1)} %get-tuple-element.35), channel_id=1, source_target_pairs={{0,1},{1,0},{2,3},{3,2},{4,5},{5,4},{6,7},{7,6},{8,9},{9,8},{10,11... | collective-permute-start | bytes 3145736 | tf_op jit(solution)/shard_map/ppermute | solution.py:233
  10.8 12.2 %collective-permute-start.3 = (bf16[2,2,5,16,256]{4,3,2,1,0:T(8,128)(2,1)S(1)}, bf16[2,2,5,16,256]{4,3,2,1,0:T(8,128)(2,1)S(1)}, u32[]{:S(2)}, u32[]{:S(2)}) collective-permute-start(bf16[2,2,5,16,256]{4,3,2,1,0:T(8,128)(2,1)S(1)} %fusion.2), channel_id=1, source_target_pairs={{0,8},{1,9},{2,10},{3,11},{4,12},{5,13},{6,14},{7,15},{8,0},{9,1},... | collective-permute-start | bytes 491528 | tf_op jit(solution)/shard_map/ppermute | solution.py:217
  14.9 9.7 %collective-permute-start.1 = (bf16[2,2,8,16,256]{4,3,2,1,0:T(8,128)(2,1)S(1)}, bf16[2,2,8,16,256]{4,3,2,1,0:T(8,128)(2,1)S(1)}, u32[]{:S(2)}, u32[]{:S(2)}) collective-permute-start(bf16[2,2,8,16,256]{4,3,2,1,0:T(8,128)(2,1)S(1)} %pad_maximum_fusion), channel_id=1, source_target_pairs={{0,2},{1,3},{2,0},{3,1},{4,6},{5,7},{6,4},{7,5},{8,10},{9,11},{10,... | collective-permute-start | bytes 786440 | tf_op jit(solution)/shard_map/ppermute | solution.py:217
  16.4 13.1 %collective-permute-start.2 = (bf16[2,2,8,16,256]{4,3,2,1,0:T(8,128)(2,1)S(1)}, bf16[2,2,8,16,256]{4,3,2,1,0:T(8,128)(2,1)S(1)}, u32[]{:S(2)}, u32[]{:S(2)}) collective-permute-start(bf16[2,2,8,16,256]{4,3,2,1,0:T(8,128)(2,1)S(1)} %pad_maximum_fusion.2), channel_id=1, source_target_pairs={{0,4},{1,5},{2,6},{3,7},{4,0},{5,1},{6,2},{7,3},{8,12},{9,13},{10,... | collective-permute-start | bytes 786440 | tf_op jit(solution)/shard_map/ppermute | solution.py:217
  18.1 11.5 %collective-permute-start.10 = (bf16[2,2,8,16,256]{4,3,2,1,0:T(8,128)(2,1)S(1)}, bf16[2,2,8,16,256]{4,3,2,1,0:T(8,128)(2,1)S(1)}, u32[]{:S(2)}, u32[]{:S(2)}) collective-permute-start(bf16[2,2,8,16,256]{4,3,2,1,0:T(8,128)(2,1)S(1)} %pad_maximum_fusion.1.rest_0_), channel_id=1, source_target_pairs={{0,16},{16,0},{1,17},{17,1},{2,18},{18,2},{3,19},{19,3},{4,20},{20... | collective-permute-start | bytes 786440 | tf_op jit(solution)/shard_map/ppermute | solution.py:217
  23.0 12.3 %collective-permute-start.4 = (bf16[2,2,8,16,256]{4,3,2,1,0:T(8,128)(2,1)S(1)}, bf16[2,2,8,16,256]{4,3,2,1,0:T(8,128)(2,1)S(1)}, u32[]{:S(2)}, u32[]{:S(2)}) collective-permute-start(bf16[2,2,8,16,256]{4,3,2,1,0:T(8,128)(2,1)S(1)} %pad_maximum_fusion.3), channel_id=1, source_target_pairs={{0,6},{1,7},{2,4},{3,5},{4,2},{5,3},{6,0},{7,1},{8,14},{9,15},{10,... | collective-permute-start | bytes 786440 | tf_op jit(solution)/shard_map/ppermute | solution.py:217
  24.5 10.7 %collective-permute-start.5 = (bf16[2,2,8,16,256]{4,3,2,1,0:T(8,128)(2,1)S(1)}, bf16[2,2,8,16,256]{4,3,2,1,0:T(8,128)(2,1)S(1)}, u32[]{:S(2)}, u32[]{:S(2)}) collective-permute-start(bf16[2,2,8,16,256]{4,3,2,1,0:T(8,128)(2,1)S(1)} %collective-permute-done.1.rest_1_), channel_id=1, source_target_pairs={{0,16},{16,0},{1,17},{17,1},{2,18},{18,2},{3,19},{19,3},{4,20},{20... | collective-permute-start | bytes 786440 | tf_op jit(solution)/shard_map/ppermute | solution.py:217
  26.1 16.0 %collective-permute-start.9 = (bf16[2,2,5,16,256]{4,3,2,1,0:T(8,128)(2,1)S(1)}, bf16[2,2,5,16,256]{4,3,2,1,0:T(8,128)(2,1)S(1)}, u32[]{:S(2)}, u32[]{:S(2)}) collective-permute-start(bf16[2,2,5,16,256]{4,3,2,1,0:T(8,128)(2,1)S(1)} %get-tuple-element.48), channel_id=1, source_target_pairs={{0,10},{1,11},{2,8},{3,9},{4,14},{5,15},{6,12},{7,13},{8,2},{9,3},... | collective-permute-start | bytes 491528 | tf_op jit(solution)/shard_map/ppermute | solution.py:217
  29.6 12.5 %collective-permute-start.11 = (bf16[2,2,8,16,256]{4,3,2,1,0:T(8,128)(2,1)S(1)}, bf16[2,2,8,16,256]{4,3,2,1,0:T(8,128)(2,1)S(1)}, u32[]{:S(2)}, u32[]{:S(2)}) collective-permute-start(bf16[2,2,8,16,256]{4,3,2,1,0:T(8,128)(2,1)S(1)} %collective-permute-done.2.rest_2_), channel_id=1, source_target_pairs={{0,16},{16,0},{1,17},{17,1},{2,18},{18,2},{3,19},{19,3},{4,20},{20... | collective-permute-start | bytes 786440 | tf_op jit(solution)/shard_map/ppermute | solution.py:217
  30.1 15.6 %collective-permute-start.7 = (bf16[2,2,5,16,256]{4,3,2,1,0:T(8,128)(2,1)S(1)}, bf16[2,2,5,16,256]{4,3,2,1,0:T(8,128)(2,1)S(1)}, u32[]{:S(2)}, u32[]{:S(2)}) collective-permute-start(bf16[2,2,5,16,256]{4,3,2,1,0:T(8,128)(2,1)S(1)} %get-tuple-element.45), channel_id=1, source_target_pairs={{0,12},{1,13},{2,14},{3,15},{4,8},{5,9},{6,10},{7,11},{8,4},{9,5},... | collective-permute-start | bytes 491528 | tf_op jit(solution)/shard_map/ppermute | solution.py:217
  35.2 10.5 %collective-permute-start.6 = (bf16[2,2,8,16,256]{4,3,2,1,0:T(8,128)(2,1)S(1)}, bf16[2,2,8,16,256]{4,3,2,1,0:T(8,128)(2,1)S(1)}, u32[]{:S(2)}, u32[]{:S(2)}) collective-permute-start(bf16[2,2,8,16,256]{4,3,2,1,0:T(8,128)(2,1)S(1)} %collective-permute-done.4.rest_3_), channel_id=1, source_target_pairs={{0,16},{16,0},{1,17},{17,1},{2,18},{18,2},{3,19},{19,3},{4,20},{20... | collective-permute-start | bytes 786440 | tf_op jit(solution)/shard_map/ppermute | solution.py:217
  42.1 10.4 %collective-permute-start.12 = (bf16[4,2,5,16,256]{4,3,2,1,0:T(8,128)(2,1)S(1)}, bf16[4,2,5,16,256]{4,3,2,1,0:T(8,128)(2,1)S(1)}, u32[]{:S(2)}, u32[]{:S(2)}) collective-permute-start(bf16[4,2,5,16,256]{4,3,2,1,0:T(8,128)(2,1)S(1)} %constant_dynamic-update-slice_fusion.rest_4_), channel_id=1, source_target_pairs={{0,16},{16,0},{1,17},{17,1},{2,18},{18,2},{3,19},{19,3},{4,20},{20... | collective-permute-start | bytes 983048 | tf_op jit(solution)/shard_map/ppermute | solution.py:217
  42.2 8.2 %collective-permute-start.13 = (bf16[2,2,5,16,256]{4,3,2,1,0:T(8,128)(2,1)S(1)}, bf16[2,2,5,16,256]{4,3,2,1,0:T(8,128)(2,1)S(1)}, u32[]{:S(2)}, u32[]{:S(2)}) collective-permute-start(bf16[2,2,5,16,256]{4,3,2,1,0:T(8,128)(2,1)S(1)} %fusion), channel_id=1, source_target_pairs={{0,14},{1,15},{2,12},{3,13},{4,10},{5,11},{6,8},{7,9},{8,6},{9,7},... | collective-permute-start | bytes 491528 | tf_op jit(solution)/shard_map/ppermute | solution.py:217
  45.7 11.6 %collective-permute-start.8 = (bf16[2,2,3,16,256]{4,3,2,1,0:T(8,128)(2,1)S(1)}, bf16[2,2,3,16,256]{4,3,2,1,0:T(8,128)(2,1)S(1)}, u32[]{:S(2)}, u32[]{:S(2)}) collective-permute-start(bf16[2,2,3,16,256]{4,3,2,1,0:T(8,128)(2,1)S(1)} %pad_maximum_fusion.8), channel_id=1, source_target_pairs={{0,8},{1,9},{2,10},{3,11},{4,12},{5,13},{6,14},{7,15},{8,0},{9,1},... | collective-permute-start | bytes 294920 | tf_op jit(solution)/shard_map/ppermute | solution.py:217
  48.4 11.8 %collective-permute-start.15 = (bf16[2,2,5,16,256]{4,3,2,1,0:T(8,128)(2,1)S(1)}, bf16[2,2,5,16,256]{4,3,2,1,0:T(8,128)(2,1)S(1)}, u32[]{:S(2)}, u32[]{:S(2)}) collective-permute-start(bf16[2,2,5,16,256]{4,3,2,1,0:T(8,128)(2,1)S(1)} %collective-permute-done.7.rest_5_), channel_id=1, source_target_pairs={{0,16},{16,0},{1,17},{17,1},{2,18},{18,2},{3,19},{19,3},{4,20},{20... | collective-permute-start | bytes 491528 | tf_op jit(solution)/shard_map/ppermute | solution.py:217
  52.5 7.7 %collective-permute-start.14 = (bf16[2,2,3,16,256]{4,3,2,1,0:T(8,128)(2,1)S(1)}, bf16[2,2,3,16,256]{4,3,2,1,0:T(8,128)(2,1)S(1)}, u32[]{:S(2)}, u32[]{:S(2)}) collective-permute-start(bf16[2,2,3,16,256]{4,3,2,1,0:T(8,128)(2,1)S(1)} %pad_maximum_fusion.7), channel_id=1, source_target_pairs={{0,10},{1,11},{2,8},{3,9},{4,14},{5,15},{6,12},{7,13},{8,2},{9,3},... | collective-permute-start | bytes 294920 | tf_op jit(solution)/shard_map/ppermute | solution.py:217
  56.6 8.1 %collective-permute-start.17 = (bf16[2,2,5,16,256]{4,3,2,1,0:T(8,128)(2,1)S(1)}, bf16[2,2,5,16,256]{4,3,2,1,0:T(8,128)(2,1)S(1)}, u32[]{:S(2)}, u32[]{:S(2)}) collective-permute-start(bf16[2,2,5,16,256]{4,3,2,1,0:T(8,128)(2,1)S(1)} %collective-permute-done.13.rest_6_), channel_id=1, source_target_pairs={{0,16},{16,0},{1,17},{17,1},{2,18},{18,2},{3,19},{19,3},{4,20},{20... | collective-permute-start | bytes 491528 | tf_op jit(solution)/shard_map/ppermute | solution.py:217
  60.3 13.1 %collective-permute-start.19 = (bf16[4,2,3,16,256]{4,3,2,1,0:T(8,128)(2,1)S(1)}, bf16[4,2,3,16,256]{4,3,2,1,0:T(8,128)(2,1)S(1)}, u32[]{:S(2)}, u32[]{:S(2)}) collective-permute-start(bf16[4,2,3,16,256]{4,3,2,1,0:T(8,128)(2,1)S(1)} %constant_dynamic-update-slice_fusion.2.rest_4_), channel_id=1, source_target_pairs={{0,16},{16,0},{1,17},{17,1},{2,18},{18,2},{3,19},{19,3},{4,20},{20... | collective-permute-start | bytes 589832 | tf_op jit(solution)/shard_map/ppermute | solution.py:217
  61.2 11.0 %collective-permute-start.16 = (bf16[2,2,3,16,256]{4,3,2,1,0:T(8,128)(2,1)S(1)}, bf16[2,2,3,16,256]{4,3,2,1,0:T(8,128)(2,1)S(1)}, u32[]{:S(2)}, u32[]{:S(2)}) collective-permute-start(bf16[2,2,3,16,256]{4,3,2,1,0:T(8,128)(2,1)S(1)} %pad_maximum_fusion.6), channel_id=1, source_target_pairs={{0,12},{1,13},{2,14},{3,15},{4,8},{5,9},{6,10},{7,11},{8,4},{9,5},... | collective-permute-start | bytes 294920 | tf_op jit(solution)/shard_map/ppermute | solution.py:217
  62.9 10.4 %collective-permute-start.18 = (bf16[2,2,3,16,256]{4,3,2,1,0:T(8,128)(2,1)S(1)}, bf16[2,2,3,16,256]{4,3,2,1,0:T(8,128)(2,1)S(1)}, u32[]{:S(2)}, u32[]{:S(2)}) collective-permute-start(bf16[2,2,3,16,256]{4,3,2,1,0:T(8,128)(2,1)S(1)} %pad_maximum_fusion.5), channel_id=1, source_target_pairs={{0,14},{1,15},{2,12},{3,13},{4,10},{5,11},{6,8},{7,9},{8,6},{9,7},... | collective-permute-start | bytes 294920 | tf_op jit(solution)/shard_map/ppermute | solution.py:217
  72.1 4.7 %collective-permute-start.20 = (bf16[2,2,3,16,256]{4,3,2,1,0:T(8,128)(2,1)S(1)}, bf16[2,2,3,16,256]{4,3,2,1,0:T(8,128)(2,1)S(1)}, u32[]{:S(2)}, u32[]{:S(2)}) collective-permute-start(bf16[2,2,3,16,256]{4,3,2,1,0:T(8,128)(2,1)S(1)} %collective-permute-done.16.rest_5_), channel_id=1, source_target_pairs={{0,16},{16,0},{1,17},{17,1},{2,18},{18,2},{3,19},{19,3},{4,20},{20... | collective-permute-start | bytes 294920 | tf_op jit(solution)/shard_map/ppermute | solution.py:217
  73.4 4.6 %collective-permute-start.21 = (bf16[2,2,3,16,256]{4,3,2,1,0:T(8,128)(2,1)S(1)}, bf16[2,2,3,16,256]{4,3,2,1,0:T(8,128)(2,1)S(1)}, u32[]{:S(2)}, u32[]{:S(2)}) collective-permute-start(bf16[2,2,3,16,256]{4,3,2,1,0:T(8,128)(2,1)S(1)} %collective-permute-done.18.rest_6_), channel_id=1, source_target_pairs={{0,16},{16,0},{1,17},{17,1},{2,18},{18,2},{3,19},{19,3},{4,20},{20... | collective-permute-start | bytes 294920 | tf_op jit(solution)/shard_map/ppermute | solution.py:217

commit v4 on v3

--- a/solution.py
+++ b/solution.py
@@ -224,6 +224,7 @@
     chips = parts // PLANES // 2
     bins_local = F // parts
     middle = (5 * bins_local + 4) // 8
+    halfway = max(1, middle // 2)
     group = lax.axis_index("grp")
     rounds = plan.shape[1]
     offset = lax.dynamic_index_in_dim(plan, group, 0, keepdims=False) ^ group
@@ -231,7 +232,7 @@
 
     *mine, for_sibling = head(waveform, valid_count, lax.axis_index("seg"), parts)
     theirs = lax.ppermute(for_sibling, "seg", [(s, s ^ 1) for s in range(parts)])
-    seg_lane, far_lane, grp_lane = Lane(parts), Lane(2), Lane(2 * (groups - 1))
+    seg_lane, far_lane, late_lane, grp_lane = Lane(parts), Lane(2), Lane(parts), Lane(3 * (groups - 1))
     sides = [[] for _ in range(groups)]
 
     def both(n, low=0, high=bins_local):
@@ -254,25 +255,24 @@
     own_done = forward(own_blocks)
     waits = {(0, n): own_blocks for n in far[1:]}
     first = [scatter(far_lane, n, 0, middle, waits.get((0, n), ())) for n in far]
-    beside_blocks = [scatter(seg_lane, n, after=first[:1] if n > beside[0] else ()) for n in beside]
+    beside_blocks = [scatter(seg_lane, n, after=own_blocks if n > beside[0] else ()) for n in beside]
     beside_done = [forward([block]) for block in beside_blocks]
     far_done = forward(first)
     first = [scatter(far_lane, n, 0, middle, beside_done[:1] if n == farthest[-1] else ()) for n in farthest]
     last_done = [forward([block]) for block in first]
-    second = [scatter(far_lane, far[0], middle, bins_local, beside_done[-1:])]
-    second += [scatter(far_lane, n, middle, bins_local, [far_done]) for n in far[1:]]
-    forward(second)
+    second = [scatter(late_lane, far[0], middle, bins_local, [first[0], beside_done[-1]])]
+    second += [scatter(late_lane, n, middle, bins_local, [first[-1], far_done]) for n in far[1:]]
+    second += [scatter(late_lane, n, middle, bins_local, [first[-1], far_done]) for n in farthest]
     split = 1 + chips
-    whole = len(sides[0]) - 1 - split
-    out = add_bins(
-        None, select, [side[: whole + split] for side in sides], [0] * (whole + split), 0, middle, bins_local, rounds
-    )
-    second = [scatter(far_lane, n, middle, bins_local, last_done[:1]) for n in farthest]
-    second[0], out = lax.optimization_barrier((second[0], out))
-    for block in second:
-        forward([block])
-    chosen = [side[:whole] + side[-split:] for side in sides]
-    out = add_bins(out, select, chosen, [0] * whole + [middle] * split, middle, bins_local, bins_local, rounds)
+    whole = len(sides[0]) - split
+    early = [side[: whole + split] for side in sides]
+    out = add_bins(None, select, early, [0] * (whole + split), 0, halfway, bins_local, rounds)
+    second, out = lax.optimization_barrier((second, out))
+    forward(second[:chips])
+    forward(second[chips:])
+    out = add_bins(out, select, early, [0] * (whole + split), halfway, middle, bins_local, rounds)
+    chosen = [side[:whole] + side[-2:] for side in sides]
+    out = add_bins(out, select, chosen, [0] * whole + [middle] * 2, middle, bins_local, bins_local, rounds)
     rows = waveform.shape[0]
     out = out.reshape(bins_local, 2, rows, rows // LANES, rounds, LANES).transpose(0, 1, 2, 4, 3, 5)
     return out.reshape(bins_local, 2, rows, rounds, rows)

time: 83.1 us -> 85.2 us (1.025)
  waiting for transfers between devices: 22.9 us -> 26.8 us
  starting transfers between devices: 38.1 us -> 35.2 us
  Pallas kernels: 18.5 us -> 19.5 us
    ppermute x21 -> x20, waiting for transfers between devices: 21.5 us -> 25.8 us  [send(): self.sent.append(lax.ppermute(block, axis, pairs))]
    ppermute x21 -> x20, starting transfers between devices: 37.5 us -> 34.7 us  [send(): self.sent.append(lax.ppermute(block, axis, pairs))]
    pallas_call x2 -> x3, Pallas kernels: 12.3 us -> 13.3 us  [add_bins(): pl.pallas_call(functools.partial(cross_kernel, groups=groups, held=held,...]
  transfers between devices with their start and end apart: 22 -> 21, of which waited for: 10 -> 9; matrix products, arithmetic and copies ran while one was open for 2% -> 2% of each run, Pallas kernels for 9% -> 10%
where the time goes in v4:
time: 85.2 us; the launch traced here: 85 us
  starting transfers between devices  35.2 us (41%)
  waiting for transfers between devices  26.8 us (31%)
  Pallas kernels  19.5 us (23%)
  local copies, waits for them, and re-layouts  2.01 us (2%)
  other arithmetic  1.23 us (1%)
    ppermute x20, starting transfers between devices, send(): self.sent.append(lax.ppermute(block, axis, pairs))  34.7 us
    ppermute x20, waiting for transfers between devices, send(): self.sent.append(lax.ppermute(block, axis, pairs))  25.8 us
    pallas_call x3, Pallas kernels, add_bins(): pl.pallas_call(functools.partial(cross_kernel, groups=groups, held=held,...  13.3 us
    pallas_call x1, Pallas kernels, head(): pl.pallas_call(functools.partial(head_kernel, parts=parts), out_shape=[ja...  6.18 us
  transfers between devices with their start and end apart: 21, of which 9 were waited for; matrix products, arithmetic and copies ran while one was open for 2% of the time, Pallas kernels for 10%

profile of v4, /device:TPU:0, one launch (start us, length us, event | category | flops | bytes accessed | tf_op | source)
XLA Modules:
  0.0 85.0 jit_solution(8883453444870910389)
XLA Ops:
  1.7 6.2 %spectra.1 = (bf16[1,2,8,16,256]{4,3,2,1,0:T(8,128)(2,1)S(1)}, bf16[1,2,8,16,256]{4,3,2,1,0:T(8,128)(2,1)S(1)}, bf16[1,2,8,16,256]{4,3,2,1,0:T(8,128)(2,1)S(1)},...) custom-call(s32[1]{0:T(128)} %bitcast.me_ref, ...), custom_call_target="tpu_custom_call" | custom-call | tf_op jit(solution)/shard_map/spectra/pallas_call | solution.py:91
  10.8 2.9 %collective-permute-start.1 = (bf16[2,2,8,16,256]{4,3,2,1,0:T(8,128)(2,1)S(1)}, bf16[2,2,8,16,256]{4,3,2,1,0:T(8,128)(2,1)S(1)}, u32[]{:S(2)}, u32[]{:S(2)}) collective-permute-start(bf16[2,2,8,16,256]{4,3,2,1,0:T(8,128)(2,1)S(1)} %pad_maximum_fusion), channel_id=1, source_target_pairs={{0,2},{1,3},{2,0},{3,1},{4,6},{5,7},{6,4},{7,5},{8,10},{9,11},{10,... | collective-permute-start | bytes 786440 | tf_op jit(solution)/shard_map/ppermute | solution.py:217
  13.8 1.6 %collective-permute-start.2 = (bf16[2,2,8,16,256]{4,3,2,1,0:T(8,128)(2,1)S(1)}, bf16[2,2,8,16,256]{4,3,2,1,0:T(8,128)(2,1)S(1)}, u32[]{:S(2)}, u32[]{:S(2)}) collective-permute-start(bf16[2,2,8,16,256]{4,3,2,1,0:T(8,128)(2,1)S(1)} %pad_maximum_fusion.2), channel_id=1, source_target_pairs={{0,4},{1,5},{2,6},{3,7},{4,0},{5,1},{6,2},{7,3},{8,12},{9,13},{10,... | collective-permute-start | bytes 786440 | tf_op jit(solution)/shard_map/ppermute | solution.py:217
  15.4 1.6 %collective-permute-start.6 = (bf16[2,2,8,16,256]{4,3,2,1,0:T(8,128)(2,1)S(1)}, bf16[2,2,8,16,256]{4,3,2,1,0:T(8,128)(2,1)S(1)}, u32[]{:S(2)}, u32[]{:S(2)}) collective-permute-start(bf16[2,2,8,16,256]{4,3,2,1,0:T(8,128)(2,1)S(1)} %pad_maximum_fusion.1.rest_0_), channel_id=1, source_target_pairs={{0,16},{16,0},{1,17},{17,1},{2,18},{18,2},{3,19},{19,3},{4,20},{20... | collective-permute-start | bytes 786440 | tf_op jit(solution)/shard_map/ppermute | solution.py:217
  17.0 2.7 %collective-permute-start.4 = (bf16[2,2,5,16,256]{4,3,2,1,0:T(8,128)(2,1)S(1)}, bf16[2,2,5,16,256]{4,3,2,1,0:T(8,128)(2,1)S(1)}, u32[]{:S(2)}, u32[]{:S(2)}) collective-permute-start(bf16[2,2,5,16,256]{4,3,2,1,0:T(8,128)(2,1)S(1)} %pad_maximum_fusion.5), channel_id=1, source_target_pairs={{0,8},{1,9},{2,10},{3,11},{4,12},{5,13},{6,14},{7,15},{8,0},{9,1},... | collective-permute-start | bytes 491528 | tf_op jit(solution)/shard_map/ppermute | solution.py:217
  20.3 2.7 %collective-permute-start.3 = (bf16[2,2,8,16,256]{4,3,2,1,0:T(8,128)(2,1)S(1)}, bf16[2,2,8,16,256]{4,3,2,1,0:T(8,128)(2,1)S(1)}, u32[]{:S(2)}, u32[]{:S(2)}) collective-permute-start(bf16[2,2,8,16,256]{4,3,2,1,0:T(8,128)(2,1)S(1)} %pad_maximum_fusion.3), channel_id=1, source_target_pairs={{0,6},{1,7},{2,4},{3,5},{4,2},{5,3},{6,0},{7,1},{8,14},{9,15},{10,... | collective-permute-start | bytes 786440 | tf_op jit(solution)/shard_map/ppermute | solution.py:217
  23.1 3.4 %collective-permute-done.2.rest_2_ = bf16[2,2,8,16,256]{4,3,2,1,0:T(8,128)(2,1)S(1)} collective-permute-done((bf16[2,2,8,16,256]{4,3,2,1,0:T(8,128)(2,1)S(1)}, bf16[2,2,8,16,256]{4,3,2,1,0:T(8,128)(2,1)S(1)}, u32[]{:S(2)}, u32[]{:S(2)}) %collective-permute-start.2) | collective-permute-done | bytes 262176 | tf_op jit(solution)/shard_map/ppermute | solution.py:217
  28.7 1.7 %collective-permute-start.10 = (bf16[2,2,5,16,256]{4,3,2,1,0:T(8,128)(2,1)S(1)}, bf16[2,2,5,16,256]{4,3,2,1,0:T(8,128)(2,1)S(1)}, u32[]{:S(2)}, u32[]{:S(2)}) collective-permute-start(bf16[2,2,5,16,256]{4,3,2,1,0:T(8,128)(2,1)S(1)} %get-tuple-element.50), channel_id=1, source_target_pairs={{0,10},{1,11},{2,8},{3,9},{4,14},{5,15},{6,12},{7,13},{8,2},{9,3},... | collective-permute-start | bytes 491528 | tf_op jit(solution)/shard_map/ppermute | solution.py:217
  30.4 2.0 %collective-permute-start.5 = (bf16[2,2,5,16,256]{4,3,2,1,0:T(8,128)(2,1)S(1)}, bf16[2,2,5,16,256]{4,3,2,1,0:T(8,128)(2,1)S(1)}, u32[]{:S(2)}, u32[]{:S(2)}) collective-permute-start(bf16[2,2,5,16,256]{4,3,2,1,0:T(8,128)(2,1)S(1)} %get-tuple-element.45), channel_id=1, source_target_pairs={{0,12},{1,13},{2,14},{3,15},{4,8},{5,9},{6,10},{7,11},{8,4},{9,5},... | collective-permute-start | bytes 491528 | tf_op jit(solution)/shard_map/ppermute | solution.py:217
  32.6 1.7 %collective-permute-start.7 = (bf16[2,2,8,16,256]{4,3,2,1,0:T(8,128)(2,1)S(1)}, bf16[2,2,8,16,256]{4,3,2,1,0:T(8,128)(2,1)S(1)}, u32[]{:S(2)}, u32[]{:S(2)}) collective-permute-start(bf16[2,2,8,16,256]{4,3,2,1,0:T(8,128)(2,1)S(1)} %collective-permute-done.3.rest_3_), channel_id=1, source_target_pairs={{0,16},{16,0},{1,17},{17,1},{2,18},{18,2},{3,19},{19,3},{4,20},{20... | collective-permute-start | bytes 786440 | tf_op jit(solution)/shard_map/ppermute | solution.py:217
  34.3 9.3 %collective-permute-done.10 = bf16[2,2,5,16,256]{4,3,2,1,0:T(8,128)(2,1)S(1)} collective-permute-done((bf16[2,2,5,16,256]{4,3,2,1,0:T(8,128)(2,1)S(1)}, bf16[2,2,5,16,256]{4,3,2,1,0:T(8,128)(2,1)S(1)}, u32[]{:S(2)}, u32[]{:S(2)}) %collective-permute-start.10) | collective-permute-done | bytes 163872 | tf_op jit(solution)/shard_map/ppermute | solution.py:217
  43.5 2.5 %collective-permute-start.11 = (bf16[2,2,5,16,256]{4,3,2,1,0:T(8,128)(2,1)S(1)}, bf16[2,2,5,16,256]{4,3,2,1,0:T(8,128)(2,1)S(1)}, u32[]{:S(2)}, u32[]{:S(2)}) collective-permute-start(bf16[2,2,5,16,256]{4,3,2,1,0:T(8,128)(2,1)S(1)} %fusion), channel_id=1, source_target_pairs={{0,14},{1,15},{2,12},{3,13},{4,10},{5,11},{6,8},{7,9},{8,6},{9,7},... | collective-permute-start | bytes 491528 | tf_op jit(solution)/shard_map/ppermute | solution.py:217
  46.1 1.5 %collective-permute-start.13 = (bf16[4,2,5,16,256]{4,3,2,1,0:T(8,128)(2,1)S(1)}, bf16[4,2,5,16,256]{4,3,2,1,0:T(8,128)(2,1)S(1)}, u32[]{:S(2)}, u32[]{:S(2)}) collective-permute-start(bf16[4,2,5,16,256]{4,3,2,1,0:T(8,128)(2,1)S(1)} %constant_dynamic-update-slice_fusion.rest_4_), channel_id=1, source_target_pairs={{0,16},{16,0},{1,17},{17,1},{2,18},{18,2},{3,19},{19,3},{4,20},{20... | collective-permute-start | bytes 983048 | tf_op jit(solution)/shard_map/ppermute | solution.py:217
  48.2 3.4 %collective-permute-done.11.rest_6_ = bf16[2,2,5,16,256]{4,3,2,1,0:T(8,128)(2,1)S(1)} collective-permute-done((bf16[2,2,5,16,256]{4,3,2,1,0:T(8,128)(2,1)S(1)}, bf16[2,2,5,16,256]{4,3,2,1,0:T(8,128)(2,1)S(1)}, u32[]{:S(2)}, u32[]{:S(2)}) %collective-permute-start.11) | collective-permute-done | bytes 163872 | tf_op jit(solution)/shard_map/ppermute | solution.py:217
  53.2 2.6 %collective-permute-start.8 = (bf16[2,2,3,16,256]{4,3,2,1,0:T(8,128)(2,1)S(1)}, bf16[2,2,3,16,256]{4,3,2,1,0:T(8,128)(2,1)S(1)}, u32[]{:S(2)}, u32[]{:S(2)}) collective-permute-start(bf16[2,2,3,16,256]{4,3,2,1,0:T(8,128)(2,1)S(1)} %pad_maximum_fusion.9), channel_id=1, source_target_pairs={{0,8},{1,9},{2,10},{3,11},{4,12},{5,13},{6,14},{7,15},{8,0},{9,1},... | collective-permute-start | bytes 294920 | tf_op jit(solution)/shard_map/ppermute | solution.py:217
  55.8 1.9 %collective-permute-start.16 = (bf16[2,2,3,16,256]{4,3,2,1,0:T(8,128)(2,1)S(1)}, bf16[2,2,3,16,256]{4,3,2,1,0:T(8,128)(2,1)S(1)}, u32[]{:S(2)}, u32[]{:S(2)}) collective-permute-start(bf16[2,2,3,16,256]{4,3,2,1,0:T(8,128)(2,1)S(1)} %get-tuple-element.55), channel_id=1, source_target_pairs={{0,14},{1,15},{2,12},{3,13},{4,10},{5,11},{6,8},{7,9},{8,6},{9,7},... | collective-permute-start | bytes 294920 | tf_op jit(solution)/shard_map/ppermute | solution.py:217
  57.7 2.8 %collective-permute-start.15 = (bf16[2,2,3,16,256]{4,3,2,1,0:T(8,128)(2,1)S(1)}, bf16[2,2,3,16,256]{4,3,2,1,0:T(8,128)(2,1)S(1)}, u32[]{:S(2)}, u32[]{:S(2)}) collective-permute-start(bf16[2,2,3,16,256]{4,3,2,1,0:T(8,128)(2,1)S(1)} %get-tuple-element.54), channel_id=1, source_target_pairs={{0,12},{1,13},{2,14},{3,15},{4,8},{5,9},{6,10},{7,11},{8,4},{9,5},... | collective-permute-start | bytes 294920 | tf_op jit(solution)/shard_map/ppermute | solution.py:217
  60.6 3.6 %cross.3.rest_14_ = bf16[8,2,4096,128]{3,2,1,0:T(8,128)(2,1)} custom-call(bf16[1024,256]{1,0:T(8,128)(2,1)S(1)} %and_convert_fusion.select_ref, bf16[2,2,8,16,256]{4,3,2,1,0:T(8,128)(2,1)S(1)} %pad_maximum_fusion.1.rest_0_, bf16[2,2,8,16,256]{4,3,2,1,0:T(8,128)(2,1)S(1)} %collective-permute-done.1.rest_1_, ...), custom_call_target="tpu_custom_call" | custom-call | flops 536870912 | bytes 4194304 | tf_op jit(solution)/shard_map/cross/pallas_call | solution.py:187
  64.2 2.0 %collective-permute-done.8 = bf16[2,2,3,16,256]{4,3,2,1,0:T(8,128)(2,1)S(1)} collective-permute-done((bf16[2,2,3,16,256]{4,3,2,1,0:T(8,128)(2,1)S(1)}, bf16[2,2,3,16,256]{4,3,2,1,0:T(8,128)(2,1)S(1)}, u32[]{:S(2)}, u32[]{:S(2)}) %collective-permute-start.8) | collective-permute-done | bytes 98336 | tf_op jit(solution)/shard_map/ppermute | solution.py:217
  66.2 5.1 %collective-permute-done.14 = bf16[2,2,3,16,256]{4,3,2,1,0:T(8,128)(2,1)S(1)} collective-permute-done((bf16[2,2,3,16,256]{4,3,2,1,0:T(8,128)(2,1)S(1)}, bf16[2,2,3,16,256]{4,3,2,1,0:T(8,128)(2,1)S(1)}, u32[]{:S(2)}, u32[]{:S(2)}) %collective-permute-start.14) | collective-permute-done | bytes 98336 | tf_op jit(solution)/shard_map/ppermute | solution.py:217
  71.8 1.7 %collective-permute-start.19 = (bf16[4,2,3,16,256]{4,3,2,1,0:T(8,128)(2,1)S(1)}, bf16[4,2,3,16,256]{4,3,2,1,0:T(8,128)(2,1)S(1)}, u32[]{:S(2)}, u32[]{:S(2)}) collective-permute-start(bf16[4,2,3,16,256]{4,3,2,1,0:T(8,128)(2,1)S(1)} %constant_dynamic-update-slice_fusion.2.rest_4_), channel_id=1, source_target_pairs={{0,16},{16,0},{1,17},{17,1},{2,18},{18,2},{3,19},{19,3},{4,20},{20... | collective-permute-start | bytes 589832 | tf_op jit(solution)/shard_map/ppermute | solution.py:217
  73.5 4.8 %cross.4.rest_12_ = bf16[8,2,4096,128]{3,2,1,0:T(8,128)(2,1)} custom-call(bf16[1024,256]{1,0:T(8,128)(2,1)S(1)} %and_convert_fusion.select_ref, bf16[2,2,8,16,256]{4,3,2,1,0:T(8,128)(2,1)S(1)} %pad_maximum_fusion.1.rest_0_, bf16[2,2,8,16,256]{4,3,2,1,0:T(8,128)(2,1)S(1)} %collective-permute-done.1.rest_1_, ...), custom_call_target="tpu_custom_call", output_to_operand_aliasing={{}: (15, {})} | custom-call | flops 805306368 | bytes 6291456 | tf_op jit(solution)/shard_map/cross/pallas_call | solution.py:187
  78.3 1.8 %collective-permute-done.19.rest_10_ = bf16[4,2,3,16,256]{4,3,2,1,0:T(8,128)(2,1)S(1)} collective-permute-done((bf16[4,2,3,16,256]{4,3,2,1,0:T(8,128)(2,1)S(1)}, bf16[4,2,3,16,256]{4,3,2,1,0:T(8,128)(2,1)S(1)}, u32[]{:S(2)}, u32[]{:S(2)}) %collective-permute-start.19) | collective-permute-done | bytes 196640 | tf_op jit(solution)/shard_map/ppermute | solution.py:217
  80.1 4.9 %cross.5 = bf16[8,2,4096,128]{3,2,1,0:T(8,128)(2,1)} custom-call(bf16[1024,256]{1,0:T(8,128)(2,1)S(1)} %and_convert_fusion.select_ref, bf16[2,2,8,16,256]{4,3,2,1,0:T(8,128)(2,1)S(1)} %pad_maximum_fusion.1.rest_0_, bf16[2,2,8,16,256]{4,3,2,1,0:T(8,128)(2,1)S(1)} %collective-permute-done.1.rest_1_, ...), custom_call_target="tpu_custom_call", output_to_operand_aliasing={{}: (13, {})} | custom-call | flops 805306368 | bytes 6291456 | tf_op jit(solution)/shard_map/cross/pallas_call | solution.py:187
  (50 shorter events, 10.4 us)
Async XLA Ops:
  0.0 0.9 %copy-start = (bf16[256,512]{1,0:T(8,128)(2,1)S(1)}, bf16[256,512]{1,0:T(8,128)(2,1)}, u32[]{:S(2)}) copy-start(bf16[256,512]{1,0:T(8,128)(2,1)} %constant.17.clone.basis_ref) | copy-start | bytes 786436
  1.0 0.7 copy-start.1
  7.9 2.8 %collective-permute-start = (bf16[8,2,8,16,256]{4,3,2,1,0:T(8,128)(2,1)S(1)}, bf16[8,2,8,16,256]{4,3,2,1,0:T(8,128)(2,1)S(1)}, u32[]{:S(2)}, u32[]{:S(2)}) collective-permute-start(bf16[8,2,8,16,256]{4,3,2,1,0:T(8,128)(2,1)S(1)} %get-tuple-element.36), channel_id=1, source_target_pairs={{0,1},{1,0},{2,3},{3,2},{4,5},{5,4},{6,7},{7,6},{8,9},{9,8},{10,11... | collective-permute-start | bytes 3145736 | tf_op jit(solution)/shard_map/ppermute | solution.py:234
  10.8 9.5 %collective-permute-start.1 = (bf16[2,2,8,16,256]{4,3,2,1,0:T(8,128)(2,1)S(1)}, bf16[2,2,8,16,256]{4,3,2,1,0:T(8,128)(2,1)S(1)}, u32[]{:S(2)}, u32[]{:S(2)}) collective-permute-start(bf16[2,2,8,16,256]{4,3,2,1,0:T(8,128)(2,1)S(1)} %pad_maximum_fusion), channel_id=1, source_target_pairs={{0,2},{1,3},{2,0},{3,1},{4,6},{5,7},{6,4},{7,5},{8,10},{9,11},{10,... | collective-permute-start | bytes 786440 | tf_op jit(solution)/shard_map/ppermute | solution.py:217
  13.8 12.8 %collective-permute-start.2 = (bf16[2,2,8,16,256]{4,3,2,1,0:T(8,128)(2,1)S(1)}, bf16[2,2,8,16,256]{4,3,2,1,0:T(8,128)(2,1)S(1)}, u32[]{:S(2)}, u32[]{:S(2)}) collective-permute-start(bf16[2,2,8,16,256]{4,3,2,1,0:T(8,128)(2,1)S(1)} %pad_maximum_fusion.2), channel_id=1, source_target_pairs={{0,4},{1,5},{2,6},{3,7},{4,0},{5,1},{6,2},{7,3},{8,12},{9,13},{10,... | collective-permute-start | bytes 786440 | tf_op jit(solution)/shard_map/ppermute | solution.py:217
  15.4 14.9 %collective-permute-start.6 = (bf16[2,2,8,16,256]{4,3,2,1,0:T(8,128)(2,1)S(1)}, bf16[2,2,8,16,256]{4,3,2,1,0:T(8,128)(2,1)S(1)}, u32[]{:S(2)}, u32[]{:S(2)}) collective-permute-start(bf16[2,2,8,16,256]{4,3,2,1,0:T(8,128)(2,1)S(1)} %pad_maximum_fusion.1.rest_0_), channel_id=1, source_target_pairs={{0,16},{16,0},{1,17},{17,1},{2,18},{18,2},{3,19},{19,3},{4,20},{20... | collective-permute-start | bytes 786440 | tf_op jit(solution)/shard_map/ppermute | solution.py:217
  17.0 11.6 %collective-permute-start.4 = (bf16[2,2,5,16,256]{4,3,2,1,0:T(8,128)(2,1)S(1)}, bf16[2,2,5,16,256]{4,3,2,1,0:T(8,128)(2,1)S(1)}, u32[]{:S(2)}, u32[]{:S(2)}) collective-permute-start(bf16[2,2,5,16,256]{4,3,2,1,0:T(8,128)(2,1)S(1)} %pad_maximum_fusion.5), channel_id=1, source_target_pairs={{0,8},{1,9},{2,10},{3,11},{4,12},{5,13},{6,14},{7,15},{8,0},{9,1},... | collective-permute-start | bytes 491528 | tf_op jit(solution)/shard_map/ppermute | solution.py:217
  20.3 12.3 %collective-permute-start.3 = (bf16[2,2,8,16,256]{4,3,2,1,0:T(8,128)(2,1)S(1)}, bf16[2,2,8,16,256]{4,3,2,1,0:T(8,128)(2,1)S(1)}, u32[]{:S(2)}, u32[]{:S(2)}) collective-permute-start(bf16[2,2,8,16,256]{4,3,2,1,0:T(8,128)(2,1)S(1)} %pad_maximum_fusion.3), channel_id=1, source_target_pairs={{0,6},{1,7},{2,4},{3,5},{4,2},{5,3},{6,0},{7,1},{8,14},{9,15},{10,... | collective-permute-start | bytes 786440 | tf_op jit(solution)/shard_map/ppermute | solution.py:217
  26.5 17.0 %collective-permute-start.9 = (bf16[2,2,8,16,256]{4,3,2,1,0:T(8,128)(2,1)S(1)}, bf16[2,2,8,16,256]{4,3,2,1,0:T(8,128)(2,1)S(1)}, u32[]{:S(2)}, u32[]{:S(2)}) collective-permute-start(bf16[2,2,8,16,256]{4,3,2,1,0:T(8,128)(2,1)S(1)} %collective-permute-done.2.rest_2_), channel_id=1, source_target_pairs={{0,16},{16,0},{1,17},{17,1},{2,18},{18,2},{3,19},{19,3},{4,20},{20... | collective-permute-start | bytes 786440 | tf_op jit(solution)/shard_map/ppermute | solution.py:217
  28.1 18.0 %collective-permute-start.12 = (bf16[2,2,8,16,256]{4,3,2,1,0:T(8,128)(2,1)S(1)}, bf16[2,2,8,16,256]{4,3,2,1,0:T(8,128)(2,1)S(1)}, u32[]{:S(2)}, u32[]{:S(2)}) collective-permute-start(bf16[2,2,8,16,256]{4,3,2,1,0:T(8,128)(2,1)S(1)} %collective-permute-done.1.rest_1_), channel_id=1, source_target_pairs={{0,16},{16,0},{1,17},{17,1},{2,18},{18,2},{3,19},{19,3},{4,20},{20... | collective-permute-start | bytes 786440 | tf_op jit(solution)/shard_map/ppermute | solution.py:217
  28.7 14.9 %collective-permute-start.10 = (bf16[2,2,5,16,256]{4,3,2,1,0:T(8,128)(2,1)S(1)}, bf16[2,2,5,16,256]{4,3,2,1,0:T(8,128)(2,1)S(1)}, u32[]{:S(2)}, u32[]{:S(2)}) collective-permute-start(bf16[2,2,5,16,256]{4,3,2,1,0:T(8,128)(2,1)S(1)} %get-tuple-element.50), channel_id=1, source_target_pairs={{0,10},{1,11},{2,8},{3,9},{4,14},{5,15},{6,12},{7,13},{8,2},{9,3},... | collective-permute-start | bytes 491528 | tf_op jit(solution)/shard_map/ppermute | solution.py:217
  30.4 17.3 %collective-permute-start.5 = (bf16[2,2,5,16,256]{4,3,2,1,0:T(8,128)(2,1)S(1)}, bf16[2,2,5,16,256]{4,3,2,1,0:T(8,128)(2,1)S(1)}, u32[]{:S(2)}, u32[]{:S(2)}) collective-permute-start(bf16[2,2,5,16,256]{4,3,2,1,0:T(8,128)(2,1)S(1)} %get-tuple-element.45), channel_id=1, source_target_pairs={{0,12},{1,13},{2,14},{3,15},{4,8},{5,9},{6,10},{7,11},{8,4},{9,5},... | collective-permute-start | bytes 491528 | tf_op jit(solution)/shard_map/ppermute | solution.py:217
  32.6 19.0 %collective-permute-start.7 = (bf16[2,2,8,16,256]{4,3,2,1,0:T(8,128)(2,1)S(1)}, bf16[2,2,8,16,256]{4,3,2,1,0:T(8,128)(2,1)S(1)}, u32[]{:S(2)}, u32[]{:S(2)}) collective-permute-start(bf16[2,2,8,16,256]{4,3,2,1,0:T(8,128)(2,1)S(1)} %collective-permute-done.3.rest_3_), channel_id=1, source_target_pairs={{0,16},{16,0},{1,17},{17,1},{2,18},{18,2},{3,19},{19,3},{4,20},{20... | collective-permute-start | bytes 786440 | tf_op jit(solution)/shard_map/ppermute | solution.py:217
  43.5 8.1 %collective-permute-start.11 = (bf16[2,2,5,16,256]{4,3,2,1,0:T(8,128)(2,1)S(1)}, bf16[2,2,5,16,256]{4,3,2,1,0:T(8,128)(2,1)S(1)}, u32[]{:S(2)}, u32[]{:S(2)}) collective-permute-start(bf16[2,2,5,16,256]{4,3,2,1,0:T(8,128)(2,1)S(1)} %fusion), channel_id=1, source_target_pairs={{0,14},{1,15},{2,12},{3,13},{4,10},{5,11},{6,8},{7,9},{8,6},{9,7},... | collective-permute-start | bytes 491528 | tf_op jit(solution)/shard_map/ppermute | solution.py:217
  46.1 9.7 %collective-permute-start.13 = (bf16[4,2,5,16,256]{4,3,2,1,0:T(8,128)(2,1)S(1)}, bf16[4,2,5,16,256]{4,3,2,1,0:T(8,128)(2,1)S(1)}, u32[]{:S(2)}, u32[]{:S(2)}) collective-permute-start(bf16[4,2,5,16,256]{4,3,2,1,0:T(8,128)(2,1)S(1)} %constant_dynamic-update-slice_fusion.rest_4_), channel_id=1, source_target_pairs={{0,16},{16,0},{1,17},{17,1},{2,18},{18,2},{3,19},{19,3},{4,20},{20... | collective-permute-start | bytes 983048 | tf_op jit(solution)/shard_map/ppermute | solution.py:217
  47.6 12.9 %collective-permute-start.17 = (bf16[2,2,5,16,256]{4,3,2,1,0:T(8,128)(2,1)S(1)}, bf16[2,2,5,16,256]{4,3,2,1,0:T(8,128)(2,1)S(1)}, u32[]{:S(2)}, u32[]{:S(2)}) collective-permute-start(bf16[2,2,5,16,256]{4,3,2,1,0:T(8,128)(2,1)S(1)} %collective-permute-done.5.rest_5_), channel_id=1, source_target_pairs={{0,16},{16,0},{1,17},{17,1},{2,18},{18,2},{3,19},{19,3},{4,20},{20... | collective-permute-start | bytes 491528 | tf_op jit(solution)/shard_map/ppermute | solution.py:217
  51.6 9.0 %collective-permute-start.18 = (bf16[2,2,5,16,256]{4,3,2,1,0:T(8,128)(2,1)S(1)}, bf16[2,2,5,16,256]{4,3,2,1,0:T(8,128)(2,1)S(1)}, u32[]{:S(2)}, u32[]{:S(2)}) collective-permute-start(bf16[2,2,5,16,256]{4,3,2,1,0:T(8,128)(2,1)S(1)} %collective-permute-done.11.rest_6_), channel_id=1, source_target_pairs={{0,16},{16,0},{1,17},{17,1},{2,18},{18,2},{3,19},{19,3},{4,20},{20... | collective-permute-start | bytes 491528 | tf_op jit(solution)/shard_map/ppermute | solution.py:217
  53.2 13.0 %collective-permute-start.8 = (bf16[2,2,3,16,256]{4,3,2,1,0:T(8,128)(2,1)S(1)}, bf16[2,2,3,16,256]{4,3,2,1,0:T(8,128)(2,1)S(1)}, u32[]{:S(2)}, u32[]{:S(2)}) collective-permute-start(bf16[2,2,3,16,256]{4,3,2,1,0:T(8,128)(2,1)S(1)} %pad_maximum_fusion.9), channel_id=1, source_target_pairs={{0,8},{1,9},{2,10},{3,11},{4,12},{5,13},{6,14},{7,15},{8,0},{9,1},... | collective-permute-start | bytes 294920 | tf_op jit(solution)/shard_map/ppermute | solution.py:217
  55.8 10.4 %collective-permute-start.16 = (bf16[2,2,3,16,256]{4,3,2,1,0:T(8,128)(2,1)S(1)}, bf16[2,2,3,16,256]{4,3,2,1,0:T(8,128)(2,1)S(1)}, u32[]{:S(2)}, u32[]{:S(2)}) collective-permute-start(bf16[2,2,3,16,256]{4,3,2,1,0:T(8,128)(2,1)S(1)} %get-tuple-element.55), channel_id=1, source_target_pairs={{0,14},{1,15},{2,12},{3,13},{4,10},{5,11},{6,8},{7,9},{8,6},{9,7},... | collective-permute-start | bytes 294920 | tf_op jit(solution)/shard_map/ppermute | solution.py:217
  57.7 8.5 %collective-permute-start.15 = (bf16[2,2,3,16,256]{4,3,2,1,0:T(8,128)(2,1)S(1)}, bf16[2,2,3,16,256]{4,3,2,1,0:T(8,128)(2,1)S(1)}, u32[]{:S(2)}, u32[]{:S(2)}) collective-permute-start(bf16[2,2,3,16,256]{4,3,2,1,0:T(8,128)(2,1)S(1)} %get-tuple-element.54), channel_id=1, source_target_pairs={{0,12},{1,13},{2,14},{3,15},{4,8},{5,9},{6,10},{7,11},{8,4},{9,5},... | collective-permute-start | bytes 294920 | tf_op jit(solution)/shard_map/ppermute | solution.py:217
  60.6 10.7 %collective-permute-start.14 = (bf16[2,2,3,16,256]{4,3,2,1,0:T(8,128)(2,1)S(1)}, bf16[2,2,3,16,256]{4,3,2,1,0:T(8,128)(2,1)S(1)}, u32[]{:S(2)}, u32[]{:S(2)}) collective-permute-start(bf16[2,2,3,16,256]{4,3,2,1,0:T(8,128)(2,1)S(1)} %pad_maximum_fusion.8), channel_id=1, source_target_pairs={{0,10},{1,11},{2,8},{3,9},{4,14},{5,15},{6,12},{7,13},{8,2},{9,3},... | collective-permute-start | bytes 294920 | tf_op jit(solution)/shard_map/ppermute | solution.py:217
  71.3 7.0 %collective-permute-start.20 = (bf16[4,2,3,16,256]{4,3,2,1,0:T(8,128)(2,1)S(1)}, bf16[4,2,3,16,256]{4,3,2,1,0:T(8,128)(2,1)S(1)}, u32[]{:S(2)}, u32[]{:S(2)}) collective-permute-start(bf16[4,2,3,16,256]{4,3,2,1,0:T(8,128)(2,1)S(1)} %constant_dynamic-update-slice_fusion.4.rest_5_), channel_id=1, source_target_pairs={{0,16},{16,0},{1,17},{17,1},{2,18},{18,2},{3,19},{19,3},{4,20},{20... | collective-permute-start | bytes 589832 | tf_op jit(solution)/shard_map/ppermute | solution.py:217
  71.8 8.3 %collective-permute-start.19 = (bf16[4,2,3,16,256]{4,3,2,1,0:T(8,128)(2,1)S(1)}, bf16[4,2,3,16,256]{4,3,2,1,0:T(8,128)(2,1)S(1)}, u32[]{:S(2)}, u32[]{:S(2)}) collective-permute-start(bf16[4,2,3,16,256]{4,3,2,1,0:T(8,128)(2,1)S(1)} %constant_dynamic-update-slice_fusion.2.rest_4_), channel_id=1, source_target_pairs={{0,16},{16,0},{1,17},{17,1},{2,18},{18,2},{3,19},{19,3},{4,20},{20... | collective-permute-start | bytes 589832 | tf_op jit(solution)/shard_map/ppermute | solution.py:217

commit v5 on v2

--- a/solution.py
+++ b/solution.py
@@ -223,7 +223,7 @@
     parts = lax.axis_size("seg")
     chips = parts // PLANES // 2
     bins_local = F // parts
-    middle = (5 * bins_local + 4) // 8
+    middle = (4 * bins_local + 4) // 8
     group = lax.axis_index("grp")
     rounds = plan.shape[1]
     offset = lax.dynamic_index_in_dim(plan, group, 0, keepdims=False) ^ group
@@ -231,7 +231,7 @@
 
     *mine, for_sibling = head(waveform, valid_count, lax.axis_index("seg"), parts)
     theirs = lax.ppermute(for_sibling, "seg", [(s, s ^ 1) for s in range(parts)])
-    seg_lane, far_lane, grp_lane = Lane(parts), Lane(2), Lane(2 * (groups - 1))
+    seg_lane, far_lane, grp_lane = Lane(parts), Lane(2), Lane(3 * (groups - 1))
     sides = [[] for _ in range(groups)]
 
     def both(n, low=0, high=bins_local):
@@ -256,18 +256,19 @@
     beside_blocks = [scatter(seg_lane, n, after=far_blocks[:1] if n > beside[0] else ()) for n in beside]
     beside_done = [forward([block]) for block in beside_blocks][-1]
     far_done = [forward([block]) for block in far_blocks]
-    waits = {(0, farthest[0]): [own_done], (0, farthest[-1]): [beside_done]}
-    waits[middle, farthest[0]] = [far_done[0]]
-    for low, high in ((0, middle), (middle, bins_local)):
-        for n in farthest:
-            forward([scatter(far_lane, n, low, high, waits.get((low, n), ()))])
+    waits = {farthest[0]: [own_done], farthest[-1]: [beside_done]}
+    *most, last = [scatter(far_lane, n, after=waits.get(n, ())) for n in farthest]
+    for block in most:
+        forward([block])
+    whole = len(sides[0])
+    parts_of_bins = ((0, middle), (middle, bins_local))
+    for low, high in parts_of_bins:
+        forward([last[:, :, low:high]])
 
     out = None
-    whole, last = len(sides[0]) - 2 * chips, chips
-    for n, (low, high) in enumerate(((0, middle), (middle, bins_local))):
-        held = [0] * whole + [low] * last
-        chosen = [side[:whole] + side[whole + n * last :][:last] for side in sides]
-        out = add_bins(out, select, chosen, held, low, high, bins_local, rounds)
+    for n, (low, high) in enumerate(parts_of_bins):
+        chosen = [side[:whole] + side[whole + n :][:1] for side in sides]
+        out = add_bins(out, select, chosen, [0] * whole + [low], low, high, bins_local, rounds)
     rows = waveform.shape[0]
     out = out.reshape(bins_local, 2, rows, rows // LANES, rounds, LANES).transpose(0, 1, 2, 4, 3, 5)
     return out.reshape(bins_local, 2, rows, rounds, rows)

time: 83.2 us -> 90.3 us (1.085)
  the two profiles are of different devices: /device:TPU:0 before, /device:TPU:16 now
where the time goes in v5:
time: 90.3 us; the launch traced here: 90 us
  waiting for transfers between devices  47 us (52%)
  starting transfers between devices  21.1 us (23%)
  Pallas kernels  18.6 us (21%)
  local copies, waits for them, and re-layouts  1.97 us (2%)
  other arithmetic  1.23 us (1%)
    ppermute x16, waiting for transfers between devices, send(): self.sent.append(lax.ppermute(block, axis, pairs))  45.3 us
    ppermute x16, starting transfers between devices, send(): self.sent.append(lax.ppermute(block, axis, pairs))  21 us
    pallas_call x2, Pallas kernels, add_bins(): pl.pallas_call(functools.partial(cross_kernel, groups=groups, held=held,...  12.4 us
    pallas_call x1, Pallas kernels, head(): pl.pallas_call(functools.partial(head_kernel, parts=parts), out_shape=[ja...  6.21 us
  transfers between devices with their start and end apart: 17, of which 10 were waited for; matrix products, arithmetic and copies ran while one was open for 2% of the time, Pallas kernels for 7%

profile of v5, /device:TPU:16, one launch (start us, length us, event | category | flops | bytes accessed | tf_op | source)
XLA Modules:
  0.0 90.0 jit_solution(15157454405688203976)
XLA Ops:
  0.0 0.9 %copy-done = bf16[256,512]{1,0:T(8,128)(2,1)S(1)} copy-done((bf16[256,512]{1,0:T(8,128)(2,1)S(1)}, bf16[256,512]{1,0:T(8,128)(2,1)}, u32[]{:S(2)}) %copy-start) | copy-done | bytes 262168
  1.0 0.7 copy-done.1
  1.7 6.2 %spectra.1 = (bf16[1,2,8,16,256]{4,3,2,1,0:T(8,128)(2,1)S(1)}, bf16[1,2,8,16,256]{4,3,2,1,0:T(8,128)(2,1)S(1)}, bf16[1,2,8,16,256]{4,3,2,1,0:T(8,128)(2,1)S(1)},...) custom-call(s32[1]{0:T(128)} %bitcast.me_ref, ...), custom_call_target="tpu_custom_call" | custom-call | tf_op jit(solution)/shard_map/spectra/pallas_call | solution.py:91
  8.9 1.7 %collective-permute-done = bf16[8,2,8,16,256]{4,3,2,1,0:T(8,128)(2,1)S(1)} collective-permute-done((bf16[8,2,8,16,256]{4,3,2,1,0:T(8,128)(2,1)S(1)}, bf16[8,2,8,16,256]{4,3,2,1,0:T(8,128)(2,1)S(1)}, u32[]{:S(2)}, u32[]{:S(2)}) %collective-permute-start) | collective-permute-done | bytes 1048608 | tf_op jit(solution)/shard_map/ppermute | solution.py:233
  10.9 1.9 %collective-permute-start.1 = (bf16[2,2,8,16,256]{4,3,2,1,0:T(8,128)(2,1)S(1)}, bf16[2,2,8,16,256]{4,3,2,1,0:T(8,128)(2,1)S(1)}, u32[]{:S(2)}, u32[]{:S(2)}) collective-permute-start(bf16[2,2,8,16,256]{4,3,2,1,0:T(8,128)(2,1)S(1)} %pad_maximum_fusion), channel_id=1, source_target_pairs={{0,2},{1,3},{2,0},{3,1},{4,6},{5,7},{6,4},{7,5},{8,10},{9,11},{10,... | collective-permute-start | bytes 786440 | tf_op jit(solution)/shard_map/ppermute | solution.py:217
  12.7 1.6 %collective-permute-start.8 = (bf16[2,2,8,16,256]{4,3,2,1,0:T(8,128)(2,1)S(1)}, bf16[2,2,8,16,256]{4,3,2,1,0:T(8,128)(2,1)S(1)}, u32[]{:S(2)}, u32[]{:S(2)}) collective-permute-start(bf16[2,2,8,16,256]{4,3,2,1,0:T(8,128)(2,1)S(1)} %pad_maximum_fusion.1.rest_0_), channel_id=1, source_target_pairs={{0,16},{16,0},{1,17},{17,1},{2,18},{18,2},{3,19},{19,3},{4,20},{20... | collective-permute-start | bytes 786440 | tf_op jit(solution)/shard_map/ppermute | solution.py:217
  14.4 8.2 %collective-permute-done.3.rest_4_ = bf16[2,2,8,16,256]{4,3,2,1,0:T(8,128)(2,1)S(1)} collective-permute-done((bf16[2,2,8,16,256]{4,3,2,1,0:T(8,128)(2,1)S(1)}, bf16[2,2,8,16,256]{4,3,2,1,0:T(8,128)(2,1)S(1)}, u32[]{:S(2)}, u32[]{:S(2)}) %collective-permute-start.3) | collective-permute-done | bytes 262176 | tf_op jit(solution)/shard_map/ppermute | solution.py:217
  22.6 5.5 %collective-permute-start.4 = (bf16[2,2,8,16,256]{4,3,2,1,0:T(8,128)(2,1)S(1)}, bf16[2,2,8,16,256]{4,3,2,1,0:T(8,128)(2,1)S(1)}, u32[]{:S(2)}, u32[]{:S(2)}) collective-permute-start(bf16[2,2,8,16,256]{4,3,2,1,0:T(8,128)(2,1)S(1)} %get-tuple-element.34), channel_id=1, source_target_pairs={{0,6},{1,7},{2,4},{3,5},{4,2},{5,3},{6,0},{7,1},{8,14},{9,15},{10,... | collective-permute-start | bytes 786440 | tf_op jit(solution)/shard_map/ppermute | solution.py:217
  28.5 1.6 %collective-permute-start.6 = (bf16[2,2,8,16,256]{4,3,2,1,0:T(8,128)(2,1)S(1)}, bf16[2,2,8,16,256]{4,3,2,1,0:T(8,128)(2,1)S(1)}, u32[]{:S(2)}, u32[]{:S(2)}) collective-permute-start(bf16[2,2,8,16,256]{4,3,2,1,0:T(8,128)(2,1)S(1)} %collective-permute-done.1.rest_1_), channel_id=1, source_target_pairs={{0,16},{16,0},{1,17},{17,1},{2,18},{18,2},{3,19},{19,3},{4,20},{20... | collective-permute-start | bytes 786440 | tf_op jit(solution)/shard_map/ppermute | solution.py:217
  30.1 0.8 collective-permute-start.5
  30.9 9.5 %collective-permute-done.4.rest_3_ = bf16[2,2,8,16,256]{4,3,2,1,0:T(8,128)(2,1)S(1)} collective-permute-done((bf16[2,2,8,16,256]{4,3,2,1,0:T(8,128)(2,1)S(1)}, bf16[2,2,8,16,256]{4,3,2,1,0:T(8,128)(2,1)S(1)}, u32[]{:S(2)}, u32[]{:S(2)}) %collective-permute-start.4) | collective-permute-done | bytes 262176 | tf_op jit(solution)/shard_map/ppermute | solution.py:217
  40.3 1.5 %collective-permute-start.9 = (bf16[2,2,8,16,256]{4,3,2,1,0:T(8,128)(2,1)S(1)}, bf16[2,2,8,16,256]{4,3,2,1,0:T(8,128)(2,1)S(1)}, u32[]{:S(2)}, u32[]{:S(2)}) collective-permute-start(bf16[2,2,8,16,256]{4,3,2,1,0:T(8,128)(2,1)S(1)} %collective-permute-done.4.rest_3_), channel_id=1, source_target_pairs={{0,16},{16,0},{1,17},{17,1},{2,18},{18,2},{3,19},{19,3},{4,20},{20... | collective-permute-start | bytes 786440 | tf_op jit(solution)/shard_map/ppermute | solution.py:217
  41.9 3.1 %collective-permute-done.2.rest_2_ = bf16[2,2,8,16,256]{4,3,2,1,0:T(8,128)(2,1)S(1)} collective-permute-done((bf16[2,2,8,16,256]{4,3,2,1,0:T(8,128)(2,1)S(1)}, bf16[2,2,8,16,256]{4,3,2,1,0:T(8,128)(2,1)S(1)}, u32[]{:S(2)}, u32[]{:S(2)}) %collective-permute-start.2) | collective-permute-done | bytes 262176 | tf_op jit(solution)/shard_map/ppermute | solution.py:217
  45.0 1.5 %collective-permute-start.11 = (bf16[2,2,8,16,256]{4,3,2,1,0:T(8,128)(2,1)S(1)}, bf16[2,2,8,16,256]{4,3,2,1,0:T(8,128)(2,1)S(1)}, u32[]{:S(2)}, u32[]{:S(2)}) collective-permute-start(bf16[2,2,8,16,256]{4,3,2,1,0:T(8,128)(2,1)S(1)} %collective-permute-done.2.rest_2_), channel_id=1, source_target_pairs={{0,16},{16,0},{1,17},{17,1},{2,18},{18,2},{3,19},{19,3},{4,20},{20... | collective-permute-start | bytes 786440 | tf_op jit(solution)/shard_map/ppermute | solution.py:217
  46.7 1.9 %collective-permute-start.10 = (bf16[2,2,8,16,256]{4,3,2,1,0:T(8,128)(2,1)S(1)}, bf16[2,2,8,16,256]{4,3,2,1,0:T(8,128)(2,1)S(1)}, u32[]{:S(2)}, u32[]{:S(2)}) collective-permute-start(bf16[2,2,8,16,256]{4,3,2,1,0:T(8,128)(2,1)S(1)} %pad_maximum_fusion.7), channel_id=1, source_target_pairs={{0,14},{1,15},{2,12},{3,13},{4,10},{5,11},{6,8},{7,9},{8,6},{9,7},... | collective-permute-start | bytes 786440 | tf_op jit(solution)/shard_map/ppermute | solution.py:217
  49.2 5.1 %collective-permute-done.11.rest_10_ = bf16[2,2,8,16,256]{4,3,2,1,0:T(8,128)(2,1)S(1)} collective-permute-done((bf16[2,2,8,16,256]{4,3,2,1,0:T(8,128)(2,1)S(1)}, bf16[2,2,8,16,256]{4,3,2,1,0:T(8,128)(2,1)S(1)}, u32[]{:S(2)}, u32[]{:S(2)}) %collective-permute-start.11) | collective-permute-done | bytes 262176 | tf_op jit(solution)/shard_map/ppermute | solution.py:217
  54.3 1.5 %collective-permute-start.13 = (bf16[2,2,8,16,256]{4,3,2,1,0:T(8,128)(2,1)S(1)}, bf16[2,2,8,16,256]{4,3,2,1,0:T(8,128)(2,1)S(1)}, u32[]{:S(2)}, u32[]{:S(2)}) collective-permute-start(bf16[2,2,8,16,256]{4,3,2,1,0:T(8,128)(2,1)S(1)} %collective-permute-done.5.rest_5_), channel_id=1, source_target_pairs={{0,16},{16,0},{1,17},{17,1},{2,18},{18,2},{3,19},{19,3},{4,20},{20... | collective-permute-start | bytes 786440 | tf_op jit(solution)/shard_map/ppermute | solution.py:217
  55.8 11.2 %collective-permute-done.7.rest_6_ = bf16[2,2,8,16,256]{4,3,2,1,0:T(8,128)(2,1)S(1)} collective-permute-done((bf16[2,2,8,16,256]{4,3,2,1,0:T(8,128)(2,1)S(1)}, bf16[2,2,8,16,256]{4,3,2,1,0:T(8,128)(2,1)S(1)}, u32[]{:S(2)}, u32[]{:S(2)}) %collective-permute-start.7) | collective-permute-done | bytes 262176 | tf_op jit(solution)/shard_map/ppermute | solution.py:217
  67.6 3.0 %collective-permute-done.10 = bf16[2,2,8,16,256]{4,3,2,1,0:T(8,128)(2,1)S(1)} collective-permute-done((bf16[2,2,8,16,256]{4,3,2,1,0:T(8,128)(2,1)S(1)}, bf16[2,2,8,16,256]{4,3,2,1,0:T(8,128)(2,1)S(1)}, u32[]{:S(2)}, u32[]{:S(2)}) %collective-permute-start.10) | collective-permute-done | bytes 262176 | tf_op jit(solution)/shard_map/ppermute | solution.py:217
  70.9 1.7 %collective-permute-start.15 = (bf16[2,2,4,16,256]{4,3,2,1,0:T(8,128)(2,1)S(1)}, bf16[2,2,4,16,256]{4,3,2,1,0:T(8,128)(2,1)S(1)}, u32[]{:S(2)}, u32[]{:S(2)}) collective-permute-start(bf16[2,2,4,16,256]{4,3,2,1,0:T(8,128)(2,1)S(1)} %get-tuple-element.45.rest_7_), channel_id=1, source_target_pairs={{0,16},{16,0},{1,17},{17,1},{2,18},{18,2},{3,19},{19,3},{4,20},{20... | collective-permute-start | bytes 393224 | tf_op jit(solution)/shard_map/ppermute | solution.py:217
  72.7 3.0 %collective-permute-done.14.rest_14_ = bf16[2,2,8,16,256]{4,3,2,1,0:T(8,128)(2,1)S(1)} collective-permute-done((bf16[2,2,8,16,256]{4,3,2,1,0:T(8,128)(2,1)S(1)}, bf16[2,2,8,16,256]{4,3,2,1,0:T(8,128)(2,1)S(1)}, u32[]{:S(2)}, u32[]{:S(2)}) %collective-permute-start.14) | collective-permute-done | bytes 262176 | tf_op jit(solution)/shard_map/ppermute | solution.py:217
  75.7 1.9 %collective-permute-done.16.rest_15_ = bf16[2,2,4,16,256]{4,3,2,1,0:T(8,128)(2,1)S(1)} collective-permute-done((bf16[2,2,4,16,256]{4,3,2,1,0:T(8,128)(2,1)S(1)}, bf16[2,2,4,16,256]{4,3,2,1,0:T(8,128)(2,1)S(1)}, u32[]{:S(2)}, u32[]{:S(2)}) %collective-permute-start.16) | collective-permute-done | bytes 131104 | tf_op jit(solution)/shard_map/ppermute | solution.py:217
  77.6 6.2 %cross.2.rest_16_ = bf16[8,2,4096,128]{3,2,1,0:T(8,128)(2,1)} custom-call(bf16[1024,256]{1,0:T(8,128)(2,1)S(1)} %and_convert_fusion.select_ref, bf16[2,2,8,16,256]{4,3,2,1,0:T(8,128)(2,1)S(1)} %pad_maximum_fusion.1.rest_0_, bf16[2,2,8,16,256]{4,3,2,1,0:T(8,128)(2,1)S(1)} %collective-permute-done.1.rest_1_, ...), custom_call_target="tpu_custom_call" | custom-call | flops 1073741824 | bytes 8388608 | tf_op jit(solution)/shard_map/cross/pallas_call | solution.py:187
  83.8 6.2 %cross.3 = bf16[8,2,4096,128]{3,2,1,0:T(8,128)(2,1)} custom-call(bf16[1024,256]{1,0:T(8,128)(2,1)S(1)} %and_convert_fusion.select_ref, bf16[2,2,8,16,256]{4,3,2,1,0:T(8,128)(2,1)S(1)} %pad_maximum_fusion.1.rest_0_, bf16[2,2,8,16,256]{4,3,2,1,0:T(8,128)(2,1)S(1)} %collective-permute-done.1.rest_1_, ...), custom_call_target="tpu_custom_call", output_to_operand_aliasing={{}: (17, {})} | custom-call | flops 1073741824 | bytes 8388608 | tf_op jit(solution)/shard_map/cross/pallas_call | solution.py:187
  (33 shorter events, 3.4 us)
Async XLA Ops:
  0.0 0.9 %copy-start = (bf16[256,512]{1,0:T(8,128)(2,1)S(1)}, bf16[256,512]{1,0:T(8,128)(2,1)}, u32[]{:S(2)}) copy-start(bf16[256,512]{1,0:T(8,128)(2,1)} %constant.17.clone.basis_ref) | copy-start | bytes 786436
  1.0 0.7 copy-start.1
  7.9 2.7 %collective-permute-start = (bf16[8,2,8,16,256]{4,3,2,1,0:T(8,128)(2,1)S(1)}, bf16[8,2,8,16,256]{4,3,2,1,0:T(8,128)(2,1)S(1)}, u32[]{:S(2)}, u32[]{:S(2)}) collective-permute-start(bf16[8,2,8,16,256]{4,3,2,1,0:T(8,128)(2,1)S(1)} %get-tuple-element.27), channel_id=1, source_target_pairs={{0,1},{1,0},{2,3},{3,2},{4,5},{5,4},{6,7},{7,6},{8,9},{9,8},{10,11... | collective-permute-start | bytes 3145736 | tf_op jit(solution)/shard_map/ppermute | solution.py:233
  10.7 11.8 %collective-permute-start.3 = (bf16[2,2,8,16,256]{4,3,2,1,0:T(8,128)(2,1)S(1)}, bf16[2,2,8,16,256]{4,3,2,1,0:T(8,128)(2,1)S(1)}, u32[]{:S(2)}, u32[]{:S(2)}) collective-permute-start(bf16[2,2,8,16,256]{4,3,2,1,0:T(8,128)(2,1)S(1)} %pad_maximum_fusion.4), channel_id=1, source_target_pairs={{0,8},{1,9},{2,10},{3,11},{4,12},{5,13},{6,14},{7,15},{8,0},{9,1},... | collective-permute-start | bytes 786440 | tf_op jit(solution)/shard_map/ppermute | solution.py:217
  10.9 17.6 %collective-permute-start.1 = (bf16[2,2,8,16,256]{4,3,2,1,0:T(8,128)(2,1)S(1)}, bf16[2,2,8,16,256]{4,3,2,1,0:T(8,128)(2,1)S(1)}, u32[]{:S(2)}, u32[]{:S(2)}) collective-permute-start(bf16[2,2,8,16,256]{4,3,2,1,0:T(8,128)(2,1)S(1)} %pad_maximum_fusion), channel_id=1, source_target_pairs={{0,2},{1,3},{2,0},{3,1},{4,6},{5,7},{6,4},{7,5},{8,10},{9,11},{10,... | collective-permute-start | bytes 786440 | tf_op jit(solution)/shard_map/ppermute | solution.py:217
  12.7 18.1 %collective-permute-start.8 = (bf16[2,2,8,16,256]{4,3,2,1,0:T(8,128)(2,1)S(1)}, bf16[2,2,8,16,256]{4,3,2,1,0:T(8,128)(2,1)S(1)}, u32[]{:S(2)}, u32[]{:S(2)}) collective-permute-start(bf16[2,2,8,16,256]{4,3,2,1,0:T(8,128)(2,1)S(1)} %pad_maximum_fusion.1.rest_0_), channel_id=1, source_target_pairs={{0,16},{16,0},{1,17},{17,1},{2,18},{18,2},{3,19},{19,3},{4,20},{20... | collective-permute-start | bytes 786440 | tf_op jit(solution)/shard_map/ppermute | solution.py:217
  22.6 17.8 %collective-permute-start.4 = (bf16[2,2,8,16,256]{4,3,2,1,0:T(8,128)(2,1)S(1)}, bf16[2,2,8,16,256]{4,3,2,1,0:T(8,128)(2,1)S(1)}, u32[]{:S(2)}, u32[]{:S(2)}) collective-permute-start(bf16[2,2,8,16,256]{4,3,2,1,0:T(8,128)(2,1)S(1)} %get-tuple-element.34), channel_id=1, source_target_pairs={{0,6},{1,7},{2,4},{3,5},{4,2},{5,3},{6,0},{7,1},{8,14},{9,15},{10,... | collective-permute-start | bytes 786440 | tf_op jit(solution)/shard_map/ppermute | solution.py:217
  28.4 16.6 %collective-permute-start.2 = (bf16[2,2,8,16,256]{4,3,2,1,0:T(8,128)(2,1)S(1)}, bf16[2,2,8,16,256]{4,3,2,1,0:T(8,128)(2,1)S(1)}, u32[]{:S(2)}, u32[]{:S(2)}) collective-permute-start(bf16[2,2,8,16,256]{4,3,2,1,0:T(8,128)(2,1)S(1)} %pad_maximum_fusion.2), channel_id=1, source_target_pairs={{0,4},{1,5},{2,6},{3,7},{4,0},{5,1},{6,2},{7,3},{8,12},{9,13},{10,... | collective-permute-start | bytes 786440 | tf_op jit(solution)/shard_map/ppermute | solution.py:217
  28.5 18.0 %collective-permute-start.6 = (bf16[2,2,8,16,256]{4,3,2,1,0:T(8,128)(2,1)S(1)}, bf16[2,2,8,16,256]{4,3,2,1,0:T(8,128)(2,1)S(1)}, u32[]{:S(2)}, u32[]{:S(2)}) collective-permute-start(bf16[2,2,8,16,256]{4,3,2,1,0:T(8,128)(2,1)S(1)} %collective-permute-done.1.rest_1_), channel_id=1, source_target_pairs={{0,16},{16,0},{1,17},{17,1},{2,18},{18,2},{3,19},{19,3},{4,20},{20... | collective-permute-start | bytes 786440 | tf_op jit(solution)/shard_map/ppermute | solution.py:217
  30.1 16.5 %collective-permute-start.5 = (bf16[2,2,8,16,256]{4,3,2,1,0:T(8,128)(2,1)S(1)}, bf16[2,2,8,16,256]{4,3,2,1,0:T(8,128)(2,1)S(1)}, u32[]{:S(2)}, u32[]{:S(2)}) collective-permute-start(bf16[2,2,8,16,256]{4,3,2,1,0:T(8,128)(2,1)S(1)} %get-tuple-element.36), channel_id=1, source_target_pairs={{0,10},{1,11},{2,8},{3,9},{4,14},{5,15},{6,12},{7,13},{8,2},{9,3},... | collective-permute-start | bytes 786440 | tf_op jit(solution)/shard_map/ppermute | solution.py:217
  40.3 6.4 %collective-permute-start.9 = (bf16[2,2,8,16,256]{4,3,2,1,0:T(8,128)(2,1)S(1)}, bf16[2,2,8,16,256]{4,3,2,1,0:T(8,128)(2,1)S(1)}, u32[]{:S(2)}, u32[]{:S(2)}) collective-permute-start(bf16[2,2,8,16,256]{4,3,2,1,0:T(8,128)(2,1)S(1)} %collective-permute-done.4.rest_3_), channel_id=1, source_target_pairs={{0,16},{16,0},{1,17},{17,1},{2,18},{18,2},{3,19},{19,3},{4,20},{20... | collective-permute-start | bytes 786440 | tf_op jit(solution)/shard_map/ppermute | solution.py:217
  45.0 9.2 %collective-permute-start.11 = (bf16[2,2,8,16,256]{4,3,2,1,0:T(8,128)(2,1)S(1)}, bf16[2,2,8,16,256]{4,3,2,1,0:T(8,128)(2,1)S(1)}, u32[]{:S(2)}, u32[]{:S(2)}) collective-permute-start(bf16[2,2,8,16,256]{4,3,2,1,0:T(8,128)(2,1)S(1)} %collective-permute-done.2.rest_2_), channel_id=1, source_target_pairs={{0,16},{16,0},{1,17},{17,1},{2,18},{18,2},{3,19},{19,3},{4,20},{20... | collective-permute-start | bytes 786440 | tf_op jit(solution)/shard_map/ppermute | solution.py:217
  46.6 20.5 %collective-permute-start.7 = (bf16[2,2,8,16,256]{4,3,2,1,0:T(8,128)(2,1)S(1)}, bf16[2,2,8,16,256]{4,3,2,1,0:T(8,128)(2,1)S(1)}, u32[]{:S(2)}, u32[]{:S(2)}) collective-permute-start(bf16[2,2,8,16,256]{4,3,2,1,0:T(8,128)(2,1)S(1)} %pad_maximum_fusion.6), channel_id=1, source_target_pairs={{0,12},{1,13},{2,14},{3,15},{4,8},{5,9},{6,10},{7,11},{8,4},{9,5},... | collective-permute-start | bytes 786440 | tf_op jit(solution)/shard_map/ppermute | solution.py:217
  46.7 23.8 %collective-permute-start.10 = (bf16[2,2,8,16,256]{4,3,2,1,0:T(8,128)(2,1)S(1)}, bf16[2,2,8,16,256]{4,3,2,1,0:T(8,128)(2,1)S(1)}, u32[]{:S(2)}, u32[]{:S(2)}) collective-permute-start(bf16[2,2,8,16,256]{4,3,2,1,0:T(8,128)(2,1)S(1)} %pad_maximum_fusion.7), channel_id=1, source_target_pairs={{0,14},{1,15},{2,12},{3,13},{4,10},{5,11},{6,8},{7,9},{8,6},{9,7},... | collective-permute-start | bytes 786440 | tf_op jit(solution)/shard_map/ppermute | solution.py:217
  48.6 22.0 %collective-permute-start.12 = (bf16[2,2,8,16,256]{4,3,2,1,0:T(8,128)(2,1)S(1)}, bf16[2,2,8,16,256]{4,3,2,1,0:T(8,128)(2,1)S(1)}, u32[]{:S(2)}, u32[]{:S(2)}) collective-permute-start(bf16[2,2,8,16,256]{4,3,2,1,0:T(8,128)(2,1)S(1)} %collective-permute-done.3.rest_4_), channel_id=1, source_target_pairs={{0,16},{16,0},{1,17},{17,1},{2,18},{18,2},{3,19},{19,3},{4,20},{20... | collective-permute-start | bytes 786440 | tf_op jit(solution)/shard_map/ppermute | solution.py:217
  54.3 16.6 %collective-permute-start.13 = (bf16[2,2,8,16,256]{4,3,2,1,0:T(8,128)(2,1)S(1)}, bf16[2,2,8,16,256]{4,3,2,1,0:T(8,128)(2,1)S(1)}, u32[]{:S(2)}, u32[]{:S(2)}) collective-permute-start(bf16[2,2,8,16,256]{4,3,2,1,0:T(8,128)(2,1)S(1)} %collective-permute-done.5.rest_5_), channel_id=1, source_target_pairs={{0,16},{16,0},{1,17},{17,1},{2,18},{18,2},{3,19},{19,3},{4,20},{20... | collective-permute-start | bytes 786440 | tf_op jit(solution)/shard_map/ppermute | solution.py:217
  67.0 8.6 %collective-permute-start.14 = (bf16[2,2,8,16,256]{4,3,2,1,0:T(8,128)(2,1)S(1)}, bf16[2,2,8,16,256]{4,3,2,1,0:T(8,128)(2,1)S(1)}, u32[]{:S(2)}, u32[]{:S(2)}) collective-permute-start(bf16[2,2,8,16,256]{4,3,2,1,0:T(8,128)(2,1)S(1)} %collective-permute-done.7.rest_6_), channel_id=1, source_target_pairs={{0,16},{16,0},{1,17},{17,1},{2,18},{18,2},{3,19},{19,3},{4,20},{20... | collective-permute-start | bytes 786440 | tf_op jit(solution)/shard_map/ppermute | solution.py:217
  70.6 7.1 %collective-permute-start.16 = (bf16[2,2,4,16,256]{4,3,2,1,0:T(8,128)(2,1)S(1)}, bf16[2,2,4,16,256]{4,3,2,1,0:T(8,128)(2,1)S(1)}, u32[]{:S(2)}, u32[]{:S(2)}) collective-permute-start(bf16[2,2,4,16,256]{4,3,2,1,0:T(8,128)(2,1)S(1)} %get-tuple-element.46.rest_7_), channel_id=1, source_target_pairs={{0,16},{16,0},{1,17},{17,1},{2,18},{18,2},{3,19},{19,3},{4,20},{20... | collective-permute-start | bytes 393224 | tf_op jit(solution)/shard_map/ppermute | solution.py:217
  70.9 12.9 %collective-permute-start.15 = (bf16[2,2,4,16,256]{4,3,2,1,0:T(8,128)(2,1)S(1)}, bf16[2,2,4,16,256]{4,3,2,1,0:T(8,128)(2,1)S(1)}, u32[]{:S(2)}, u32[]{:S(2)}) collective-permute-start(bf16[2,2,4,16,256]{4,3,2,1,0:T(8,128)(2,1)S(1)} %get-tuple-element.45.rest_7_), channel_id=1, source_target_pairs={{0,16},{16,0},{1,17},{17,1},{2,18},{18,2},{3,19},{19,3},{4,20},{20... | collective-permute-start | bytes 393224 | tf_op jit(solution)/shard_map/ppermute | solution.py:217

commit v6 on v3

--- a/solution.py
+++ b/solution.py
@@ -3,7 +3,6 @@
 
 import jax
 import jax.numpy as jnp
-import numpy as np
 from jax import lax
 from jax.experimental import pallas as pl
 from jax.experimental.pallas import tpu as pltpu
@@ -16,14 +15,21 @@
 MIB = 1024 * 1024
 
 
-def make_basis(samples, parts):
-    bins = np.arange(F).reshape(parts, 1, F // parts)
-    bins = np.concatenate([bins, bins], axis=1)
-    imag = np.zeros_like(bins)
-    imag[:, 1] = 1
-    bins, imag = bins.reshape(-1, 1), imag.reshape(-1, 1)
-    phase = (np.arange(samples)[None, :] * (K0 + bins) % samples) * (2.0 * math.pi / samples)
-    return np.where(imag == 1, -np.sin(phase), np.cos(phase))
+def fill_basis(basis_ref, parts):
+    rows, samples = basis_ref.shape
+    bins_local = F // parts
+    row = lax.broadcasted_iota(jnp.int32, (rows, LANES), 0)
+    lane = lax.broadcasted_iota(jnp.int32, (rows, LANES), 1)
+    part = row // bins_local % 2
+    bins = K0 + row // (2 * bins_local) * bins_local + row % bins_local
+    for q in range(samples // LANES):
+        turn = ((lane + q * LANES) * bins + part * (samples // 4)) % samples
+        x = (samples // 4 - jnp.minimum(turn, samples - turn)).astype(jnp.float32) * (2.0 * math.pi / samples)
+        x2 = x * x
+        series = 1.0 / 362880 - x2 * (1.0 / 39916800)
+        for term in (-1.0 / 5040, 1.0 / 120, -1.0 / 6, 1.0):
+            series = term + x2 * series
+        basis_ref[:, q * LANES : (q + 1) * LANES] = (x * series).astype(jnp.bfloat16)
 
 
 def swap_matrix(outer, inner):
@@ -33,8 +39,8 @@
     return (source == column).astype(jnp.float32).astype(jnp.bfloat16)
 
 
-def head_kernel(me_ref, wave_ref, valid_ref, basis_ref, *rest, parts):
-    out_refs, (held_ref, gated_ref, white_ref, sems) = rest[:-4], rest[-4:]
+def head_kernel(me_ref, wave_ref, valid_ref, *rest, parts):
+    out_refs, (held_ref, gated_ref, white_ref, basis_ref, sems) = rest[:-5], rest[-5:]
     rows, segs, samples = wave_ref.shape
     half = samples // 2
     step, copies = 16, sems.shape[0]
@@ -46,6 +52,7 @@
 
     for n in range(copies):
         copy(n).start()
+    fill_basis(basis_ref, parts)
     valid_rows = valid_ref[...]
     valid_cols = valid_rows.T
     times = lax.broadcasted_iota(jnp.int32, (step * segs, samples), 1)
@@ -84,24 +91,24 @@
 
 def head(waveform, valid_count, me, parts):
     rows, segs, samples = waveform.shape
-    basis = jnp.asarray(make_basis(samples, parts), dtype=jnp.bfloat16)
     vmem = pl.BlockSpec(memory_space=pltpu.VMEM)
     pairs = parts // 2
     block = (2, F // parts, segs, rows)
     return pl.pallas_call(
         functools.partial(head_kernel, parts=parts),
         out_shape=[jax.ShapeDtypeStruct((n,) + block, jnp.bfloat16) for n in [1] * pairs + [pairs]],
-        in_specs=[pl.BlockSpec(memory_space=pltpu.SMEM), pl.BlockSpec(memory_space=pltpu.HBM), vmem, vmem],
+        in_specs=[pl.BlockSpec(memory_space=pltpu.SMEM), pl.BlockSpec(memory_space=pltpu.HBM), vmem],
         out_specs=[vmem] * (pairs + 1),
         scratch_shapes=[
             pltpu.VMEM(waveform.shape, waveform.dtype),
             pltpu.VMEM((segs, rows, samples), jnp.bfloat16),
             pltpu.VMEM((segs, 2 * F, rows), jnp.float32),
+            pltpu.VMEM((2 * F, samples), jnp.bfloat16),
             pltpu.SemaphoreType.DMA((8,)),
         ],
         compiler_params=pltpu.CompilerParams(vmem_limit_bytes=48 * MIB),
         name="spectra",
-    )(me[None].astype(jnp.int32), waveform, valid_count.T, basis)
+    )(me[None].astype(jnp.int32), waveform, valid_count.T)
 
 
 def cross_kernel(select_ref, *rest, groups, held, low):

time: 83.1 us -> 82 us (0.987)
  local copies, waits for them, and re-layouts: 2 us -> 1.05 us
    unnamed x6 -> x4, local copies, waits for them, and re-layouts: 1.69 us -> 0.74 us
  transfers between devices with their start and end apart: 22 -> 22, of which waited for: 10 -> 9; matrix products, arithmetic and copies ran while one was open for 2% -> 2% of each run, Pallas kernels for 9% -> 9%
where the time goes in v6:
time: 82 us; the launch traced here: 81.8 us
  starting transfers between devices  38.2 us (47%)
  waiting for transfers between devices  22.8 us (28%)
  Pallas kernels  18.4 us (22%)
  other arithmetic  1.23 us (2%)
  local copies, waits for them, and re-layouts  1.05 us (1%)
    ppermute x21, starting transfers between devices, send(): self.sent.append(lax.ppermute(block, axis, pairs))  37.7 us
    ppermute x21, waiting for transfers between devices, send(): self.sent.append(lax.ppermute(block, axis, pairs))  21.4 us
    pallas_call x2, Pallas kernels, add_bins(): pl.pallas_call(functools.partial(cross_kernel, groups=groups, held=held,...  12.3 us
    pallas_call x1, Pallas kernels, head(): pl.pallas_call(functools.partial(head_kernel, parts=parts), out_shape=[ja...  6.11 us
  transfers between devices with their start and end apart: 22, of which 9 were waited for; matrix products, arithmetic and copies ran while one was open for 2% of the time, Pallas kernels for 9%

profile of v6, /device:TPU:0, one launch (start us, length us, event | category | flops | bytes accessed | tf_op | source)
XLA Modules:
  0.0 81.8 jit_solution(148081984055969969)
XLA Ops:
  0.7 6.1 %spectra.1 = (bf16[1,2,8,16,256]{4,3,2,1,0:T(8,128)(2,1)S(1)}, bf16[1,2,8,16,256]{4,3,2,1,0:T(8,128)(2,1)S(1)}, bf16[1,2,8,16,256]{4,3,2,1,0:T(8,128)(2,1)S(1)},...) custom-call(s32[1]{0:T(128)} %bitcast.me_ref, ...), custom_call_target="tpu_custom_call" | custom-call | tf_op jit(solution)/shard_map/spectra/pallas_call | solution.py:97
  8.2 1.4 %collective-permute-done = bf16[8,2,8,16,256]{4,3,2,1,0:T(8,128)(2,1)S(1)} collective-permute-done((bf16[8,2,8,16,256]{4,3,2,1,0:T(8,128)(2,1)S(1)}, bf16[8,2,8,16,256]{4,3,2,1,0:T(8,128)(2,1)S(1)}, u32[]{:S(2)}, u32[]{:S(2)}) %collective-permute-start) | collective-permute-done | bytes 1048608 | tf_op jit(solution)/shard_map/ppermute | solution.py:240
  9.8 4.0 %collective-permute-start.3 = (bf16[2,2,5,16,256]{4,3,2,1,0:T(8,128)(2,1)S(1)}, bf16[2,2,5,16,256]{4,3,2,1,0:T(8,128)(2,1)S(1)}, u32[]{:S(2)}, u32[]{:S(2)}) collective-permute-start(bf16[2,2,5,16,256]{4,3,2,1,0:T(8,128)(2,1)S(1)} %fusion.2), channel_id=1, source_target_pairs={{0,8},{1,9},{2,10},{3,11},{4,12},{5,13},{6,14},{7,15},{8,0},{9,1},... | collective-permute-start | bytes 491528 | tf_op jit(solution)/shard_map/ppermute | solution.py:224
  13.8 1.6 %collective-permute-start.1 = (bf16[2,2,8,16,256]{4,3,2,1,0:T(8,128)(2,1)S(1)}, bf16[2,2,8,16,256]{4,3,2,1,0:T(8,128)(2,1)S(1)}, u32[]{:S(2)}, u32[]{:S(2)}) collective-permute-start(bf16[2,2,8,16,256]{4,3,2,1,0:T(8,128)(2,1)S(1)} %pad_maximum_fusion), channel_id=1, source_target_pairs={{0,2},{1,3},{2,0},{3,1},{4,6},{5,7},{6,4},{7,5},{8,10},{9,11},{10,... | collective-permute-start | bytes 786440 | tf_op jit(solution)/shard_map/ppermute | solution.py:224
  15.4 1.6 %collective-permute-start.2 = (bf16[2,2,8,16,256]{4,3,2,1,0:T(8,128)(2,1)S(1)}, bf16[2,2,8,16,256]{4,3,2,1,0:T(8,128)(2,1)S(1)}, u32[]{:S(2)}, u32[]{:S(2)}) collective-permute-start(bf16[2,2,8,16,256]{4,3,2,1,0:T(8,128)(2,1)S(1)} %pad_maximum_fusion.2), channel_id=1, source_target_pairs={{0,4},{1,5},{2,6},{3,7},{4,0},{5,1},{6,2},{7,3},{8,12},{9,13},{10,... | collective-permute-start | bytes 786440 | tf_op jit(solution)/shard_map/ppermute | solution.py:224
  17.1 1.6 %collective-permute-start.10 = (bf16[2,2,8,16,256]{4,3,2,1,0:T(8,128)(2,1)S(1)}, bf16[2,2,8,16,256]{4,3,2,1,0:T(8,128)(2,1)S(1)}, u32[]{:S(2)}, u32[]{:S(2)}) collective-permute-start(bf16[2,2,8,16,256]{4,3,2,1,0:T(8,128)(2,1)S(1)} %pad_maximum_fusion.1.rest_0_), channel_id=1, source_target_pairs={{0,16},{16,0},{1,17},{17,1},{2,18},{18,2},{3,19},{19,3},{4,20},{20... | collective-permute-start | bytes 786440 | tf_op jit(solution)/shard_map/ppermute | solution.py:224
  19.0 2.8 %collective-permute-done.3 = bf16[2,2,5,16,256]{4,3,2,1,0:T(8,128)(2,1)S(1)} collective-permute-done((bf16[2,2,5,16,256]{4,3,2,1,0:T(8,128)(2,1)S(1)}, bf16[2,2,5,16,256]{4,3,2,1,0:T(8,128)(2,1)S(1)}, u32[]{:S(2)}, u32[]{:S(2)}) %collective-permute-start.3) | collective-permute-done | bytes 163872 | tf_op jit(solution)/shard_map/ppermute | solution.py:224
  21.9 1.6 %collective-permute-start.4 = (bf16[2,2,8,16,256]{4,3,2,1,0:T(8,128)(2,1)S(1)}, bf16[2,2,8,16,256]{4,3,2,1,0:T(8,128)(2,1)S(1)}, u32[]{:S(2)}, u32[]{:S(2)}) collective-permute-start(bf16[2,2,8,16,256]{4,3,2,1,0:T(8,128)(2,1)S(1)} %pad_maximum_fusion.3), channel_id=1, source_target_pairs={{0,6},{1,7},{2,4},{3,5},{4,2},{5,3},{6,0},{7,1},{8,14},{9,15},{10,... | collective-permute-start | bytes 786440 | tf_op jit(solution)/shard_map/ppermute | solution.py:224
  23.5 1.5 %collective-permute-start.5 = (bf16[2,2,8,16,256]{4,3,2,1,0:T(8,128)(2,1)S(1)}, bf16[2,2,8,16,256]{4,3,2,1,0:T(8,128)(2,1)S(1)}, u32[]{:S(2)}, u32[]{:S(2)}) collective-permute-start(bf16[2,2,8,16,256]{4,3,2,1,0:T(8,128)(2,1)S(1)} %collective-permute-done.1.rest_1_), channel_id=1, source_target_pairs={{0,16},{16,0},{1,17},{17,1},{2,18},{18,2},{3,19},{19,3},{4,20},{20... | collective-permute-start | bytes 786440 | tf_op jit(solution)/shard_map/ppermute | solution.py:224
  25.0 3.5 %collective-permute-start.9 = (bf16[2,2,5,16,256]{4,3,2,1,0:T(8,128)(2,1)S(1)}, bf16[2,2,5,16,256]{4,3,2,1,0:T(8,128)(2,1)S(1)}, u32[]{:S(2)}, u32[]{:S(2)}) collective-permute-start(bf16[2,2,5,16,256]{4,3,2,1,0:T(8,128)(2,1)S(1)} %get-tuple-element.48), channel_id=1, source_target_pairs={{0,10},{1,11},{2,8},{3,9},{4,14},{5,15},{6,12},{7,13},{8,2},{9,3},... | collective-permute-start | bytes 491528 | tf_op jit(solution)/shard_map/ppermute | solution.py:224
  29.7 4.5 %collective-permute-done.4.rest_3_ = bf16[2,2,8,16,256]{4,3,2,1,0:T(8,128)(2,1)S(1)} collective-permute-done((bf16[2,2,8,16,256]{4,3,2,1,0:T(8,128)(2,1)S(1)}, bf16[2,2,8,16,256]{4,3,2,1,0:T(8,128)(2,1)S(1)}, u32[]{:S(2)}, u32[]{:S(2)}) %collective-permute-start.4) | collective-permute-done | bytes 262176 | tf_op jit(solution)/shard_map/ppermute | solution.py:224
  34.2 2.1 %collective-permute-start.6 = (bf16[2,2,8,16,256]{4,3,2,1,0:T(8,128)(2,1)S(1)}, bf16[2,2,8,16,256]{4,3,2,1,0:T(8,128)(2,1)S(1)}, u32[]{:S(2)}, u32[]{:S(2)}) collective-permute-start(bf16[2,2,8,16,256]{4,3,2,1,0:T(8,128)(2,1)S(1)} %collective-permute-done.4.rest_3_), channel_id=1, source_target_pairs={{0,16},{16,0},{1,17},{17,1},{2,18},{18,2},{3,19},{19,3},{4,20},{20... | collective-permute-start | bytes 786440 | tf_op jit(solution)/shard_map/ppermute | solution.py:224
  36.3 4.8 %collective-permute-done.9 = bf16[2,2,5,16,256]{4,3,2,1,0:T(8,128)(2,1)S(1)} collective-permute-done((bf16[2,2,5,16,256]{4,3,2,1,0:T(8,128)(2,1)S(1)}, bf16[2,2,5,16,256]{4,3,2,1,0:T(8,128)(2,1)S(1)}, u32[]{:S(2)}, u32[]{:S(2)}) %collective-permute-start.9) | collective-permute-done | bytes 163872 | tf_op jit(solution)/shard_map/ppermute | solution.py:224
  41.2 3.5 %collective-permute-start.13 = (bf16[2,2,5,16,256]{4,3,2,1,0:T(8,128)(2,1)S(1)}, bf16[2,2,5,16,256]{4,3,2,1,0:T(8,128)(2,1)S(1)}, u32[]{:S(2)}, u32[]{:S(2)}) collective-permute-start(bf16[2,2,5,16,256]{4,3,2,1,0:T(8,128)(2,1)S(1)} %fusion), channel_id=1, source_target_pairs={{0,14},{1,15},{2,12},{3,13},{4,10},{5,11},{6,8},{7,9},{8,6},{9,7},... | collective-permute-start | bytes 491528 | tf_op jit(solution)/shard_map/ppermute | solution.py:224
  44.7 2.7 %collective-permute-start.8 = (bf16[2,2,3,16,256]{4,3,2,1,0:T(8,128)(2,1)S(1)}, bf16[2,2,3,16,256]{4,3,2,1,0:T(8,128)(2,1)S(1)}, u32[]{:S(2)}, u32[]{:S(2)}) collective-permute-start(bf16[2,2,3,16,256]{4,3,2,1,0:T(8,128)(2,1)S(1)} %pad_maximum_fusion.8), channel_id=1, source_target_pairs={{0,8},{1,9},{2,10},{3,11},{4,12},{5,13},{6,14},{7,15},{8,0},{9,1},... | collective-permute-start | bytes 294920 | tf_op jit(solution)/shard_map/ppermute | solution.py:224
  47.4 1.6 %collective-permute-start.15 = (bf16[2,2,5,16,256]{4,3,2,1,0:T(8,128)(2,1)S(1)}, bf16[2,2,5,16,256]{4,3,2,1,0:T(8,128)(2,1)S(1)}, u32[]{:S(2)}, u32[]{:S(2)}) collective-permute-start(bf16[2,2,5,16,256]{4,3,2,1,0:T(8,128)(2,1)S(1)} %collective-permute-done.7.rest_5_), channel_id=1, source_target_pairs={{0,16},{16,0},{1,17},{17,1},{2,18},{18,2},{3,19},{19,3},{4,20},{20... | collective-permute-start | bytes 491528 | tf_op jit(solution)/shard_map/ppermute | solution.py:224
  49.4 2.1 %collective-permute-done.12.rest_11_ = bf16[4,2,5,16,256]{4,3,2,1,0:T(8,128)(2,1)S(1)} collective-permute-done((bf16[4,2,5,16,256]{4,3,2,1,0:T(8,128)(2,1)S(1)}, bf16[4,2,5,16,256]{4,3,2,1,0:T(8,128)(2,1)S(1)}, u32[]{:S(2)}, u32[]{:S(2)}) %collective-permute-start.12) | collective-permute-done | bytes 327712 | tf_op jit(solution)/shard_map/ppermute | solution.py:224
  51.5 4.1 %collective-permute-start.14 = (bf16[2,2,3,16,256]{4,3,2,1,0:T(8,128)(2,1)S(1)}, bf16[2,2,3,16,256]{4,3,2,1,0:T(8,128)(2,1)S(1)}, u32[]{:S(2)}, u32[]{:S(2)}) collective-permute-start(bf16[2,2,3,16,256]{4,3,2,1,0:T(8,128)(2,1)S(1)} %pad_maximum_fusion.7), channel_id=1, source_target_pairs={{0,10},{1,11},{2,8},{3,9},{4,14},{5,15},{6,12},{7,13},{8,2},{9,3},... | collective-permute-start | bytes 294920 | tf_op jit(solution)/shard_map/ppermute | solution.py:224
  56.3 2.9 %collective-permute-done.14 = bf16[2,2,3,16,256]{4,3,2,1,0:T(8,128)(2,1)S(1)} collective-permute-done((bf16[2,2,3,16,256]{4,3,2,1,0:T(8,128)(2,1)S(1)}, bf16[2,2,3,16,256]{4,3,2,1,0:T(8,128)(2,1)S(1)}, u32[]{:S(2)}, u32[]{:S(2)}) %collective-permute-start.14) | collective-permute-done | bytes 98336 | tf_op jit(solution)/shard_map/ppermute | solution.py:224
  60.1 1.8 %collective-permute-start.16 = (bf16[2,2,3,16,256]{4,3,2,1,0:T(8,128)(2,1)S(1)}, bf16[2,2,3,16,256]{4,3,2,1,0:T(8,128)(2,1)S(1)}, u32[]{:S(2)}, u32[]{:S(2)}) collective-permute-start(bf16[2,2,3,16,256]{4,3,2,1,0:T(8,128)(2,1)S(1)} %pad_maximum_fusion.6), channel_id=1, source_target_pairs={{0,12},{1,13},{2,14},{3,15},{4,8},{5,9},{6,10},{7,11},{8,4},{9,5},... | collective-permute-start | bytes 294920 | tf_op jit(solution)/shard_map/ppermute | solution.py:224
  61.9 1.7 %collective-permute-start.18 = (bf16[2,2,3,16,256]{4,3,2,1,0:T(8,128)(2,1)S(1)}, bf16[2,2,3,16,256]{4,3,2,1,0:T(8,128)(2,1)S(1)}, u32[]{:S(2)}, u32[]{:S(2)}) collective-permute-start(bf16[2,2,3,16,256]{4,3,2,1,0:T(8,128)(2,1)S(1)} %pad_maximum_fusion.5), channel_id=1, source_target_pairs={{0,14},{1,15},{2,12},{3,13},{4,10},{5,11},{6,8},{7,9},{8,6},{9,7},... | collective-permute-start | bytes 294920 | tf_op jit(solution)/shard_map/ppermute | solution.py:224
  63.6 7.5 %cross.2.rest_14_ = bf16[8,2,4096,128]{3,2,1,0:T(8,128)(2,1)} custom-call(bf16[1024,256]{1,0:T(8,128)(2,1)S(1)} %and_convert_fusion.select_ref, bf16[2,2,8,16,256]{4,3,2,1,0:T(8,128)(2,1)S(1)} %pad_maximum_fusion.1.rest_0_, bf16[2,2,8,16,256]{4,3,2,1,0:T(8,128)(2,1)S(1)} %collective-permute-done.1.rest_1_, ...), custom_call_target="tpu_custom_call" | custom-call | flops 1342177280 | bytes 10485760 | tf_op jit(solution)/shard_map/cross/pallas_call | solution.py:194
  73.2 2.6 %collective-permute-done.20.rest_12_ = bf16[2,2,3,16,256]{4,3,2,1,0:T(8,128)(2,1)S(1)} collective-permute-done((bf16[2,2,3,16,256]{4,3,2,1,0:T(8,128)(2,1)S(1)}, bf16[2,2,3,16,256]{4,3,2,1,0:T(8,128)(2,1)S(1)}, u32[]{:S(2)}, u32[]{:S(2)}) %collective-permute-start.20) | collective-permute-done | bytes 98336 | tf_op jit(solution)/shard_map/ppermute | solution.py:224
  77.0 4.8 %cross.3 = bf16[8,2,4096,128]{3,2,1,0:T(8,128)(2,1)} custom-call(bf16[1024,256]{1,0:T(8,128)(2,1)S(1)} %and_convert_fusion.select_ref, bf16[2,2,8,16,256]{4,3,2,1,0:T(8,128)(2,1)S(1)} %pad_maximum_fusion.1.rest_0_, bf16[2,2,8,16,256]{4,3,2,1,0:T(8,128)(2,1)S(1)} %collective-permute-done.1.rest_1_, ...), custom_call_target="tpu_custom_call", output_to_operand_aliasing={{}: (15, {})} | custom-call | flops 805306368 | bytes 6291456 | tf_op jit(solution)/shard_map/cross/pallas_call | solution.py:194
  (48 shorter events, 9.2 us)
Async XLA Ops:
  0.0 0.7 copy-start
  6.8 2.8 %collective-permute-start = (bf16[8,2,8,16,256]{4,3,2,1,0:T(8,128)(2,1)S(1)}, bf16[8,2,8,16,256]{4,3,2,1,0:T(8,128)(2,1)S(1)}, u32[]{:S(2)}, u32[]{:S(2)}) collective-permute-start(bf16[8,2,8,16,256]{4,3,2,1,0:T(8,128)(2,1)S(1)} %get-tuple-element.35), channel_id=1, source_target_pairs={{0,1},{1,0},{2,3},{3,2},{4,5},{5,4},{6,7},{7,6},{8,9},{9,8},{10,11... | collective-permute-start | bytes 3145736 | tf_op jit(solution)/shard_map/ppermute | solution.py:240
  9.8 12.1 %collective-permute-start.3 = (bf16[2,2,5,16,256]{4,3,2,1,0:T(8,128)(2,1)S(1)}, bf16[2,2,5,16,256]{4,3,2,1,0:T(8,128)(2,1)S(1)}, u32[]{:S(2)}, u32[]{:S(2)}) collective-permute-start(bf16[2,2,5,16,256]{4,3,2,1,0:T(8,128)(2,1)S(1)} %fusion.2), channel_id=1, source_target_pairs={{0,8},{1,9},{2,10},{3,11},{4,12},{5,13},{6,14},{7,15},{8,0},{9,1},... | collective-permute-start | bytes 491528 | tf_op jit(solution)/shard_map/ppermute | solution.py:224
  13.8 9.7 %collective-permute-start.1 = (bf16[2,2,8,16,256]{4,3,2,1,0:T(8,128)(2,1)S(1)}, bf16[2,2,8,16,256]{4,3,2,1,0:T(8,128)(2,1)S(1)}, u32[]{:S(2)}, u32[]{:S(2)}) collective-permute-start(bf16[2,2,8,16,256]{4,3,2,1,0:T(8,128)(2,1)S(1)} %pad_maximum_fusion), channel_id=1, source_target_pairs={{0,2},{1,3},{2,0},{3,1},{4,6},{5,7},{6,4},{7,5},{8,10},{9,11},{10,... | collective-permute-start | bytes 786440 | tf_op jit(solution)/shard_map/ppermute | solution.py:224
  15.4 13.1 %collective-permute-start.2 = (bf16[2,2,8,16,256]{4,3,2,1,0:T(8,128)(2,1)S(1)}, bf16[2,2,8,16,256]{4,3,2,1,0:T(8,128)(2,1)S(1)}, u32[]{:S(2)}, u32[]{:S(2)}) collective-permute-start(bf16[2,2,8,16,256]{4,3,2,1,0:T(8,128)(2,1)S(1)} %pad_maximum_fusion.2), channel_id=1, source_target_pairs={{0,4},{1,5},{2,6},{3,7},{4,0},{5,1},{6,2},{7,3},{8,12},{9,13},{10,... | collective-permute-start | bytes 786440 | tf_op jit(solution)/shard_map/ppermute | solution.py:224
  17.1 11.5 %collective-permute-start.10 = (bf16[2,2,8,16,256]{4,3,2,1,0:T(8,128)(2,1)S(1)}, bf16[2,2,8,16,256]{4,3,2,1,0:T(8,128)(2,1)S(1)}, u32[]{:S(2)}, u32[]{:S(2)}) collective-permute-start(bf16[2,2,8,16,256]{4,3,2,1,0:T(8,128)(2,1)S(1)} %pad_maximum_fusion.1.rest_0_), channel_id=1, source_target_pairs={{0,16},{16,0},{1,17},{17,1},{2,18},{18,2},{3,19},{19,3},{4,20},{20... | collective-permute-start | bytes 786440 | tf_op jit(solution)/shard_map/ppermute | solution.py:224
  21.9 12.3 %collective-permute-start.4 = (bf16[2,2,8,16,256]{4,3,2,1,0:T(8,128)(2,1)S(1)}, bf16[2,2,8,16,256]{4,3,2,1,0:T(8,128)(2,1)S(1)}, u32[]{:S(2)}, u32[]{:S(2)}) collective-permute-start(bf16[2,2,8,16,256]{4,3,2,1,0:T(8,128)(2,1)S(1)} %pad_maximum_fusion.3), channel_id=1, source_target_pairs={{0,6},{1,7},{2,4},{3,5},{4,2},{5,3},{6,0},{7,1},{8,14},{9,15},{10,... | collective-permute-start | bytes 786440 | tf_op jit(solution)/shard_map/ppermute | solution.py:224
  23.5 10.7 %collective-permute-start.5 = (bf16[2,2,8,16,256]{4,3,2,1,0:T(8,128)(2,1)S(1)}, bf16[2,2,8,16,256]{4,3,2,1,0:T(8,128)(2,1)S(1)}, u32[]{:S(2)}, u32[]{:S(2)}) collective-permute-start(bf16[2,2,8,16,256]{4,3,2,1,0:T(8,128)(2,1)S(1)} %collective-permute-done.1.rest_1_), channel_id=1, source_target_pairs={{0,16},{16,0},{1,17},{17,1},{2,18},{18,2},{3,19},{19,3},{4,20},{20... | collective-permute-start | bytes 786440 | tf_op jit(solution)/shard_map/ppermute | solution.py:224
  25.0 16.0 %collective-permute-start.9 = (bf16[2,2,5,16,256]{4,3,2,1,0:T(8,128)(2,1)S(1)}, bf16[2,2,5,16,256]{4,3,2,1,0:T(8,128)(2,1)S(1)}, u32[]{:S(2)}, u32[]{:S(2)}) collective-permute-start(bf16[2,2,5,16,256]{4,3,2,1,0:T(8,128)(2,1)S(1)} %get-tuple-element.48), channel_id=1, source_target_pairs={{0,10},{1,11},{2,8},{3,9},{4,14},{5,15},{6,12},{7,13},{8,2},{9,3},... | collective-permute-start | bytes 491528 | tf_op jit(solution)/shard_map/ppermute | solution.py:224
  28.5 12.6 %collective-permute-start.11 = (bf16[2,2,8,16,256]{4,3,2,1,0:T(8,128)(2,1)S(1)}, bf16[2,2,8,16,256]{4,3,2,1,0:T(8,128)(2,1)S(1)}, u32[]{:S(2)}, u32[]{:S(2)}) collective-permute-start(bf16[2,2,8,16,256]{4,3,2,1,0:T(8,128)(2,1)S(1)} %collective-permute-done.2.rest_2_), channel_id=1, source_target_pairs={{0,16},{16,0},{1,17},{17,1},{2,18},{18,2},{3,19},{19,3},{4,20},{20... | collective-permute-start | bytes 786440 | tf_op jit(solution)/shard_map/ppermute | solution.py:224
  29.0 15.6 %collective-permute-start.7 = (bf16[2,2,5,16,256]{4,3,2,1,0:T(8,128)(2,1)S(1)}, bf16[2,2,5,16,256]{4,3,2,1,0:T(8,128)(2,1)S(1)}, u32[]{:S(2)}, u32[]{:S(2)}) collective-permute-start(bf16[2,2,5,16,256]{4,3,2,1,0:T(8,128)(2,1)S(1)} %get-tuple-element.45), channel_id=1, source_target_pairs={{0,12},{1,13},{2,14},{3,15},{4,8},{5,9},{6,10},{7,11},{8,4},{9,5},... | collective-permute-start | bytes 491528 | tf_op jit(solution)/shard_map/ppermute | solution.py:224
  34.2 10.5 %collective-permute-start.6 = (bf16[2,2,8,16,256]{4,3,2,1,0:T(8,128)(2,1)S(1)}, bf16[2,2,8,16,256]{4,3,2,1,0:T(8,128)(2,1)S(1)}, u32[]{:S(2)}, u32[]{:S(2)}) collective-permute-start(bf16[2,2,8,16,256]{4,3,2,1,0:T(8,128)(2,1)S(1)} %collective-permute-done.4.rest_3_), channel_id=1, source_target_pairs={{0,16},{16,0},{1,17},{17,1},{2,18},{18,2},{3,19},{19,3},{4,20},{20... | collective-permute-start | bytes 786440 | tf_op jit(solution)/shard_map/ppermute | solution.py:224
  41.1 10.4 %collective-permute-start.12 = (bf16[4,2,5,16,256]{4,3,2,1,0:T(8,128)(2,1)S(1)}, bf16[4,2,5,16,256]{4,3,2,1,0:T(8,128)(2,1)S(1)}, u32[]{:S(2)}, u32[]{:S(2)}) collective-permute-start(bf16[4,2,5,16,256]{4,3,2,1,0:T(8,128)(2,1)S(1)} %constant_dynamic-update-slice_fusion.rest_4_), channel_id=1, source_target_pairs={{0,16},{16,0},{1,17},{17,1},{2,18},{18,2},{3,19},{19,3},{4,20},{20... | collective-permute-start | bytes 983048 | tf_op jit(solution)/shard_map/ppermute | solution.py:224
  41.2 8.2 %collective-permute-start.13 = (bf16[2,2,5,16,256]{4,3,2,1,0:T(8,128)(2,1)S(1)}, bf16[2,2,5,16,256]{4,3,2,1,0:T(8,128)(2,1)S(1)}, u32[]{:S(2)}, u32[]{:S(2)}) collective-permute-start(bf16[2,2,5,16,256]{4,3,2,1,0:T(8,128)(2,1)S(1)} %fusion), channel_id=1, source_target_pairs={{0,14},{1,15},{2,12},{3,13},{4,10},{5,11},{6,8},{7,9},{8,6},{9,7},... | collective-permute-start | bytes 491528 | tf_op jit(solution)/shard_map/ppermute | solution.py:224
  44.7 11.6 %collective-permute-start.8 = (bf16[2,2,3,16,256]{4,3,2,1,0:T(8,128)(2,1)S(1)}, bf16[2,2,3,16,256]{4,3,2,1,0:T(8,128)(2,1)S(1)}, u32[]{:S(2)}, u32[]{:S(2)}) collective-permute-start(bf16[2,2,3,16,256]{4,3,2,1,0:T(8,128)(2,1)S(1)} %pad_maximum_fusion.8), channel_id=1, source_target_pairs={{0,8},{1,9},{2,10},{3,11},{4,12},{5,13},{6,14},{7,15},{8,0},{9,1},... | collective-permute-start | bytes 294920 | tf_op jit(solution)/shard_map/ppermute | solution.py:224
  47.4 11.8 %collective-permute-start.15 = (bf16[2,2,5,16,256]{4,3,2,1,0:T(8,128)(2,1)S(1)}, bf16[2,2,5,16,256]{4,3,2,1,0:T(8,128)(2,1)S(1)}, u32[]{:S(2)}, u32[]{:S(2)}) collective-permute-start(bf16[2,2,5,16,256]{4,3,2,1,0:T(8,128)(2,1)S(1)} %collective-permute-done.7.rest_5_), channel_id=1, source_target_pairs={{0,16},{16,0},{1,17},{17,1},{2,18},{18,2},{3,19},{19,3},{4,20},{20... | collective-permute-start | bytes 491528 | tf_op jit(solution)/shard_map/ppermute | solution.py:224
  51.5 7.7 %collective-permute-start.14 = (bf16[2,2,3,16,256]{4,3,2,1,0:T(8,128)(2,1)S(1)}, bf16[2,2,3,16,256]{4,3,2,1,0:T(8,128)(2,1)S(1)}, u32[]{:S(2)}, u32[]{:S(2)}) collective-permute-start(bf16[2,2,3,16,256]{4,3,2,1,0:T(8,128)(2,1)S(1)} %pad_maximum_fusion.7), channel_id=1, source_target_pairs={{0,10},{1,11},{2,8},{3,9},{4,14},{5,15},{6,12},{7,13},{8,2},{9,3},... | collective-permute-start | bytes 294920 | tf_op jit(solution)/shard_map/ppermute | solution.py:224
  55.6 8.0 %collective-permute-start.17 = (bf16[2,2,5,16,256]{4,3,2,1,0:T(8,128)(2,1)S(1)}, bf16[2,2,5,16,256]{4,3,2,1,0:T(8,128)(2,1)S(1)}, u32[]{:S(2)}, u32[]{:S(2)}) collective-permute-start(bf16[2,2,5,16,256]{4,3,2,1,0:T(8,128)(2,1)S(1)} %collective-permute-done.13.rest_6_), channel_id=1, source_target_pairs={{0,16},{16,0},{1,17},{17,1},{2,18},{18,2},{3,19},{19,3},{4,20},{20... | collective-permute-start | bytes 491528 | tf_op jit(solution)/shard_map/ppermute | solution.py:224
  59.2 13.1 %collective-permute-start.19 = (bf16[4,2,3,16,256]{4,3,2,1,0:T(8,128)(2,1)S(1)}, bf16[4,2,3,16,256]{4,3,2,1,0:T(8,128)(2,1)S(1)}, u32[]{:S(2)}, u32[]{:S(2)}) collective-permute-start(bf16[4,2,3,16,256]{4,3,2,1,0:T(8,128)(2,1)S(1)} %constant_dynamic-update-slice_fusion.2.rest_4_), channel_id=1, source_target_pairs={{0,16},{16,0},{1,17},{17,1},{2,18},{18,2},{3,19},{19,3},{4,20},{20... | collective-permute-start | bytes 589832 | tf_op jit(solution)/shard_map/ppermute | solution.py:224
  60.1 11.0 %collective-permute-start.16 = (bf16[2,2,3,16,256]{4,3,2,1,0:T(8,128)(2,1)S(1)}, bf16[2,2,3,16,256]{4,3,2,1,0:T(8,128)(2,1)S(1)}, u32[]{:S(2)}, u32[]{:S(2)}) collective-permute-start(bf16[2,2,3,16,256]{4,3,2,1,0:T(8,128)(2,1)S(1)} %pad_maximum_fusion.6), channel_id=1, source_target_pairs={{0,12},{1,13},{2,14},{3,15},{4,8},{5,9},{6,10},{7,11},{8,4},{9,5},... | collective-permute-start | bytes 294920 | tf_op jit(solution)/shard_map/ppermute | solution.py:224
  61.9 10.4 %collective-permute-start.18 = (bf16[2,2,3,16,256]{4,3,2,1,0:T(8,128)(2,1)S(1)}, bf16[2,2,3,16,256]{4,3,2,1,0:T(8,128)(2,1)S(1)}, u32[]{:S(2)}, u32[]{:S(2)}) collective-permute-start(bf16[2,2,3,16,256]{4,3,2,1,0:T(8,128)(2,1)S(1)} %pad_maximum_fusion.5), channel_id=1, source_target_pairs={{0,14},{1,15},{2,12},{3,13},{4,10},{5,11},{6,8},{7,9},{8,6},{9,7},... | collective-permute-start | bytes 294920 | tf_op jit(solution)/shard_map/ppermute | solution.py:224
  71.1 4.7 %collective-permute-start.20 = (bf16[2,2,3,16,256]{4,3,2,1,0:T(8,128)(2,1)S(1)}, bf16[2,2,3,16,256]{4,3,2,1,0:T(8,128)(2,1)S(1)}, u32[]{:S(2)}, u32[]{:S(2)}) collective-permute-start(bf16[2,2,3,16,256]{4,3,2,1,0:T(8,128)(2,1)S(1)} %collective-permute-done.16.rest_5_), channel_id=1, source_target_pairs={{0,16},{16,0},{1,17},{17,1},{2,18},{18,2},{3,19},{19,3},{4,20},{20... | collective-permute-start | bytes 294920 | tf_op jit(solution)/shard_map/ppermute | solution.py:224
  72.3 4.6 %collective-permute-start.21 = (bf16[2,2,3,16,256]{4,3,2,1,0:T(8,128)(2,1)S(1)}, bf16[2,2,3,16,256]{4,3,2,1,0:T(8,128)(2,1)S(1)}, u32[]{:S(2)}, u32[]{:S(2)}) collective-permute-start(bf16[2,2,3,16,256]{4,3,2,1,0:T(8,128)(2,1)S(1)} %collective-permute-done.18.rest_6_), channel_id=1, source_target_pairs={{0,16},{16,0},{1,17},{17,1},{2,18},{18,2},{3,19},{19,3},{4,20},{20... | collective-permute-start | bytes 294920 | tf_op jit(solution)/shard_map/ppermute | solution.py:224
